TPU v7x, 32 devices: a whole 2x2x4 slice. The times are simulated.
32 devices in a mesh: parts: 2 (over x), harm: 4 (over y, core), tile: 4 (over z).
Axes of the slice: x: 2, y: 2, z: 4, core: 2. Of those that a mesh axis runs over, the one named last changes fastest.
Arguments:
- perturbation: float32 [8, 2, 5, 128, 256], P('harm', None, None, ('parts', 'tile')), parts along dimension 3, may hold values from -6 to 6
- base_flow: float32 [8, 2, 3, 128, 256], P('harm', None, None, ('parts', 'tile')), parts along dimension 3, may hold values from -0.9 to 0.9
- viscosity: float32 [128, 256], P(('parts', 'tile')), parts along dimension 0, may hold values from 0.05 to 0.5
Outputs:
- resolvent_image: float32 [8, 2, 5, 128, 256], P('harm', None, None, ('parts', 'tile')), parts along dimension 3
There are 2 independent parts, one for each index of `parts`. A program takes and returns all parts, laid end to end along the dimension named above; each array names one. Nothing has to cross between parts.
All inputs are finite; a program needn't handle non-finite values.
Results may differ from a plain program's by a relative error of at most 0.00002.
Values sent between devices are 32-bit elements; how exact they have to be, the bound alone decides.
No kernel may reach another device: no remote copies, remote signals or barrier semaphores. Data moves between devices by JAX's collectives and lax.ppermute only.
A program may use at most 64 MiB of HBM per device.

v0:
```python
import jax
import jax.numpy as jnp
import numpy as np
from jax import lax
from jax.sharding import PartitionSpec as P

omega_base = 0.25


def extended(cells, sides, width):
    for axis, dim in sides:
        count = lax.axis_size(axis)
        head = lax.slice_in_dim(cells, 0, width, axis=dim)
        tail = lax.slice_in_dim(cells, cells.shape[dim] - width, cells.shape[dim], axis=dim)
        cells = jnp.concatenate(
            [
                lax.ppermute(tail, axis, [(i, (i + 1) % count) for i in range(count)]),
                cells,
                lax.ppermute(head, axis, [((i + 1) % count, i) for i in range(count)]),
            ],
            axis=dim,
        )
    return cells


def shifted(value, axis, steps):
    count = lax.axis_size(axis)
    pairs = [(source, (source + steps) % count) for source in range(count)]
    return lax.ppermute(value, axis, pairs)


def split_rows(padded):
    middle = padded[..., 1:-1, :]
    grad_x = 0.5 * (padded[..., 2:, :] - padded[..., :-2, :])
    grad_y = 0.5 * (jnp.roll(middle, -1, -1) - jnp.roll(middle, 1, -1))
    return (middle, grad_x, grad_y)


def diffusion(padded, visc_padded):
    middle = padded[..., 1:-1, :]
    center = visc_padded[1:-1]
    east_face = 0.5 * (center + visc_padded[2:])
    west_face = 0.5 * (center + visc_padded[:-2])
    north_face = 0.5 * (center + jnp.roll(center, -1, -1))
    south_face = 0.5 * (center + jnp.roll(center, 1, -1))
    return (
        east_face * (padded[..., 2:, :] - middle)
        - west_face * (middle - padded[..., :-2, :])
        + north_face * (jnp.roll(middle, -1, -1) - middle)
        - south_face * (middle - jnp.roll(middle, 1, -1))
    )


def acoustic(grad_x, grad_y):
    dilation = grad_x[..., 1, :, :] + grad_y[..., 2, :, :]
    return jnp.stack(
        [dilation, grad_x[..., 4, :, :], grad_y[..., 4, :, :], jnp.zeros_like(dilation), dilation],
        axis=-3,
    )


def own_terms(middle, grad_x, grad_y, damping, frequency):
    rotation = jnp.stack([-frequency * middle[:, 1], frequency * middle[:, 0]], axis=1)
    return rotation + acoustic(grad_x, grad_y) - damping


def coupling(
    u_real, u_imag, v_real, v_imag, g_real, g_imag, q_real, q_imag, x_real, x_imag, y_real, y_imag
):
    real_part = (
        u_real * x_real
        - u_imag * x_imag
        + v_real * y_real
        - v_imag * y_imag
        + g_real * q_real
        - g_imag * q_imag
    )
    imag_part = (
        u_real * x_imag
        + u_imag * x_real
        + v_real * y_imag
        + v_imag * y_real
        + g_real * q_imag
        + g_imag * q_real
    )
    return (real_part, imag_part)


def block_terms(blocks, middle, grad_x, grad_y):
    local_count = middle.shape[0]
    index_table = np.array(
        [
            [local_count + target - source for source in range(local_count)]
            for target in range(local_count)
        ],
        dtype=np.int32,
    )
    chosen = blocks[index_table]

    def base_part(complex_index, field_index):
        return chosen[:, :, complex_index, field_index][:, :, None]

    def moved_part(values, complex_index):
        return values[None, :, complex_index]

    real_part, imag_part = coupling(
        base_part(0, 0),
        base_part(1, 0),
        base_part(0, 1),
        base_part(1, 1),
        base_part(0, 2),
        base_part(1, 2),
        moved_part(middle, 0),
        moved_part(middle, 1),
        moved_part(grad_x, 0),
        moved_part(grad_x, 1),
        moved_part(grad_y, 0),
        moved_part(grad_y, 1),
    )
    return jnp.stack([jnp.sum(real_part, axis=1), jnp.sum(imag_part, axis=1)], axis=1)


def shards(perturbation, base_flow, viscosity):
    local_count = perturbation.shape[0]
    width_x = perturbation.shape[3]
    width_y = perturbation.shape[4]
    groups = lax.axis_size("harm")
    first_index = lax.axis_index("harm") * local_count
    flattened = perturbation.reshape(local_count * 10, width_x, width_y)
    stacked = jnp.concatenate([flattened, viscosity[None]], axis=0)
    padded = extended(stacked, (("tile", 1),), 1)
    own_padded = padded[:-1].reshape(local_count, 2, 5, width_x + 2, width_y)
    visc_padded = padded[-1]
    numbers = first_index + jnp.arange(local_count, dtype=jnp.int32)
    total_count = local_count * groups
    signed = jnp.where(numbers < total_count // 2, numbers, numbers - total_count)
    frequency = (omega_base * signed.astype(jnp.float32)).reshape(local_count, 1, 1, 1)
    middle, grad_x, grad_y = split_rows(own_padded)
    summed = own_terms(middle, grad_x, grad_y, diffusion(own_padded, visc_padded), frequency)
    whole_base = lax.all_gather(base_flow, "harm", axis=0, tiled=True)

    def base_pair(position, earlier):
        before = lax.dynamic_slice_in_dim(
            whole_base, (position + groups - 1) % groups * local_count, local_count, 0
        )
        current = lax.dynamic_slice_in_dim(whole_base, position * local_count, local_count, 0)
        return (jnp.concatenate([before, current], axis=0), earlier)

    earlier = base_flow
    moving = own_padded

    def advance(moving):
        moved = shifted(moving, "harm", 1)
        return (moved, moved)

    blocks, earlier = base_pair(0, earlier)
    summed = summed + block_terms(blocks, middle, grad_x, grad_y)

    def advance_step(position, carried):
        summed, moving, earlier = carried
        moving, rimmed = advance(moving)
        blocks, earlier = base_pair(position, earlier)
        values, slope_x, slope_y = split_rows(rimmed)
        return (summed + block_terms(blocks, values, slope_x, slope_y), moving, earlier)

    summed, moving, earlier = lax.fori_loop(1, groups, advance_step, (summed, moving, earlier))
    return summed


def solution(mesh):
    placed = (
        P("harm", None, None, ("parts", "tile"), None),
        P("harm", None, None, ("parts", "tile"), None),
        P(("parts", "tile"), None),
    )
    return jax.shard_map(
        shards,
        mesh=mesh,
        in_specs=placed,
        out_specs=P("harm", None, None, ("parts", "tile"), None),
        check_vma=False,
    )
```

profile of v0, /device:TPU:0, one launch (start us, length us, event | category | flops | bytes accessed | tf_op | source)
XLA Modules:
  0.0 47.7 jit_solution(18082950959541213090)
XLA Ops:
  0.0 1.1 %pad_maximum_fusion.8 = (f32[21,1,256]{2,1,0:T(1,128)S(1)}, f32[21,1,256]{2,1,0:T(1,128)S(1)}) fusion(f32[1,16,256]{2,1,0:T(8,128)} %bitcast.94, f32[20,16,256]{2,1,0:T(8,128)} %bitcast.90), kind=kLoop, calls=%fused_computation.57 | loop fusion | flops 10752 | bytes 387072 | tf_op jit(solution)/shard_map/slice | solution.py:14
  1.1 5.1 %collective-permute-start.2 = (f32[21,1,256]{2,1,0:T(1,128)S(1)}, f32[21,1,256]{2,1,0:T(1,128)S(1)}, u32[]{:S(2)}, u32[]{:S(2)}) collective-permute-start(f32[21,1,256]{2,1,0:T(1,128)S(1)} %get-tuple-element.304), channel_id=1, source_target_pairs={{1,0},{2,1},{3,2},{0,3},{5,4},{6,5},{7,6},{4,7},{9,8},{10,9},{11,1... | collective-permute-start | bytes 64520 | tf_op jit(solution)/shard_map/ppermute | solution.py:19
  6.4 8.6 %all_gather.3 = f32[8,2,3,16,256]{4,3,2,1,0:T(8,128)S(1)} all-gather(f32[2,2,3,16,256]{4,3,2,1,0:T(8,128)S(1)} %copy-done.2), channel_id=1, replica_groups=mesh['parts'=2,'harm'=4,'tile'=4] {'harm'}, dimensions={0}, use_global_device_ids=true | all-gather | bytes 983040 | tf_op jit(solution)/shard_map/all_gather | solution.py:140
  15.0 0.6 %copy-done.3 = s32[4]{0:T(128)S(1)} copy-done((s32[4]{0:T(128)S(1)}, s32[4]{0:T(128)}, u32[]{:S(2)}) %copy-start.3) | copy-done | bytes 40
  15.7 0.6 %gather_fusion.1 = f32[4,2,3,16,256]{4,3,2,1,0:T(8,128)S(1)} fusion(f32[4,2,3,16,256]{4,3,2,1,0:T(8,128)S(1)} %pad_maximum_fusion.4, s32[1024]{0:T(1024)S(1)} %pad_clamp_fusion.1), kind=kCustom, calls=%fused_computation.1 | custom fusion | bytes 786448 | tf_op jit(solution)/shard_map/gather | solution.py:98
  16.3 0.9 %copy-done = f32[2,2,5,16,256]{4,3,2,1,0:T(8,128)S(1)} copy-done((f32[2,2,5,16,256]{4,3,2,1,0:T(8,128)S(1)}, f32[2,2,5,16,256]{4,3,2,1,0:T(8,128)}, u32[]{:S(2)}) %copy-start) | copy-done | bytes 327704
  17.6 0.2 subtract_multiply_fusion
  18.1 0.3 subtract_reduce_fusion.1
  18.5 0.3 fusion.3
  18.8 28.2 %while.21 = (s32[]{:T(128)}, f32[2,2,5,16,256]{4,3,2,0,1:T(8,128)S(1)}, f32[2,2,5,18,256]{4,3,2,0,1:T(8,128)S(1)}, f32[8,2,3,16,256]{4,3,2,1,0:T(8,128)S(1)}, s3...) while((s32[]{:T(128)}, ...), condition=%wide.region_5.6_spmd.clone, body=%wide.region_2.5_spmd.sunk.clone.sunk | while | flops 2638870 | bytes 13291922 | solution.py:166
  18.8 0.4 collective-permute-start
  19.3 0.6 %gather_fusion = f32[4,2,3,16,256]{4,3,2,1,0:T(8,128)S(1)} fusion(f32[4,2,3,16,256]{4,3,2,1,0:T(8,128)S(1)} %pad_maximum_fusion.14, s32[1024]{0:T(1024)S(1)} %pad_clamp_fusion.3), kind=kCustom, calls=%fused_computation.clone.1 | custom fusion | bytes 786448 | tf_op jit(solution)/shard_map/while/body/eval_jaxpr/gather | solution.py:98
  19.9 7.2 %collective-permute-done = f32[2,2,5,18,256]{4,3,2,0,1:T(8,128)S(1)} collective-permute-done((f32[2,2,5,18,256]{4,3,2,0,1:T(8,128)S(1)}, f32[2,2,5,18,256]{4,3,2,0,1:T(8,128)S(1)}, u32[]{:S(2)}, u32[]{:S(2)}) %collective-permute-start) | collective-permute-done | bytes 368672 | tf_op jit(solution)/shard_map/while/body/eval_jaxpr/ppermute | solution.py:29
  27.5 0.2 fusion.35
  27.7 0.3 subtract_reduce_fusion.3
  28.4 0.6 %gather_fusion = f32[4,2,3,16,256]{4,3,2,1,0:T(8,128)S(1)} fusion(f32[4,2,3,16,256]{4,3,2,1,0:T(8,128)S(1)} %pad_maximum_fusion.14, s32[1024]{0:T(1024)S(1)} %pad_clamp_fusion.3), kind=kCustom, calls=%fused_computation.clone.1 | custom fusion | bytes 786448 | tf_op jit(solution)/shard_map/while/body/eval_jaxpr/gather | solution.py:98
  29.0 7.5 %collective-permute-done = f32[2,2,5,18,256]{4,3,2,0,1:T(8,128)S(1)} collective-permute-done((f32[2,2,5,18,256]{4,3,2,0,1:T(8,128)S(1)}, f32[2,2,5,18,256]{4,3,2,0,1:T(8,128)S(1)}, u32[]{:S(2)}, u32[]{:S(2)}) %collective-permute-start) | collective-permute-done | bytes 368672 | tf_op jit(solution)/shard_map/while/body/eval_jaxpr/ppermute | solution.py:29
  36.8 0.2 fusion.35
  37.1 0.3 subtract_reduce_fusion.3
  37.7 0.6 %gather_fusion = f32[4,2,3,16,256]{4,3,2,1,0:T(8,128)S(1)} fusion(f32[4,2,3,16,256]{4,3,2,1,0:T(8,128)S(1)} %pad_maximum_fusion.14, s32[1024]{0:T(1024)S(1)} %pad_clamp_fusion.3), kind=kCustom, calls=%fused_computation.clone.1 | custom fusion | bytes 786448 | tf_op jit(solution)/shard_map/while/body/eval_jaxpr/gather | solution.py:98
  38.4 7.5 %collective-permute-done = f32[2,2,5,18,256]{4,3,2,0,1:T(8,128)S(1)} collective-permute-done((f32[2,2,5,18,256]{4,3,2,0,1:T(8,128)S(1)}, f32[2,2,5,18,256]{4,3,2,0,1:T(8,128)S(1)}, u32[]{:S(2)}, u32[]{:S(2)}) %collective-permute-start) | collective-permute-done | bytes 368672 | tf_op jit(solution)/shard_map/while/body/eval_jaxpr/ppermute | solution.py:29
  46.2 0.2 fusion.35
  46.5 0.3 subtract_reduce_fusion.3
  46.9 0.7 %copy.19 = f32[2,2,5,16,256]{4,3,2,1,0:T(8,128)} copy(f32[2,2,5,16,256]{4,3,2,0,1:T(8,128)S(1)} %get-tuple-element.231) | data formatting | bytes 655360 | tf_op jit(solution)/shard_map/while | solution.py:166
  (64 shorter events, 2.9 us)
Async XLA Ops:
  0.0 6.2 %copy-start.1 = (f32[16,256]{1,0:T(8,128)S(1)}, f32[16,256]{1,0:T(8,128)}, u32[]{:S(2)}) copy-start(f32[16,256]{1,0:T(8,128)} %param.11) | copy-start | bytes 49156
  0.0 6.4 %copy-start.2 = (f32[2,2,3,16,256]{4,3,2,1,0:T(8,128)S(1)}, f32[2,2,3,16,256]{4,3,2,1,0:T(8,128)}, u32[]{:S(2)}) copy-start(f32[2,2,3,16,256]{4,3,2,1,0:T(8,128)} %param.10) | copy-start | bytes 589828
  1.1 15.2 %collective-permute-start.2 = (f32[21,1,256]{2,1,0:T(1,128)S(1)}, f32[21,1,256]{2,1,0:T(1,128)S(1)}, u32[]{:S(2)}, u32[]{:S(2)}) collective-permute-start(f32[21,1,256]{2,1,0:T(1,128)S(1)} %get-tuple-element.304), channel_id=1, source_target_pairs={{1,0},{2,1},{3,2},{0,3},{5,4},{6,5},{7,6},{4,7},{9,8},{10,9},{11,1... | collective-permute-start | bytes 64520 | tf_op jit(solution)/shard_map/ppermute | solution.py:19
  6.2 10.1 %collective-permute-start.1 = (f32[21,1,256]{2,1,0:T(1,128)S(1)}, f32[21,1,256]{2,1,0:T(1,128)S(1)}, u32[]{:S(2)}, u32[]{:S(2)}) collective-permute-start(f32[21,1,256]{2,1,0:T(1,128)S(1)} %get-tuple-element.303), channel_id=1, source_target_pairs={{0,1},{1,2},{2,3},{3,0},{4,5},{5,6},{6,7},{7,4},{8,9},{9,10},{10,1... | collective-permute-start | bytes 64520 | tf_op jit(solution)/shard_map/ppermute | solution.py:17
  15.0 0.7 %copy-start.3 = (s32[4]{0:T(128)S(1)}, s32[4]{0:T(128)}, u32[]{:S(2)}) copy-start(s32[4]{0:T(128)} %constant.163) | copy-start | bytes 52
  16.3 1.0 %copy-start = (f32[2,2,5,16,256]{4,3,2,1,0:T(8,128)S(1)}, f32[2,2,5,16,256]{4,3,2,1,0:T(8,128)}, u32[]{:S(2)}) copy-start(f32[2,2,5,16,256]{4,3,2,1,0:T(8,128)} %param.9) | copy-start | bytes 983044
  18.8 8.3 %collective-permute-start = (f32[2,2,5,18,256]{4,3,2,0,1:T(8,128)S(1)}, f32[2,2,5,18,256]{4,3,2,0,1:T(8,128)S(1)}, u32[]{:S(2)}, u32[]{:S(2)}) collective-permute-start(f32[2,2,5,18,256]{4,3,2,0,1:T(8,128)S(1)} %get-tuple-element.397), channel_id=1, source_target_pairs={{0,4},{4,8},{8,12},{12,0},{1,5},{5,9},{9,13},{13,1},{2,6},{6,10},{... | collective-permute-start | bytes 1105928 | tf_op jit(solution)/shard_map/while/body/eval_jaxpr/ppermute | solution.py:29
  28.2 8.3 %collective-permute-start = (f32[2,2,5,18,256]{4,3,2,0,1:T(8,128)S(1)}, f32[2,2,5,18,256]{4,3,2,0,1:T(8,128)S(1)}, u32[]{:S(2)}, u32[]{:S(2)}) collective-permute-start(f32[2,2,5,18,256]{4,3,2,0,1:T(8,128)S(1)} %get-tuple-element.397), channel_id=1, source_target_pairs={{0,4},{4,8},{8,12},{12,0},{1,5},{5,9},{9,13},{13,1},{2,6},{6,10},{... | collective-permute-start | bytes 1105928 | tf_op jit(solution)/shard_map/while/body/eval_jaxpr/ppermute | solution.py:29
  37.6 8.3 %collective-permute-start = (f32[2,2,5,18,256]{4,3,2,0,1:T(8,128)S(1)}, f32[2,2,5,18,256]{4,3,2,0,1:T(8,128)S(1)}, u32[]{:S(2)}, u32[]{:S(2)}) collective-permute-start(f32[2,2,5,18,256]{4,3,2,0,1:T(8,128)S(1)} %get-tuple-element.397), channel_id=1, source_target_pairs={{0,4},{4,8},{8,12},{12,0},{1,5},{5,9},{9,13},{13,1},{2,6},{6,10},{... | collective-permute-start | bytes 1105928 | tf_op jit(solution)/shard_map/while/body/eval_jaxpr/ppermute | solution.py:29
where the time goes:
time: 47.9 us; the launch traced here: 47.7 us
  waiting for transfers between devices  22.2 us (46%)
  blocking collectives  8.62 us (18%)
  local copies, waits for them, and re-layouts  6.52 us (14%)
  starting transfers between devices  5.62 us (12%)
  other arithmetic  4.13 us (9%)
    ppermute x3, waiting for transfers between devices, shifted(): return lax.ppermute(value, axis, pairs)  22.2 us
    all_gather x1, blocking collectives, shards(): whole_base = lax.all_gather(base_flow, 'harm', axis=0, tiled=True)  8.62 us
    ppermute x1, starting transfers between devices, extended(): lax.ppermute(head, axis, [((i + 1) % count, i) for i in range(count)])  5.1 us
    gather x4, local copies, waits for them, and re-layouts, block_terms(): chosen = blocks[index_table]  2.3 us
    unnamed x11, local copies, waits for them, and re-layouts  1.54 us
    reduce_sum x4, other arithmetic, block_terms(): jnp.sum(real_part, axis=1)  1.12 us
    slice x1, other arithmetic, extended(): lax.slice_in_dim(cells, cells.shape[dim] - width, cells.shape[dim], axis=...  1.1 us
    slice x8, local copies, waits for them, and re-layouts, split_rows(): grad_y = 0.5 * (jnp.roll(middle, -1, -1) - jnp.roll(middle, 1, -1))  1.09 us
  transfers between devices with their start and end apart: 5, of which 3 were waited for; matrix products, arithmetic and copies ran while one was open for 6% of the time, Pallas kernels for 0%

commit v1 on v0

--- a/solution.py
+++ b/solution.py
@@ -1,7 +1,11 @@
+import functools
+
 import jax
 import jax.numpy as jnp
 import numpy as np
 from jax import lax
+from jax.experimental import pallas as pl
+from jax.experimental.pallas import tpu as pltpu
 from jax.sharding import PartitionSpec as P
 
 omega_base = 0.25
@@ -167,14 +171,323 @@
     return summed
 
 
+def ceil_to(count, unit):
+    return -(-count // unit) * unit
+
+
+def block_call(kernel, outs, scratch=()):
+    shapes = [jax.ShapeDtypeStruct(shape, jnp.float32) for shape in outs]
+    return pl.pallas_call(
+        kernel,
+        out_shape=shapes,
+        out_specs=[pl.BlockSpec(memory_space=pltpu.VMEM)] * len(outs),
+        scratch_shapes=[pltpu.VMEM(shape, jnp.float32) for shape in scratch],
+    )
+
+
+def lanes_next(value):
+    return pltpu.roll(value, value.shape[1] - 1, 1)
+
+
+def lanes_before(value):
+    return pltpu.roll(value, 1, 1)
+
+
+def rows_next(value, below):
+    count = value.shape[0]
+    row = lax.broadcasted_iota(jnp.int32, value.shape, 0)
+    return jnp.where(row == count - 1, below, pltpu.roll(value, count - 1, 0))
+
+
+def rows_before(value, above):
+    row = lax.broadcasted_iota(jnp.int32, value.shape, 0)
+    return jnp.where(row == 0, above, pltpu.roll(value, 1, 0))
+
+
+class Sizes:
+    def __init__(self, perturbation, groups):
+        self.local, _, self.fields, self.width, self.columns = perturbation.shape
+        self.groups = groups
+        self.half = self.width // 2
+        self.total = self.local * groups
+        self.components = self.local * 2 * self.fields
+        self.edge = ceil_to(self.components + 1, 8)
+        cut = self.fields // 2
+        self.chunks = ((0, cut), (cut, self.fields))
+
+    def at(self, harmonic, part, field):
+        return (harmonic * 2 + part) * self.fields + field
+
+    def block(self, chunk, harmonic, part, field):
+        first, last = self.chunks[chunk]
+        start = ((harmonic * 2 + part) * (last - first) + field - first) * self.half
+        return slice(start, start + self.half)
+
+    def block_rows(self, chunk):
+        first, last = self.chunks[chunk]
+        return self.local * 2 * (last - first) * self.half
+
+    def each(self, fields=None):
+        for harmonic in range(self.local):
+            for part in range(2):
+                for field in fields if fields is not None else range(self.fields):
+                    yield harmonic, part, field
+
+
+def pack_kernel(sizes, q_ref, visc_ref, first_ref, second_ref, outer_ref, other_ref):
+    chip = lax.axis_index("harm") // 2
+    lower = chip == 0
+    far = pl.multiple_of((1 - chip) * sizes.half, sizes.half)
+    last, half = sizes.width - 1, sizes.half
+    messages = (first_ref, second_ref)
+    inner_at = sizes.block_rows(0)
+    for harmonic, part, field in sizes.each():
+        chunk = 0 if field < sizes.chunks[0][1] else 1
+        value = q_ref[harmonic, part, field, pl.ds(far, half), :]
+        messages[chunk][sizes.block(chunk, harmonic, part, field), :] = value
+        at = sizes.at(harmonic, part, field)
+        top = q_ref[harmonic, part, field, 0:1, :]
+        bottom = q_ref[harmonic, part, field, last : last + 1, :]
+        outer_ref[at : at + 1, :] = jnp.where(lower, bottom, top)
+        other_ref[at : at + 1, :] = jnp.where(lower, top, bottom)
+        above = q_ref[harmonic, part, field, half - 1 : half, :]
+        below = q_ref[harmonic, part, field, half : half + 1, :]
+        first_ref[inner_at + at : inner_at + at + 1, :] = jnp.where(lower, above, below)
+    at = sizes.components
+    top, bottom = visc_ref[0:1, :], visc_ref[last : last + 1, :]
+    outer_ref[at : at + 1, :] = jnp.where(lower, bottom, top)
+    other_ref[at : at + 1, :] = jnp.where(lower, top, bottom)
+    spare = jnp.zeros((sizes.edge - at - 1, sizes.columns), jnp.float32)
+    outer_ref[at + 1 :, :] = spare
+    other_ref[at + 1 :, :] = spare
+    first_ref[inner_at + at :, :] = jnp.zeros((sizes.edge - at, sizes.columns), jnp.float32)
+
+
+def own_kernel(sizes, q_ref, visc_ref, outer_ref, other_ref, sum_ref):
+    me = lax.axis_index("harm")
+    lower = me // 2 == 0
+
+    def neighbours(value, at):
+        outer, other = outer_ref[at : at + 1, :], other_ref[at : at + 1, :]
+        above, below = jnp.where(lower, outer, other), jnp.where(lower, other, outer)
+        return rows_next(value, below), rows_before(value, above)
+
+    center = visc_ref[...]
+    east_visc, west_visc = neighbours(center, sizes.components)
+    east, west = 0.5 * (center + east_visc), 0.5 * (center + west_visc)
+    north = 0.5 * (center + lanes_next(center))
+    south = 0.5 * (center + lanes_before(center))
+    for harmonic in range(sizes.local):
+        number = me * sizes.local + harmonic
+        signed = jnp.where(number < sizes.total // 2, number, number - sizes.total)
+        frequency = omega_base * signed.astype(jnp.float32)
+        for part in range(2):
+            terms = {}
+            for field in range(sizes.fields):
+                value = q_ref[harmonic, part, field]
+                x_next, x_before = neighbours(value, sizes.at(harmonic, part, field))
+                y_next, y_before = lanes_next(value), lanes_before(value)
+                damping = (
+                    east * (x_next - value)
+                    - west * (value - x_before)
+                    + north * (y_next - value)
+                    - south * (value - y_before)
+                )
+                turned = q_ref[harmonic, 1 - part, field]
+                turn = -frequency if part == 0 else frequency
+                terms[field] = turn * turned - damping
+                if field == 1:
+                    dilation = 0.5 * (x_next - x_before)
+                elif field == 2:
+                    dilation = dilation + 0.5 * (y_next - y_before)
+                elif field == 4:
+                    terms[1] = terms[1] + 0.5 * (x_next - x_before)
+                    terms[2] = terms[2] + 0.5 * (y_next - y_before)
+            terms[0] = terms[0] + dilation
+            terms[4] = terms[4] + dilation
+            for field in range(sizes.fields):
+                sum_ref[harmonic, part, field] = terms[field]
+
+
+def couple_kernel(sizes, chunk, *refs):
+    base_refs, (q_own, q_sib), message_refs = refs[0:4], refs[4:6], refs[6:8]
+    inner_refs, outer_refs = refs[8:10], refs[10:14]
+    own_ref, back_ref, base, values, slopes_x, slopes_y = refs[14:]
+    me = lax.axis_index("harm")
+    chip = me // 2
+    lower = chip == 0
+    half, total = sizes.half, sizes.total
+    near = pl.multiple_of(chip * half, half)
+    first, last = sizes.chunks[chunk]
+    inner_at = sizes.block_rows(0)
+    for place in range(4):
+        group = lax.bitwise_xor(me, place)
+        rows = pl.ds(near, half) if place < 2 else slice(0, half)
+        for harmonic in range(sizes.local):
+            number = group * sizes.local + harmonic
+            for part in range(2):
+                for field in range(3):
+                    base[number, part, field] = base_refs[place][harmonic, part, field, rows, :]
+                for field in range(first, last):
+                    at = sizes.at(harmonic, part, field)
+                    outer = outer_refs[place][at : at + 1, :]
+                    if place < 2:
+                        source = (q_own, q_sib)[place]
+                        value = source[harmonic, part, field, rows, :]
+                        inner = jnp.where(
+                            lower,
+                            source[harmonic, part, field, half : half + 1, :],
+                            source[harmonic, part, field, half - 1 : half, :],
+                        )
+                    else:
+                        value = message_refs[place - 2][
+                            sizes.block(chunk, harmonic, part, field), :
+                        ]
+                        inner = inner_refs[place - 2][inner_at + at : inner_at + at + 1, :]
+                    above = jnp.where(lower, outer, inner)
+                    below = jnp.where(lower, inner, outer)
+                    values[number, part, field - first] = value
+                    slopes_x[number, part, field - first] = 0.5 * (
+                        rows_next(value, below) - rows_before(value, above)
+                    )
+                    slopes_y[number, part, field - first] = 0.5 * (
+                        lanes_next(value) - lanes_before(value)
+                    )
+    targets = []
+    for place, ref in ((0, own_ref), (2, back_ref)):
+        for harmonic in range(sizes.local):
+            number = lax.bitwise_xor(me, place) * sizes.local + harmonic
+            targets.append((number, ref, harmonic))
+    for field in range(last - first):
+        sums = [None] * len(targets)
+        for source in range(total):
+            moved = [
+                ref[source, part, field] for ref in (slopes_x, slopes_y, values) for part in (0, 1)
+            ]
+            for place, (number, _, _) in enumerate(targets):
+                at = lax.rem(number - source + total, total)
+                chosen = [base[at, part, term] for term in range(3) for part in (0, 1)]
+                real = imag = None
+                for term in range(3):
+                    c_real, c_imag = chosen[2 * term : 2 * term + 2]
+                    m_real, m_imag = moved[2 * term : 2 * term + 2]
+                    more_real = c_real * m_real - c_imag * m_imag
+                    more_imag = c_real * m_imag + c_imag * m_real
+                    real = more_real if real is None else real + more_real
+                    imag = more_imag if imag is None else imag + more_imag
+                if sums[place] is not None:
+                    real, imag = sums[place][0] + real, sums[place][1] + imag
+                sums[place] = (real, imag)
+        for (_, ref, harmonic), (real, imag) in zip(targets, sums, strict=True):
+            ref[harmonic, 0, field] = real
+            ref[harmonic, 1, field] = imag
+
+
+def join_kernel(sizes, sum_ref, *refs):
+    out_ref = refs[-1]
+    chip = lax.axis_index("harm") // 2
+    near = pl.multiple_of(chip * sizes.half, sizes.half)
+    far = pl.multiple_of((1 - chip) * sizes.half, sizes.half)
+    for chunk, (first, last) in enumerate(sizes.chunks):
+        for harmonic, part, field in sizes.each(range(first, last)):
+            for rows, ref in ((near, refs[2 * chunk]), (far, refs[2 * chunk + 1])):
+                where = (harmonic, part, field, pl.ds(rows, sizes.half), slice(None))
+                out_ref[where] = sum_ref[where] + ref[harmonic, part, field - first]
+
+
+def paired_shards(perturbation, base_flow, viscosity):
+    groups, tiles = lax.axis_size("harm"), lax.axis_size("tile")
+    sizes = Sizes(perturbation, groups)
+    me = lax.axis_index("harm")
+    chip = me // 2
+
+    def to_chip(value):
+        return lax.ppermute(value, "harm", [(i, i ^ 2) for i in range(groups)])
+
+    def to_core(value):
+        return lax.ppermute(value, "harm", [(i, i ^ 1) for i in range(groups)])
+
+    def along_tile(value, steps, across):
+        pairs = []
+        for group in range(groups):
+            step = steps[group // 2]
+            for tile in range(tiles):
+                target = (group ^ 2 if across else group) * tiles + (tile + step) % tiles
+                pairs.append((group * tiles + tile, target))
+        return lax.ppermute(value, ("harm", "tile"), pairs)
+
+    base_half = lax.dynamic_slice_in_dim(base_flow, (1 - chip) * sizes.half, sizes.half, 3)
+    base_chip = to_chip(base_half)
+    base_core = to_core(base_flow)
+    q_core = to_core(perturbation)
+
+    rows = sizes.block_rows
+    first, second, outer, other = block_call(
+        functools.partial(pack_kernel, sizes),
+        [
+            (rows(0) + sizes.edge, sizes.columns),
+            (rows(1), sizes.columns),
+            (sizes.edge, sizes.columns),
+            (sizes.edge, sizes.columns),
+        ],
+    )(perturbation, viscosity)
+    first_chip = to_chip(first)
+    outer_chip = along_tile(other, (-1, 1), True)
+    outer_own = along_tile(outer, (1, -1), False)
+    other_own = along_tile(other, (-1, 1), False)
+    second_chip = to_chip(second)
+    base_diag = to_core(base_chip)
+    outer_core = to_core(outer_own)
+    outer_diag = to_core(outer_chip)
+    first_diag = to_core(first_chip)
+    second_diag = to_core(second_chip)
+
+    own = block_call(functools.partial(own_kernel, sizes), [perturbation.shape])(
+        perturbation, viscosity, outer_own, other_own
+    )[0]
+    parts = []
+    messages = ((first_chip, first_diag), (second_chip, second_diag))
+    for chunk, (begin, end) in enumerate(sizes.chunks):
+        shape = (sizes.local, 2, end - begin, sizes.half, sizes.columns)
+        moved = (sizes.total, 2, end - begin, sizes.half, sizes.columns)
+        kept, back = block_call(
+            functools.partial(couple_kernel, sizes, chunk),
+            [shape, shape],
+            [(sizes.total, 2, 3, sizes.half, sizes.columns), moved, moved, moved],
+        )(
+            base_flow,
+            base_core,
+            base_chip,
+            base_diag,
+            perturbation,
+            q_core,
+            *messages[chunk],
+            first_chip,
+            first_diag,
+            outer_own,
+            outer_core,
+            outer_chip,
+            outer_diag,
+        )
+        parts += [kept, to_chip(back)]
+    return block_call(functools.partial(join_kernel, sizes), [perturbation.shape])(own, *parts)[0]
+
+
 def solution(mesh):
     placed = (
         P("harm", None, None, ("parts", "tile"), None),
         P("harm", None, None, ("parts", "tile"), None),
         P(("parts", "tile"), None),
     )
+
+    def chosen(perturbation, base_flow, viscosity):
+        two_chips = mesh.shape["harm"] == 2 * 2
+        whole_tiles = perturbation.shape[3] % 16 == 0 and perturbation.shape[4] % 128 == 0
+        body = paired_shards if two_chips and whole_tiles else shards
+        return body(perturbation, base_flow, viscosity)
+
     return jax.shard_map(
-        shards,
+        chosen,
         mesh=mesh,
         in_specs=placed,
         out_specs=P("harm", None, None, ("parts", "tile"), None),

time: 47.9 us -> 43.6 us (0.910)
  Pallas kernels: 0 us -> 11.3 us
  blocking collectives: 8.62 us -> 0 us
  starting transfers between devices: 5.62 us -> 10.5 us
  waiting for transfers between devices: 22.2 us -> 17.8 us
  other arithmetic: 4.13 us -> 0 us
  local copies, waits for them, and re-layouts: 6.52 us -> 3.58 us
    pallas_call x0 -> x5, Pallas kernels: none -> 11.3 us  [the longest x2 5.62 us: paired_shards(): block_call(functools.partial(couple_kernel, sizes, chunk), [shape, shape]...]
    all_gather x1 -> x0, blocking collectives: 8.62 us -> none  [shards(): whole_base = lax.all_gather(base_flow, 'harm', axis=0, tiled=True)]
    ppermute x5 -> x15, starting transfers between devices: 5.62 us -> 10.5 us  [the longest x3 6.01 us: along_tile(): return lax.ppermute(value, ('harm', 'tile'), pairs)]
    ppermute x5 -> x15, waiting for transfers between devices: 22.2 us -> 17.8 us  [the longest x3 9.62 us: along_tile(): return lax.ppermute(value, ('harm', 'tile'), pairs)]
    gather x4 -> x0, local copies, waits for them, and re-layouts: 2.3 us -> none  [block_terms(): chosen = blocks[index_table]]
    slice x10 -> x0, local copies, waits for them, and re-layouts: 1.24 us -> none  [the longest x8 1.09 us: split_rows(): grad_y = 0.5 * (jnp.roll(middle, -1, -1) - jnp.roll(middle, 1, -1))]
    unnamed x11 -> x36, local copies, waits for them, and re-layouts: 1.54 us -> 2.67 us
    reduce_sum x4 -> x0, other arithmetic: 1.12 us -> none  [block_terms(): jnp.sum(real_part, axis=1)]
  transfers between devices with their start and end apart: 5 -> 15, of which waited for: 3 -> 7; matrix products, arithmetic and copies ran while one was open for 6% -> 2% of each run, Pallas kernels for 0% -> 11%
where the time goes in v1:
time: 43.6 us; the launch traced here: 43.3 us
  waiting for transfers between devices  17.8 us (41%)
  Pallas kernels  11.3 us (26%)
  starting transfers between devices  10.5 us (24%)
  local copies, waits for them, and re-layouts  3.58 us (8%)
    ppermute x3, waiting for transfers between devices, along_tile(): return lax.ppermute(value, ('harm', 'tile'), pairs)  9.62 us
    ppermute x5, waiting for transfers between devices, to_chip(): return lax.ppermute(value, 'harm', [(i, i ^ 2) for i in range(groups)])  6.85 us
    ppermute x3, starting transfers between devices, along_tile(): return lax.ppermute(value, ('harm', 'tile'), pairs)  6.01 us
    pallas_call x2, Pallas kernels, paired_shards(): block_call(functools.partial(couple_kernel, sizes, chunk), [shape, shape]...  5.62 us
    ppermute x5, starting transfers between devices, to_chip(): return lax.ppermute(value, 'harm', [(i, i ^ 2) for i in range(groups)])  4.38 us
    unnamed x36, local copies, waits for them, and re-layouts  2.67 us
    pallas_call x1, Pallas kernels, paired_shards(): block_call(functools.partial(own_kernel, sizes), [perturbation.shape])  2.05 us
    pallas_call x1, Pallas kernels, paired_shards(): block_call(functools.partial(join_kernel, sizes), [perturbation.shape])  1.87 us
  transfers between devices with their start and end apart: 15, of which 7 were waited for; matrix products, arithmetic and copies ran while one was open for 2% of the time, Pallas kernels for 11%

profile of v1, /device:TPU:0, one launch (start us, length us, event | category | flops | bytes accessed | tf_op | source)
XLA Modules:
  0.0 43.3 jit_solution(10267642634308112950)
XLA Ops:
  0.0 1.8 %shard_map.37 = (f32[88,256]{1,0:T(8,128)}, f32[96,256]{1,0:T(8,128)}, f32[24,256]{1,0:T(8,128)}, f32[24,256]{1,0:T(8,128)}) custom-call(f32[2,2,5,16,256]{4,3,2,1,0:T(8,128)} %refs_4_.3, f32[16,256]{1,0:T(8,128)} %visc_ref.3), custom_call_target="tpu_custom_call" | custom-call | tf_op jit(solution)/shard_map/pallas_call | solution.py:425
  1.8 6.0 %collective-permute-start.9 = (f32[24,256]{1,0:T(8,128)}, f32[24,256]{1,0:T(8,128)S(1)}, u32[]{:S(2)}, u32[]{:S(2)}) collective-permute-start(f32[24,256]{1,0:T(8,128)} %get-tuple-element.14), channel_id=1, source_target_pairs={{0,11},{1,8},{2,9},{3,10},{4,15},{5,12},{6,13},{7,14},{8,1},{9,2},... | collective-permute-start | bytes 73736 | tf_op jit(solution)/shard_map/ppermute | solution.py:417
  7.8 2.1 %collective-permute-done.9.refs_12_ = f32[24,256]{1,0:T(8,128)S(1)} collective-permute-done((f32[24,256]{1,0:T(8,128)}, f32[24,256]{1,0:T(8,128)S(1)}, u32[]{:S(2)}, u32[]{:S(2)}) %collective-permute-start.9) | collective-permute-done | bytes 24608 | tf_op jit(solution)/shard_map/ppermute | solution.py:417
  9.9 3.7 %collective-permute-done.outer_ref.refs_10_ = f32[24,256]{1,0:T(8,128)S(1)} collective-permute-done((f32[24,256]{1,0:T(8,128)}, f32[24,256]{1,0:T(8,128)S(1)}, u32[]{:S(2)}, u32[]{:S(2)}) %collective-permute-start) | collective-permute-done | bytes 24608 | tf_op jit(solution)/shard_map/ppermute | solution.py:417
  13.6 0.9 %constant_dynamic-slice_fusion = f32[2,2,3,8,256]{4,3,2,1,0:T(8,128)S(1)} fusion(f32[2,2,3,16,256]{4,3,2,1,0:T(8,128)} %refs_0_.3, s32[]{:T(128)S(6)} %select_n.9), kind=kLoop, calls=%fused_computation | loop fusion | bytes 196612 | tf_op jit(solution)/shard_map/dynamic_slice | solution.py:419
  14.5 0.1 collective-permute-start.3
  14.6 2.0 %collective-permute-start.12 = (f32[96,256]{1,0:T(8,128)}, f32[96,256]{1,0:T(8,128)S(1)}, u32[]{:S(2)}, u32[]{:S(2)}) collective-permute-start(f32[96,256]{1,0:T(8,128)} %get-tuple-element.18), channel_id=1, source_target_pairs={{0,8},{4,12},{8,0},{12,4},{1,9},{5,13},{9,1},{13,5},{2,10},{6,14},... | collective-permute-start | bytes 294920 | tf_op jit(solution)/shard_map/ppermute | solution.py:405
  16.7 0.3 collective-permute-start.6
  17.0 3.2 %collective-permute-done.3.refs_2_ = f32[2,2,3,8,256]{4,3,2,1,0:T(8,128)S(1)} collective-permute-done((f32[2,2,3,8,256]{4,3,2,1,0:T(8,128)S(1)}, f32[2,2,3,8,256]{4,3,2,1,0:T(8,128)S(1)}, u32[]{:S(2)}, u32[]{:S(2)}) %collective-permute-start.3) | collective-permute-done | bytes 98336 | tf_op jit(solution)/shard_map/ppermute | solution.py:405
  20.2 2.1 %collective-permute-done.12.refs_6_ = f32[96,256]{1,0:T(8,128)S(1)} collective-permute-done((f32[96,256]{1,0:T(8,128)}, f32[96,256]{1,0:T(8,128)S(1)}, u32[]{:S(2)}, u32[]{:S(2)}) %collective-permute-start.12) | collective-permute-done | bytes 98336 | tf_op jit(solution)/shard_map/ppermute | solution.py:405
  22.3 1.5 %collective-permute-done.6.refs_6_.refs_8_ = f32[88,256]{1,0:T(8,128)S(1)} collective-permute-done((f32[88,256]{1,0:T(8,128)}, f32[88,256]{1,0:T(8,128)S(1)}, u32[]{:S(2)}, u32[]{:S(2)}) %collective-permute-start.6) | collective-permute-done | bytes 90144 | tf_op jit(solution)/shard_map/ppermute | solution.py:405
  23.9 1.3 %collective-permute-done.7.refs_7_.refs_9_ = f32[88,256]{1,0:T(8,128)S(1)} collective-permute-done((f32[88,256]{1,0:T(8,128)S(1)}, f32[88,256]{1,0:T(8,128)S(1)}, u32[]{:S(2)}, u32[]{:S(2)}) %collective-permute-start.7) | collective-permute-done | bytes 90144 | tf_op jit(solution)/shard_map/ppermute | solution.py:408
  25.2 0.5 %copy-done.4 = f32[88,256]{1,0:T(8,128)} copy-done((f32[88,256]{1,0:T(8,128)}, f32[88,256]{1,0:T(8,128)S(1)}, u32[]{:S(2)}) %copy-start.4) | copy-done | bytes 90136
  25.8 0.1 copy-done.5
  25.9 0.7 %copy-done.1 = f32[2,2,5,16,256]{4,3,2,1,0:T(8,128)} copy-done((f32[2,2,5,16,256]{4,3,2,1,0:T(8,128)}, f32[2,2,5,16,256]{4,3,2,1,0:T(8,128)S(1)}, u32[]{:S(2)}) %copy-start.1) | copy-done | bytes 327704
  26.6 3.0 %shard_map.40 = (f32[2,2,3,8,256]{4,3,2,1,0:T(8,128)}, f32[2,2,3,8,256]{4,3,2,1,0:T(8,128)}) custom-call(f32[2,2,3,16,256]{4,3,2,1,0:T(8,128)} %refs_0_.3, f32[2,2,3,16,256]{4,3,2,1,0:T(8,128)} %copy-done.5, f32[2,2,3,8,256]{4,3,2,1,0:T(8,128)} %copy-done.6, f32[2,2,3,8,256]{4,3,2,1,0:T(8,128)} %copy-done.7, f32[2,2,5,16,256]{4,3,2,1,0:T(8,128)} %refs_4_.3, ...), custom_call_target="tpu_custom_call" | custom-call | tf_op jit(solution)/shard_map/pallas_call | solution.py:453
  29.6 0.3 collective-permute-start.14
  29.9 2.7 %shard_map.39 = (f32[2,2,2,8,256]{4,3,2,1,0:T(8,128)}, f32[2,2,2,8,256]{4,3,2,1,0:T(8,128)}) custom-call(f32[2,2,3,16,256]{4,3,2,1,0:T(8,128)} %refs_0_.3, f32[2,2,3,16,256]{4,3,2,1,0:T(8,128)} %copy-done.5, f32[2,2,3,8,256]{4,3,2,1,0:T(8,128)} %copy-done.6, f32[2,2,3,8,256]{4,3,2,1,0:T(8,128)} %copy-done.7, f32[2,2,5,16,256]{4,3,2,1,0:T(8,128)} %refs_4_.3, ...), custom_call_target="tpu_custom_call" | custom-call | tf_op jit(solution)/shard_map/pallas_call | solution.py:453
  32.5 1.8 %collective-permute-start.11 = (f32[2,2,2,8,256]{4,3,2,1,0:T(8,128)}, f32[2,2,2,8,256]{4,3,2,1,0:T(8,128)S(1)}, u32[]{:S(2)}, u32[]{:S(2)}) collective-permute-start(f32[2,2,2,8,256]{4,3,2,1,0:T(8,128)} %get-tuple-element.17), channel_id=1, source_target_pairs={{0,8},{4,12},{8,0},{12,4},{1,9},{5,13},{9,1},{13,5},{2,10},{6,14},... | collective-permute-start | bytes 196616 | tf_op jit(solution)/shard_map/ppermute | solution.py:405
  34.3 3.8 %collective-permute-done.1.other_ref = f32[24,256]{1,0:T(8,128)S(1)} collective-permute-done((f32[24,256]{1,0:T(8,128)S(1)}, f32[24,256]{1,0:T(8,128)S(1)}, u32[]{:S(2)}, u32[]{:S(2)}) %collective-permute-start.1) | collective-permute-done | bytes 24608 | tf_op jit(solution)/shard_map/ppermute | solution.py:417
  38.1 0.6 %copy-done.16 = f32[24,256]{1,0:T(8,128)} copy-done((f32[24,256]{1,0:T(8,128)}, f32[24,256]{1,0:T(8,128)S(1)}, u32[]{:S(2)}) %copy-start.16) | copy-done | bytes 24600
  38.7 2.1 %shard_map.38.sum_ref = f32[2,2,5,16,256]{4,3,2,1,0:T(8,128)} custom-call(f32[2,2,5,16,256]{4,3,2,1,0:T(8,128)} %refs_4_.3, f32[16,256]{1,0:T(8,128)} %visc_ref.3, f32[24,256]{1,0:T(8,128)} %copy-done.8, f32[24,256]{1,0:T(8,128)} %copy-done.16), custom_call_target="tpu_custom_call" | custom-call | tf_op jit(solution)/shard_map/pallas_call | solution.py:445
  40.8 0.6 %copy-done.15 = f32[2,2,2,8,256]{4,3,2,1,0:T(8,128)} copy-done((f32[2,2,2,8,256]{4,3,2,1,0:T(8,128)}, f32[2,2,2,8,256]{4,3,2,1,0:T(8,128)S(1)}, u32[]{:S(2)}) %copy-start.15) | copy-done | bytes 65560
  41.4 1.9 %shard_map.41 = f32[2,2,5,16,256]{4,3,2,1,0:T(8,128)} custom-call(f32[2,2,5,16,256]{4,3,2,1,0:T(8,128)} %shard_map.38.sum_ref, f32[2,2,2,8,256]{4,3,2,1,0:T(8,128)} %get-tuple-element.16.refs_0_, f32[2,2,2,8,256]{4,3,2,1,0:T(8,128)} %copy-done.15, f32[2,2,3,8,256]{4,3,2,1,0:T(8,128)} %get-tuple-element.19.refs_2_, f32[2,2,3,8,256]{4,3,2,1,0:T(8,128)} %copy-done.10), custom_call_target="tpu_custom_call" | custom-call | tf_op jit(solution)/shard_map/pallas_call | solution.py:473
  (48 shorter events, 0.3 us)
Async XLA Ops:
  0.0 7.8 %copy-start = (f32[2,2,5,16,256]{4,3,2,1,0:T(8,128)S(1)}, f32[2,2,5,16,256]{4,3,2,1,0:T(8,128)}, u32[]{:S(2)}) copy-start(f32[2,2,5,16,256]{4,3,2,1,0:T(8,128)} %refs_4_.3) | copy-start | bytes 983044
  1.8 14.9 %copy-start.2 = (f32[2,2,3,16,256]{4,3,2,1,0:T(8,128)S(1)}, f32[2,2,3,16,256]{4,3,2,1,0:T(8,128)}, u32[]{:S(2)}) copy-start(f32[2,2,3,16,256]{4,3,2,1,0:T(8,128)} %refs_0_.3) | copy-start | bytes 589828
  1.8 8.1 %collective-permute-start.9 = (f32[24,256]{1,0:T(8,128)}, f32[24,256]{1,0:T(8,128)S(1)}, u32[]{:S(2)}, u32[]{:S(2)}) collective-permute-start(f32[24,256]{1,0:T(8,128)} %get-tuple-element.14), channel_id=1, source_target_pairs={{0,11},{1,8},{2,9},{3,10},{4,15},{5,12},{6,13},{7,14},{8,1},{9,2},... | collective-permute-start | bytes 73736 | tf_op jit(solution)/shard_map/ppermute | solution.py:417
  7.8 5.8 %collective-permute-start = (f32[24,256]{1,0:T(8,128)}, f32[24,256]{1,0:T(8,128)S(1)}, u32[]{:S(2)}, u32[]{:S(2)}) collective-permute-start(f32[24,256]{1,0:T(8,128)} %get-tuple-element.13), channel_id=1, source_target_pairs={{0,1},{1,2},{2,3},{3,0},{4,5},{5,6},{6,7},{7,4},{8,11},{9,8},{10,9... | collective-permute-start | bytes 73736 | tf_op jit(solution)/shard_map/ppermute | solution.py:417
  7.8 17.4 %collective-permute-start.5 = (f32[2,2,5,16,256]{4,3,2,1,0:T(8,128)S(1)}, f32[2,2,5,16,256]{4,3,2,1,0:T(8,128)S(1)}, u32[]{:S(2)}, u32[]{:S(2)}) collective-permute-start(f32[2,2,5,16,256]{4,3,2,1,0:T(8,128)S(1)} %copy-done), channel_id=1, source_target_pairs={{0,4},{4,0},{8,12},{12,8},{1,5},{5,1},{9,13},{13,9},{2,6},{6,2},{1... | collective-permute-start | bytes 983048 | tf_op jit(solution)/shard_map/ppermute | solution.py:408
  9.9 4.6 %copy-start.12 = (f32[24,256]{1,0:T(8,128)}, f32[24,256]{1,0:T(8,128)S(1)}, u32[]{:S(2)}) copy-start(f32[24,256]{1,0:T(8,128)S(1)} %collective-permute-done.9.refs_12_) | copy-start | bytes 73732
  9.9 6.7 %collective-permute-start.10 = (f32[24,256]{1,0:T(8,128)S(1)}, f32[24,256]{1,0:T(8,128)S(1)}, u32[]{:S(2)}, u32[]{:S(2)}) collective-permute-start(f32[24,256]{1,0:T(8,128)S(1)} %collective-permute-done.9.refs_12_), channel_id=1, source_target_pairs={{0,4},{4,0},{8,12},{12,8},{1,5},{5,1},{9,13},{13,9},{2,6},{6,2},{1... | collective-permute-start | bytes 73736 | tf_op jit(solution)/shard_map/ppermute | solution.py:408
  13.6 3.1 %collective-permute-start.8 = (f32[24,256]{1,0:T(8,128)S(1)}, f32[24,256]{1,0:T(8,128)S(1)}, u32[]{:S(2)}, u32[]{:S(2)}) collective-permute-start(f32[24,256]{1,0:T(8,128)S(1)} %collective-permute-done.outer_ref.refs_10_), channel_id=1, source_target_pairs={{0,4},{4,0},{8,12},{12,8},{1,5},{5,1},{9,13},{13,9},{2,6},{6,2},{1... | collective-permute-start | bytes 73736 | tf_op jit(solution)/shard_map/ppermute | solution.py:408
  14.5 5.7 %collective-permute-start.3 = (f32[2,2,3,8,256]{4,3,2,1,0:T(8,128)S(1)}, f32[2,2,3,8,256]{4,3,2,1,0:T(8,128)S(1)}, u32[]{:S(2)}, u32[]{:S(2)}) collective-permute-start(f32[2,2,3,8,256]{4,3,2,1,0:T(8,128)S(1)} %constant_dynamic-slice_fusion), channel_id=1, source_target_pairs={{0,8},{4,12},{8,0},{12,4},{1,9},{5,13},{9,1},{13,5},{2,10},{6,14},... | collective-permute-start | bytes 294920 | tf_op jit(solution)/shard_map/ppermute | solution.py:405
  14.6 7.7 %collective-permute-start.12 = (f32[96,256]{1,0:T(8,128)}, f32[96,256]{1,0:T(8,128)S(1)}, u32[]{:S(2)}, u32[]{:S(2)}) collective-permute-start(f32[96,256]{1,0:T(8,128)} %get-tuple-element.18), channel_id=1, source_target_pairs={{0,8},{4,12},{8,0},{12,4},{1,9},{5,13},{9,1},{13,5},{2,10},{6,14},... | collective-permute-start | bytes 294920 | tf_op jit(solution)/shard_map/ppermute | solution.py:405
  16.6 8.6 %copy-start.13 = (f32[24,256]{1,0:T(8,128)}, f32[24,256]{1,0:T(8,128)S(1)}, u32[]{:S(2)}) copy-start(f32[24,256]{1,0:T(8,128)S(1)} %collective-permute-done.10.refs_13_) | copy-start | bytes 73732
  16.6 8.5 %collective-permute-start.2 = (f32[2,2,3,16,256]{4,3,2,1,0:T(8,128)S(1)}, f32[2,2,3,16,256]{4,3,2,1,0:T(8,128)S(1)}, u32[]{:S(2)}, u32[]{:S(2)}) collective-permute-start(f32[2,2,3,16,256]{4,3,2,1,0:T(8,128)S(1)} %copy-done.2), channel_id=1, source_target_pairs={{0,4},{4,0},{8,12},{12,8},{1,5},{5,1},{9,13},{13,9},{2,6},{6,2},{1... | collective-permute-start | bytes 589832 | tf_op jit(solution)/shard_map/ppermute | solution.py:408
  16.7 8.5 %copy-start.14 = (f32[24,256]{1,0:T(8,128)}, f32[24,256]{1,0:T(8,128)S(1)}, u32[]{:S(2)}) copy-start(f32[24,256]{1,0:T(8,128)S(1)} %collective-permute-done.8.refs_11_) | copy-start | bytes 73732
  16.7 7.1 %collective-permute-start.6 = (f32[88,256]{1,0:T(8,128)}, f32[88,256]{1,0:T(8,128)S(1)}, u32[]{:S(2)}, u32[]{:S(2)}) collective-permute-start(f32[88,256]{1,0:T(8,128)} %get-tuple-element.15), channel_id=1, source_target_pairs={{0,8},{4,12},{8,0},{12,4},{1,9},{5,13},{9,1},{13,5},{2,10},{6,14},... | collective-permute-start | bytes 270344 | tf_op jit(solution)/shard_map/ppermute | solution.py:405
  20.2 5.0 %copy-start.6 = (f32[2,2,3,8,256]{4,3,2,1,0:T(8,128)}, f32[2,2,3,8,256]{4,3,2,1,0:T(8,128)S(1)}, u32[]{:S(2)}) copy-start(f32[2,2,3,8,256]{4,3,2,1,0:T(8,128)S(1)} %collective-permute-done.3.refs_2_) | copy-start | bytes 294916
  20.2 5.0 %collective-permute-start.4 = (f32[2,2,3,8,256]{4,3,2,1,0:T(8,128)S(1)}, f32[2,2,3,8,256]{4,3,2,1,0:T(8,128)S(1)}, u32[]{:S(2)}, u32[]{:S(2)}) collective-permute-start(f32[2,2,3,8,256]{4,3,2,1,0:T(8,128)S(1)} %collective-permute-done.3.refs_2_), channel_id=1, source_target_pairs={{0,4},{4,0},{8,12},{12,8},{1,5},{5,1},{9,13},{13,9},{2,6},{6,2},{1... | collective-permute-start | bytes 294920 | tf_op jit(solution)/shard_map/ppermute | solution.py:408
  22.3 2.9 %copy-start.9 = (f32[96,256]{1,0:T(8,128)}, f32[96,256]{1,0:T(8,128)S(1)}, u32[]{:S(2)}) copy-start(f32[96,256]{1,0:T(8,128)S(1)} %collective-permute-done.12.refs_6_) | copy-start | bytes 294916
  22.3 2.9 %collective-permute-start.13 = (f32[96,256]{1,0:T(8,128)S(1)}, f32[96,256]{1,0:T(8,128)S(1)}, u32[]{:S(2)}, u32[]{:S(2)}) collective-permute-start(f32[96,256]{1,0:T(8,128)S(1)} %collective-permute-done.12.refs_6_), channel_id=1, source_target_pairs={{0,4},{4,0},{8,12},{12,8},{1,5},{5,1},{9,13},{13,9},{2,6},{6,2},{1... | collective-permute-start | bytes 294920 | tf_op jit(solution)/shard_map/ppermute | solution.py:408
  23.9 1.4 %copy-start.3 = (f32[88,256]{1,0:T(8,128)}, f32[88,256]{1,0:T(8,128)S(1)}, u32[]{:S(2)}) copy-start(f32[88,256]{1,0:T(8,128)S(1)} %collective-permute-done.6.refs_6_.refs_8_) | copy-start | bytes 270340
  23.9 1.3 %collective-permute-start.7 = (f32[88,256]{1,0:T(8,128)S(1)}, f32[88,256]{1,0:T(8,128)S(1)}, u32[]{:S(2)}, u32[]{:S(2)}) collective-permute-start(f32[88,256]{1,0:T(8,128)S(1)} %collective-permute-done.6.refs_6_.refs_8_), channel_id=1, source_target_pairs={{0,4},{4,0},{8,12},{12,8},{1,5},{5,1},{9,13},{13,9},{2,6},{6,2},{1... | collective-permute-start | bytes 270344 | tf_op jit(solution)/shard_map/ppermute | solution.py:408
  29.6 4.7 %copy-start.17 = (f32[24,256]{1,0:T(8,128)S(1)}, f32[24,256]{1,0:T(8,128)}, u32[]{:S(2)}) copy-start(f32[24,256]{1,0:T(8,128)} %get-tuple-element.14) | copy-start | bytes 73732
  29.6 11.2 %collective-permute-start.14 = (f32[2,2,3,8,256]{4,3,2,1,0:T(8,128)}, f32[2,2,3,8,256]{4,3,2,1,0:T(8,128)S(1)}, u32[]{:S(2)}, u32[]{:S(2)}) collective-permute-start(f32[2,2,3,8,256]{4,3,2,1,0:T(8,128)} %get-tuple-element.20), channel_id=1, source_target_pairs={{0,8},{4,12},{8,0},{12,4},{1,9},{5,13},{9,1},{13,5},{2,10},{6,14},... | collective-permute-start | bytes 294920 | tf_op jit(solution)/shard_map/ppermute | solution.py:405
  32.5 8.2 %collective-permute-start.11 = (f32[2,2,2,8,256]{4,3,2,1,0:T(8,128)}, f32[2,2,2,8,256]{4,3,2,1,0:T(8,128)S(1)}, u32[]{:S(2)}, u32[]{:S(2)}) collective-permute-start(f32[2,2,2,8,256]{4,3,2,1,0:T(8,128)} %get-tuple-element.17), channel_id=1, source_target_pairs={{0,8},{4,12},{8,0},{12,4},{1,9},{5,13},{9,1},{13,5},{2,10},{6,14},... | collective-permute-start | bytes 196616 | tf_op jit(solution)/shard_map/ppermute | solution.py:405
  34.3 3.8 %collective-permute-start.1 = (f32[24,256]{1,0:T(8,128)S(1)}, f32[24,256]{1,0:T(8,128)S(1)}, u32[]{:S(2)}, u32[]{:S(2)}) collective-permute-start(f32[24,256]{1,0:T(8,128)S(1)} %copy-done.17), channel_id=1, source_target_pairs={{0,3},{1,0},{2,1},{3,2},{4,7},{5,4},{6,5},{7,6},{8,9},{9,10},{10,1... | collective-permute-start | bytes 73736 | tf_op jit(solution)/shard_map/ppermute | solution.py:417
  (9 other events, 6.2 us)

commit v2 on v0

--- a/solution.py
+++ b/solution.py
@@ -1,7 +1,11 @@
+import functools
+
 import jax
 import jax.numpy as jnp
 import numpy as np
 from jax import lax
+from jax.experimental import pallas as pl
+from jax.experimental.pallas import tpu as pltpu
 from jax.sharding import PartitionSpec as P
 
 omega_base = 0.25
@@ -167,14 +171,261 @@
     return summed
 
 
+def ceil_to(count, unit):
+    return -(-count // unit) * unit
+
+
+scoped_bytes = 12 * 1024 * 1024
+in_vmem = pl.BlockSpec(memory_space=pltpu.VMEM)
+anywhere = pl.BlockSpec(memory_space=pl.ANY)
+
+
+def lanes_next(value):
+    return pltpu.roll(value, value.shape[1] - 1, 1)
+
+
+def lanes_before(value):
+    return pltpu.roll(value, 1, 1)
+
+
+def rows_next(value, below):
+    count = value.shape[0]
+    row = lax.broadcasted_iota(jnp.int32, value.shape, 0)
+    return jnp.where(row == count - 1, below, pltpu.roll(value, count - 1, 0))
+
+
+def rows_before(value, above):
+    row = lax.broadcasted_iota(jnp.int32, value.shape, 0)
+    return jnp.where(row == 0, above, pltpu.roll(value, 1, 0))
+
+
+class Sizes:
+    def __init__(self, perturbation, groups):
+        self.local, _, self.fields, self.width, self.columns = perturbation.shape
+        self.groups = groups
+        self.total = self.local * groups
+        self.components = self.local * 2 * self.fields
+        self.edge = ceil_to(self.components + 1, 8)
+        cut = self.fields - 1
+        self.chunks = ((0, cut), (cut, self.fields))
+
+    def at(self, harmonic, part, field):
+        return (harmonic * 2 + part) * self.fields + field
+
+    def chunk_shape(self, chunk, harmonics):
+        first, last = self.chunks[chunk]
+        return (harmonics, 2, last - first, self.width, self.columns)
+
+    def each(self):
+        for harmonic in range(self.local):
+            for part in range(2):
+                for field in range(self.fields):
+                    yield harmonic, part, field
+
+
+def pack_kernel(sizes, q_ref, visc_ref, first_ref, second_ref, up_ref, down_ref):
+    last = sizes.width - 1
+    for harmonic, part, field in sizes.each():
+        at = sizes.at(harmonic, part, field)
+        up_ref[at : at + 1, :] = q_ref[harmonic, part, field, last : last + 1, :]
+        down_ref[at : at + 1, :] = q_ref[harmonic, part, field, 0:1, :]
+    at = sizes.components
+    up_ref[at : at + 1, :] = visc_ref[last : last + 1, :]
+    down_ref[at : at + 1, :] = visc_ref[0:1, :]
+    spare = jnp.zeros((sizes.edge - at - 1, sizes.columns), jnp.float32)
+    up_ref[at + 1 :, :] = spare
+    down_ref[at + 1 :, :] = spare
+    for ref, (begin, end) in zip((first_ref, second_ref), sizes.chunks, strict=True):
+        ref[...] = q_ref[:, :, begin:end]
+
+
+def halo(sizes, ref, at):
+    below = sizes.edge + at
+    return ref[at : at + 1, :], ref[below : below + 1, :]
+
+
+def own_terms_of(sizes, chunk, me, q_ref, visc_ref, halo_ref):
+    center = visc_ref[...]
+    above, below = halo(sizes, halo_ref, sizes.components)
+    east = 0.5 * (center + rows_next(center, below))
+    west = 0.5 * (center + rows_before(center, above))
+    north = 0.5 * (center + lanes_next(center))
+    south = 0.5 * (center + lanes_before(center))
+    first, last = sizes.chunks[chunk]
+    results = {}
+    for harmonic in range(sizes.local):
+        number = me * sizes.local + harmonic
+        signed = jnp.where(number < sizes.total // 2, number, number - sizes.total)
+        frequency = omega_base * signed.astype(jnp.float32)
+        for part in range(2):
+
+            def beside(field):
+                value = q_ref[harmonic, part, field]
+                above, below = halo(sizes, halo_ref, sizes.at(harmonic, part, field))
+                return value, rows_next(value, below), rows_before(value, above)
+
+            def slope_x(field):
+                _, x_next, x_before = beside(field)
+                return 0.5 * (x_next - x_before)
+
+            def slope_y(field):
+                value = q_ref[harmonic, part, field]
+                return 0.5 * (lanes_next(value) - lanes_before(value))
+
+            for field in range(first, last):
+                value, x_next, x_before = beside(field)
+                damping = (
+                    east * (x_next - value)
+                    - west * (value - x_before)
+                    + north * (lanes_next(value) - value)
+                    - south * (value - lanes_before(value))
+                )
+                turned = q_ref[harmonic, 1 - part, field]
+                turn = -frequency if part == 0 else frequency
+                term = turn * turned - damping
+                if field in (0, 4):
+                    term = term + (slope_x(1) + slope_y(2))
+                elif field == 1:
+                    term = term + slope_x(4)
+                elif field == 2:
+                    term = term + slope_y(4)
+                results[harmonic, part, field] = term
+    return results
+
+
+def couple_kernel(sizes, chunk, *refs):
+    base_refs, q_refs, halo_refs, visc_ref = refs[0:4], refs[4:8], refs[8:12], refs[12]
+    out_ref, base, values, slopes_x, slopes_y, result, sem = refs[-7:]
+    me = lax.axis_index("harm")
+    total = sizes.total
+    first, last = sizes.chunks[chunk]
+    for place in range(4):
+        group = lax.bitwise_xor(me, place)
+        skipped = first if place < 2 else 0
+        for harmonic in range(sizes.local):
+            number = group * sizes.local + harmonic
+            base[number] = base_refs[place][harmonic]
+            for part in range(2):
+                for field in range(last - first):
+                    value = q_refs[place][harmonic, part, field + skipped]
+                    at = sizes.at(harmonic, part, field + first)
+                    above, below = halo(sizes, halo_refs[place], at)
+                    values[number, part, field] = value
+                    slopes_x[number, part, field] = 0.5 * (
+                        rows_next(value, below) - rows_before(value, above)
+                    )
+                    slopes_y[number, part, field] = 0.5 * (lanes_next(value) - lanes_before(value))
+    for (harmonic, part, field), term in own_terms_of(
+        sizes, chunk, me, q_refs[0], visc_ref, halo_refs[0]
+    ).items():
+        result[harmonic, part, field - first] = term
+    moved_refs = (slopes_x, slopes_y, values)
+    for field in range(last - first):
+        for start in range(0, sizes.width, 8):
+            rows = slice(start, start + 8)
+            sums = [
+                [result[harmonic, part, field, rows, :] for part in (0, 1)]
+                for harmonic in range(sizes.local)
+            ]
+            for source in range(total):
+                moved = [[ref[source, part, field, rows, :] for part in (0, 1)] for ref in moved_refs]
+                for harmonic in range(sizes.local):
+                    number = me * sizes.local + harmonic
+                    at = lax.rem(number - source + total, total)
+                    real, imag = sums[harmonic]
+                    for term, (m_real, m_imag) in enumerate(moved):
+                        c_real = base[at, 0, term, rows, :]
+                        c_imag = base[at, 1, term, rows, :]
+                        real = real + c_real * m_real - c_imag * m_imag
+                        imag = imag + c_real * m_imag + c_imag * m_real
+                    sums[harmonic] = [real, imag]
+            for harmonic in range(sizes.local):
+                for part in (0, 1):
+                    result[harmonic, part, field, rows, :] = sums[harmonic][part]
+    copy = pltpu.make_async_copy(result, out_ref.at[:, :, first:last], sem)
+    copy.start()
+    copy.wait()
+
+
+def paired_shards(perturbation, base_flow, viscosity):
+    groups, tiles = lax.axis_size("harm"), lax.axis_size("tile")
+    sizes = Sizes(perturbation, groups)
+
+    def to_chip(value):
+        return lax.ppermute(value, "harm", [(i, i ^ 2) for i in range(groups)])
+
+    def to_core(value):
+        return lax.ppermute(value, "harm", [(i, i ^ 1) for i in range(groups)])
+
+    def along_tile(value, step):
+        return lax.ppermute(value, "tile", [(i, (i + step) % tiles) for i in range(tiles)])
+
+    base_chip = to_chip(base_flow)
+    edges = jax.ShapeDtypeStruct((sizes.edge, sizes.columns), jnp.float32)
+    chunk_types = [
+        jax.ShapeDtypeStruct(sizes.chunk_shape(chunk, sizes.local), jnp.float32) for chunk in (0, 1)
+    ]
+    first, second, up, down = pl.pallas_call(
+        functools.partial(pack_kernel, sizes),
+        in_specs=[in_vmem] * 2,
+        out_shape=[*chunk_types, edges, edges],
+        out_specs=[in_vmem] * 4,
+        compiler_params=pltpu.CompilerParams(vmem_limit_bytes=scoped_bytes),
+    )(perturbation, viscosity)
+    base_core = to_core(base_flow)
+    q_core = to_core(perturbation)
+    above = along_tile(up, 1)
+    first_chip = to_chip(first)
+    below = along_tile(down, -1)
+    halo_own = jnp.concatenate([above, below], axis=0)
+    halo_chip = to_chip(halo_own)
+    second_chip = to_chip(second)
+    halo_core = to_core(halo_own)
+    base_diag = to_core(base_chip)
+    halo_diag = to_core(halo_chip)
+    first_diag = to_core(first_chip)
+    second_diag = to_core(second_chip)
+
+    def couple(chunk, chip, diag, earlier):
+        moved = pltpu.VMEM(sizes.chunk_shape(chunk, sizes.total), jnp.float32)
+        operands = [base_flow, base_core, base_chip, base_diag, perturbation, q_core, chip, diag]
+        operands += [halo_own, halo_core, halo_chip, halo_diag, viscosity, *earlier]
+        return pl.pallas_call(
+            functools.partial(couple_kernel, sizes, chunk),
+            in_specs=[in_vmem] * 13 + [anywhere] * len(earlier),
+            out_shape=jax.ShapeDtypeStruct(perturbation.shape, jnp.float32),
+            out_specs=anywhere,
+            input_output_aliases={13: 0} if earlier else {},
+            scratch_shapes=[
+                pltpu.VMEM((sizes.total, *base_flow.shape[1:]), jnp.float32),
+                moved,
+                moved,
+                moved,
+                pltpu.VMEM(sizes.chunk_shape(chunk, sizes.local), jnp.float32),
+                pltpu.SemaphoreType.DMA,
+            ],
+            compiler_params=pltpu.CompilerParams(vmem_limit_bytes=scoped_bytes),
+        )(*operands)
+
+    partial = couple(0, first_chip, first_diag, [])
+    return couple(1, second_chip, second_diag, [partial])
+
+
 def solution(mesh):
     placed = (
         P("harm", None, None, ("parts", "tile"), None),
         P("harm", None, None, ("parts", "tile"), None),
         P(("parts", "tile"), None),
     )
+
+    def chosen(perturbation, base_flow, viscosity):
+        two_chips = mesh.shape["harm"] == 2 * 2
+        whole_tiles = perturbation.shape[3] % 8 == 0 and perturbation.shape[4] % 128 == 0
+        body = paired_shards if two_chips and whole_tiles else shards
+        return body(perturbation, base_flow, viscosity)
+
     return jax.shard_map(
-        shards,
+        chosen,
         mesh=mesh,
         in_specs=placed,
         out_specs=P("harm", None, None, ("parts", "tile"), None),

time: 47.9 us -> 25.3 us (0.53)
  waiting for transfers between devices: 22.2 us -> 8.08 us
  blocking collectives: 8.62 us -> 0 us
  starting transfers between devices: 5.62 us -> 11 us
  local copies, waits for them, and re-layouts: 6.52 us -> 1.7 us
  Pallas kernels: 0 us -> 4.25 us
  other arithmetic: 4.13 us -> 0 us
    ppermute x5 -> x13, waiting for transfers between devices: 22.2 us -> 8.08 us  [the longest x4 4.31 us: to_chip(): return lax.ppermute(value, 'harm', [(i, i ^ 2) for i in range(groups)])]
    all_gather x1 -> x0, blocking collectives: 8.62 us -> none  [shards(): whole_base = lax.all_gather(base_flow, 'harm', axis=0, tiled=True)]
    ppermute x5 -> x13, starting transfers between devices: 5.62 us -> 11 us  [the longest x4 6.14 us: to_chip(): return lax.ppermute(value, 'harm', [(i, i ^ 2) for i in range(groups)])]
    pallas_call x0 -> x3, Pallas kernels: none -> 4.25 us  [the longest x2 4.21 us: couple(): pl.pallas_call(functools.partial(couple_kernel, sizes, chunk), in_specs=[...]
    gather x4 -> x0, local copies, waits for them, and re-layouts: 2.3 us -> none  [block_terms(): chosen = blocks[index_table]]
    slice x10 -> x0, local copies, waits for them, and re-layouts: 1.24 us -> none  [the longest x8 1.09 us: split_rows(): grad_y = 0.5 * (jnp.roll(middle, -1, -1) - jnp.roll(middle, 1, -1))]
    reduce_sum x4 -> x0, other arithmetic: 1.12 us -> none  [block_terms(): jnp.sum(real_part, axis=1)]
    mul x10 -> x0, other arithmetic: 1.12 us -> none  [the longest x4 0.79 us: split_rows(): grad_y = 0.5 * (jnp.roll(middle, -1, -1) - jnp.roll(middle, 1, -1))]
  transfers between devices with their start and end apart: 5 -> 13, of which waited for: 3 -> 5; matrix products, arithmetic and copies ran while one was open for 6% -> 0% of each run, Pallas kernels for 0% -> 12%
where the time goes in v2:
time: 25.3 us; the launch traced here: 25.1 us
  starting transfers between devices  11 us (43%)
  waiting for transfers between devices  8.08 us (32%)
  Pallas kernels  4.25 us (17%)
  local copies, waits for them, and re-layouts  1.7 us (7%)
    ppermute x4, starting transfers between devices, to_chip(): return lax.ppermute(value, 'harm', [(i, i ^ 2) for i in range(groups)])  6.14 us
    ppermute x4, waiting for transfers between devices, to_chip(): return lax.ppermute(value, 'harm', [(i, i ^ 2) for i in range(groups)])  4.31 us
    pallas_call x2, Pallas kernels, couple(): pl.pallas_call(functools.partial(couple_kernel, sizes, chunk), in_specs=[...  4.21 us
    ppermute x2, starting transfers between devices, along_tile(): lax.ppermute(value, 'tile', [(i, (i + step) % tiles) for i in range(tiles)])  3.82 us
    ppermute x7, waiting for transfers between devices, to_core(): return lax.ppermute(value, 'harm', [(i, i ^ 1) for i in range(groups)])  2.22 us
    unnamed x7, local copies, waits for them, and re-layouts  1.7 us
    ppermute x2, waiting for transfers between devices, along_tile(): lax.ppermute(value, 'tile', [(i, (i + step) % tiles) for i in range(tiles)])  1.55 us
    ppermute x7, starting transfers between devices, to_core(): return lax.ppermute(value, 'harm', [(i, i ^ 1) for i in range(groups)])  1.04 us
  transfers between devices with their start and end apart: 13, of which 5 were waited for; matrix products, arithmetic and copies ran while one was open for 0% of the time, Pallas kernels for 12%

profile of v2, /device:TPU:0, one launch (start us, length us, event | category | flops | bytes accessed | tf_op | source)
XLA Modules:
  0.0 25.1 jit_solution(12463104548611093271)
XLA Ops:
  0.0 1.0 %copy-done = f32[2,2,5,16,256]{4,3,2,1,0:T(8,128)S(1)} copy-done((f32[2,2,5,16,256]{4,3,2,1,0:T(8,128)S(1)}, f32[2,2,5,16,256]{4,3,2,1,0:T(8,128)}, u32[]{:S(2)}) %copy-start) | copy-done | bytes 327704
  1.0 0.7 %copy-done.2 = f32[16,256]{1,0:T(8,128)S(1)} copy-done((f32[16,256]{1,0:T(8,128)S(1)}, f32[16,256]{1,0:T(8,128)}, u32[]{:S(2)}) %copy-start.2) | copy-done | bytes 16408
  1.7 3.0 %collective-permute-start.11 = (f32[2,2,4,16,256]{4,3,2,1,0:T(8,128)S(1)}, f32[2,2,4,16,256]{4,3,2,1,0:T(8,128)S(1)}, u32[]{:S(2)}, u32[]{:S(2)}) collective-permute-start(f32[2,2,4,16,256]{4,3,2,1,0:T(8,128)S(1)} %get-tuple-element.12), channel_id=1, source_target_pairs={{0,8},{4,12},{8,0},{12,4},{1,9},{5,13},{9,1},{13,5},{2,10},{6,14},... | collective-permute-start | bytes 786440 | tf_op jit(solution)/shard_map/ppermute | solution.py:355
  4.8 1.6 %collective-permute-start.6 = (f32[24,256]{1,0:T(8,128)S(1)}, f32[24,256]{1,0:T(8,128)S(1)}, u32[]{:S(2)}, u32[]{:S(2)}) collective-permute-start(f32[24,256]{1,0:T(8,128)S(1)} %get-tuple-element.10), channel_id=1, source_target_pairs={{0,1},{1,2},{2,3},{3,0},{4,5},{5,6},{6,7},{7,4},{8,9},{9,10},{10,1... | collective-permute-start | bytes 73736 | tf_op jit(solution)/shard_map/ppermute | solution.py:361
  6.4 2.2 %collective-permute-start.7 = (f32[24,256]{1,0:T(8,128)S(1)}, f32[24,256]{1,0:T(8,128)S(1)}, u32[]{:S(2)}, u32[]{:S(2)}) collective-permute-start(f32[24,256]{1,0:T(8,128)S(1)} %get-tuple-element.11), channel_id=1, source_target_pairs={{0,3},{1,0},{2,1},{3,2},{4,7},{5,4},{6,5},{7,6},{8,11},{9,8},{10,9... | collective-permute-start | bytes 73736 | tf_op jit(solution)/shard_map/ppermute | solution.py:361
  8.6 0.3 %collective-permute-start.1 = (f32[2,2,3,16,256]{4,3,2,1,0:T(8,128)S(1)}, f32[2,2,3,16,256]{4,3,2,1,0:T(8,128)S(1)}, u32[]{:S(2)}, u32[]{:S(2)}) collective-permute-start(f32[2,2,3,16,256]{4,3,2,1,0:T(8,128)S(1)} %copy-done.1), channel_id=1, source_target_pairs={{0,8},{4,12},{8,0},{12,4},{1,9},{5,13},{9,1},{13,5},{2,10},{6,14},... | collective-permute-start | bytes 589832 | tf_op jit(solution)/shard_map/ppermute | solution.py:355
  8.9 1.6 %collective-permute-done.6 = f32[24,256]{1,0:T(8,128)S(1)} collective-permute-done((f32[24,256]{1,0:T(8,128)S(1)}, f32[24,256]{1,0:T(8,128)S(1)}, u32[]{:S(2)}, u32[]{:S(2)}) %collective-permute-start.6) | collective-permute-done | bytes 24608 | tf_op jit(solution)/shard_map/ppermute | solution.py:361
  10.4 0.3 %collective-permute-start.4 = (f32[2,2,1,16,256]{4,3,2,1,0:T(8,128)S(1)}, f32[2,2,1,16,256]{4,3,2,1,0:T(8,128)S(1)}, u32[]{:S(2)}, u32[]{:S(2)}) collective-permute-start(f32[2,2,1,16,256]{4,3,2,1,0:T(8,128)S(1)} %get-tuple-element.9), channel_id=1, source_target_pairs={{0,8},{4,12},{8,0},{12,4},{1,9},{5,13},{9,1},{13,5},{2,10},{6,14},... | collective-permute-start | bytes 196616 | tf_op jit(solution)/shard_map/ppermute | solution.py:355
  10.7 0.7 %collective-permute-done.11.refs_6_ = f32[2,2,4,16,256]{4,3,2,1,0:T(8,128)S(1)} collective-permute-done((f32[2,2,4,16,256]{4,3,2,1,0:T(8,128)S(1)}, f32[2,2,4,16,256]{4,3,2,1,0:T(8,128)S(1)}, u32[]{:S(2)}, u32[]{:S(2)}) %collective-permute-start.11) | collective-permute-done | bytes 262176 | tf_op jit(solution)/shard_map/ppermute | solution.py:355
  11.4 2.5 %collective-permute-start.9 = (f32[48,256]{1,0:T(8,128)S(1)}, f32[48,256]{1,0:T(8,128)S(1)}, u32[]{:S(2)}, u32[]{:S(2)}) collective-permute-start(f32[48,256]{1,0:T(8,128)S(1)} %constant_dynamic-update-slice_fusion.refs_8_), channel_id=1, source_target_pairs={{0,8},{4,12},{8,0},{12,4},{1,9},{5,13},{9,1},{13,5},{2,10},{6,14},... | collective-permute-start | bytes 147464 | tf_op jit(solution)/shard_map/ppermute | solution.py:355
  13.9 3.6 %collective-permute-done.4.refs_6_ = f32[2,2,1,16,256]{4,3,2,1,0:T(8,128)S(1)} collective-permute-done((f32[2,2,1,16,256]{4,3,2,1,0:T(8,128)S(1)}, f32[2,2,1,16,256]{4,3,2,1,0:T(8,128)S(1)}, u32[]{:S(2)}, u32[]{:S(2)}) %collective-permute-start.4) | collective-permute-done | bytes 65568 | tf_op jit(solution)/shard_map/ppermute | solution.py:355
  17.6 0.0 collective-permute-start
  17.6 0.0 collective-permute-done.1.refs_2_
  17.6 0.5 %collective-permute-start.2 = (f32[2,2,3,16,256]{4,3,2,1,0:T(8,128)S(1)}, f32[2,2,3,16,256]{4,3,2,1,0:T(8,128)S(1)}, u32[]{:S(2)}, u32[]{:S(2)}) collective-permute-start(f32[2,2,3,16,256]{4,3,2,1,0:T(8,128)S(1)} %collective-permute-done.1.refs_2_), channel_id=1, source_target_pairs={{0,4},{4,0},{8,12},{12,8},{1,5},{5,1},{9,13},{13,9},{2,6},{6,2},{1... | collective-permute-start | bytes 589832 | tf_op jit(solution)/shard_map/ppermute | solution.py:358
  18.1 0.0 collective-permute-done.9.refs_10_
  18.1 0.1 collective-permute-start.8
  18.2 1.2 %collective-permute-done.8.refs_9_ = f32[48,256]{1,0:T(8,128)S(1)} collective-permute-done((f32[48,256]{1,0:T(8,128)S(1)}, f32[48,256]{1,0:T(8,128)S(1)}, u32[]{:S(2)}, u32[]{:S(2)}) %collective-permute-start.8) | collective-permute-done | bytes 49184 | tf_op jit(solution)/shard_map/ppermute | solution.py:358
  19.4 0.2 collective-permute-start.10
  19.6 1.0 %collective-permute-done.10.refs_11_ = f32[48,256]{1,0:T(8,128)S(1)} collective-permute-done((f32[48,256]{1,0:T(8,128)S(1)}, f32[48,256]{1,0:T(8,128)S(1)}, u32[]{:S(2)}, u32[]{:S(2)}) %collective-permute-start.10) | collective-permute-done | bytes 49184 | tf_op jit(solution)/shard_map/ppermute | solution.py:358
  20.6 0.2 collective-permute-start.5
  20.8 0.0 collective-permute-done.12.refs_7_
  20.9 2.9 %shard_map.38.refs_13_ = f32[2,2,5,16,256]{4,3,2,1,0:T(8,128)} custom-call(f32[2,2,3,16,256]{4,3,2,1,0:T(8,128)S(1)} %copy-done.1, f32[2,2,3,16,256]{4,3,2,1,0:T(8,128)S(1)} %collective-permute-done.refs_1_, f32[2,2,3,16,256]{4,3,2,1,0:T(8,128)S(1)} %collective-permute-done.1.refs_2_, f32[2,2,3,16,256]{4,3,2,1,0:T(8,128)S(1)} %collective-permute-done.2.refs_3_, ...), custom_call_target="tpu_custom_call" | custom-call | tf_op jit(solution)/shard_map/pallas_call | solution.py:393
  23.8 0.0 collective-permute-done.5.refs_7_
  23.8 1.3 %shard_map.39 = f32[2,2,5,16,256]{4,3,2,1,0:T(8,128)} custom-call(f32[2,2,3,16,256]{4,3,2,1,0:T(8,128)S(1)} %copy-done.1, f32[2,2,3,16,256]{4,3,2,1,0:T(8,128)S(1)} %collective-permute-done.refs_1_, f32[2,2,3,16,256]{4,3,2,1,0:T(8,128)S(1)} %collective-permute-done.1.refs_2_, ...), custom_call_target="tpu_custom_call", output_to_operand_aliasing={{}: (13, {})} | custom-call | tf_op jit(solution)/shard_map/pallas_call | solution.py:393
  (13 shorter events, 0.1 us)
Async XLA Ops:
  0.0 1.0 %copy-start = (f32[2,2,5,16,256]{4,3,2,1,0:T(8,128)S(1)}, f32[2,2,5,16,256]{4,3,2,1,0:T(8,128)}, u32[]{:S(2)}) copy-start(f32[2,2,5,16,256]{4,3,2,1,0:T(8,128)} %refs_4_.3) | copy-start | bytes 983044
  1.0 0.7 %copy-start.2 = (f32[16,256]{1,0:T(8,128)S(1)}, f32[16,256]{1,0:T(8,128)}, u32[]{:S(2)}) copy-start(f32[16,256]{1,0:T(8,128)} %refs_12_.3) | copy-start | bytes 49156
  1.7 6.9 %copy-start.1 = (f32[2,2,3,16,256]{4,3,2,1,0:T(8,128)S(1)}, f32[2,2,3,16,256]{4,3,2,1,0:T(8,128)}, u32[]{:S(2)}) copy-start(f32[2,2,3,16,256]{4,3,2,1,0:T(8,128)} %refs_0_.3) | copy-start | bytes 589828
  1.7 9.6 %collective-permute-start.11 = (f32[2,2,4,16,256]{4,3,2,1,0:T(8,128)S(1)}, f32[2,2,4,16,256]{4,3,2,1,0:T(8,128)S(1)}, u32[]{:S(2)}, u32[]{:S(2)}) collective-permute-start(f32[2,2,4,16,256]{4,3,2,1,0:T(8,128)S(1)} %get-tuple-element.12), channel_id=1, source_target_pairs={{0,8},{4,12},{8,0},{12,4},{1,9},{5,13},{9,1},{13,5},{2,10},{6,14},... | collective-permute-start | bytes 786440 | tf_op jit(solution)/shard_map/ppermute | solution.py:355
  4.8 5.7 %collective-permute-start.6 = (f32[24,256]{1,0:T(8,128)S(1)}, f32[24,256]{1,0:T(8,128)S(1)}, u32[]{:S(2)}, u32[]{:S(2)}) collective-permute-start(f32[24,256]{1,0:T(8,128)S(1)} %get-tuple-element.10), channel_id=1, source_target_pairs={{0,1},{1,2},{2,3},{3,0},{4,5},{5,6},{6,7},{7,4},{8,9},{9,10},{10,1... | collective-permute-start | bytes 73736 | tf_op jit(solution)/shard_map/ppermute | solution.py:361
  6.4 14.5 %collective-permute-start.3 = (f32[2,2,5,16,256]{4,3,2,1,0:T(8,128)S(1)}, f32[2,2,5,16,256]{4,3,2,1,0:T(8,128)S(1)}, u32[]{:S(2)}, u32[]{:S(2)}) collective-permute-start(f32[2,2,5,16,256]{4,3,2,1,0:T(8,128)S(1)} %copy-done), channel_id=1, source_target_pairs={{0,4},{4,0},{8,12},{12,8},{1,5},{5,1},{9,13},{13,9},{2,6},{6,2},{1... | collective-permute-start | bytes 983048 | tf_op jit(solution)/shard_map/ppermute | solution.py:358
  6.4 5.0 %collective-permute-start.7 = (f32[24,256]{1,0:T(8,128)S(1)}, f32[24,256]{1,0:T(8,128)S(1)}, u32[]{:S(2)}, u32[]{:S(2)}) collective-permute-start(f32[24,256]{1,0:T(8,128)S(1)} %get-tuple-element.11), channel_id=1, source_target_pairs={{0,3},{1,0},{2,1},{3,2},{4,7},{5,4},{6,5},{7,6},{8,11},{9,8},{10,9... | collective-permute-start | bytes 73736 | tf_op jit(solution)/shard_map/ppermute | solution.py:361
  8.6 9.0 %collective-permute-start.1 = (f32[2,2,3,16,256]{4,3,2,1,0:T(8,128)S(1)}, f32[2,2,3,16,256]{4,3,2,1,0:T(8,128)S(1)}, u32[]{:S(2)}, u32[]{:S(2)}) collective-permute-start(f32[2,2,3,16,256]{4,3,2,1,0:T(8,128)S(1)} %copy-done.1), channel_id=1, source_target_pairs={{0,8},{4,12},{8,0},{12,4},{1,9},{5,13},{9,1},{13,5},{2,10},{6,14},... | collective-permute-start | bytes 589832 | tf_op jit(solution)/shard_map/ppermute | solution.py:355
  10.4 7.1 %collective-permute-start.4 = (f32[2,2,1,16,256]{4,3,2,1,0:T(8,128)S(1)}, f32[2,2,1,16,256]{4,3,2,1,0:T(8,128)S(1)}, u32[]{:S(2)}, u32[]{:S(2)}) collective-permute-start(f32[2,2,1,16,256]{4,3,2,1,0:T(8,128)S(1)} %get-tuple-element.9), channel_id=1, source_target_pairs={{0,8},{4,12},{8,0},{12,4},{1,9},{5,13},{9,1},{13,5},{2,10},{6,14},... | collective-permute-start | bytes 196616 | tf_op jit(solution)/shard_map/ppermute | solution.py:355
  11.4 9.5 %collective-permute-start.12 = (f32[2,2,4,16,256]{4,3,2,1,0:T(8,128)S(1)}, f32[2,2,4,16,256]{4,3,2,1,0:T(8,128)S(1)}, u32[]{:S(2)}, u32[]{:S(2)}) collective-permute-start(f32[2,2,4,16,256]{4,3,2,1,0:T(8,128)S(1)} %collective-permute-done.11.refs_6_), channel_id=1, source_target_pairs={{0,4},{4,0},{8,12},{12,8},{1,5},{5,1},{9,13},{13,9},{2,6},{6,2},{1... | collective-permute-start | bytes 786440 | tf_op jit(solution)/shard_map/ppermute | solution.py:358
  11.4 6.7 %collective-permute-start.9 = (f32[48,256]{1,0:T(8,128)S(1)}, f32[48,256]{1,0:T(8,128)S(1)}, u32[]{:S(2)}, u32[]{:S(2)}) collective-permute-start(f32[48,256]{1,0:T(8,128)S(1)} %constant_dynamic-update-slice_fusion.refs_8_), channel_id=1, source_target_pairs={{0,8},{4,12},{8,0},{12,4},{1,9},{5,13},{9,1},{13,5},{2,10},{6,14},... | collective-permute-start | bytes 147464 | tf_op jit(solution)/shard_map/ppermute | solution.py:355
  17.6 3.3 %collective-permute-start = (f32[2,2,3,16,256]{4,3,2,1,0:T(8,128)S(1)}, f32[2,2,3,16,256]{4,3,2,1,0:T(8,128)S(1)}, u32[]{:S(2)}, u32[]{:S(2)}) collective-permute-start(f32[2,2,3,16,256]{4,3,2,1,0:T(8,128)S(1)} %copy-done.1), channel_id=1, source_target_pairs={{0,4},{4,0},{8,12},{12,8},{1,5},{5,1},{9,13},{13,9},{2,6},{6,2},{1... | collective-permute-start | bytes 589832 | tf_op jit(solution)/shard_map/ppermute | solution.py:358
  17.6 3.3 %collective-permute-start.2 = (f32[2,2,3,16,256]{4,3,2,1,0:T(8,128)S(1)}, f32[2,2,3,16,256]{4,3,2,1,0:T(8,128)S(1)}, u32[]{:S(2)}, u32[]{:S(2)}) collective-permute-start(f32[2,2,3,16,256]{4,3,2,1,0:T(8,128)S(1)} %collective-permute-done.1.refs_2_), channel_id=1, source_target_pairs={{0,4},{4,0},{8,12},{12,8},{1,5},{5,1},{9,13},{13,9},{2,6},{6,2},{1... | collective-permute-start | bytes 589832 | tf_op jit(solution)/shard_map/ppermute | solution.py:358
  18.1 1.3 %collective-permute-start.8 = (f32[48,256]{1,0:T(8,128)S(1)}, f32[48,256]{1,0:T(8,128)S(1)}, u32[]{:S(2)}, u32[]{:S(2)}) collective-permute-start(f32[48,256]{1,0:T(8,128)S(1)} %constant_dynamic-update-slice_fusion.refs_8_), channel_id=1, source_target_pairs={{0,4},{4,0},{8,12},{12,8},{1,5},{5,1},{9,13},{13,9},{2,6},{6,2},{1... | collective-permute-start | bytes 147464 | tf_op jit(solution)/shard_map/ppermute | solution.py:358
  19.4 1.2 %collective-permute-start.10 = (f32[48,256]{1,0:T(8,128)S(1)}, f32[48,256]{1,0:T(8,128)S(1)}, u32[]{:S(2)}, u32[]{:S(2)}) collective-permute-start(f32[48,256]{1,0:T(8,128)S(1)} %collective-permute-done.9.refs_10_), channel_id=1, source_target_pairs={{0,4},{4,0},{8,12},{12,8},{1,5},{5,1},{9,13},{13,9},{2,6},{6,2},{1... | collective-permute-start | bytes 147464 | tf_op jit(solution)/shard_map/ppermute | solution.py:358
  20.6 3.2 %collective-permute-start.5 = (f32[2,2,1,16,256]{4,3,2,1,0:T(8,128)S(1)}, f32[2,2,1,16,256]{4,3,2,1,0:T(8,128)S(1)}, u32[]{:S(2)}, u32[]{:S(2)}) collective-permute-start(f32[2,2,1,16,256]{4,3,2,1,0:T(8,128)S(1)} %collective-permute-done.4.refs_6_), channel_id=1, source_target_pairs={{0,4},{4,0},{8,12},{12,8},{1,5},{5,1},{9,13},{13,9},{2,6},{6,2},{1... | collective-permute-start | bytes 196616 | tf_op jit(solution)/shard_map/ppermute | solution.py:358

commit v3 on v0

--- a/solution.py
+++ b/solution.py
@@ -1,7 +1,11 @@
+import functools
+
 import jax
 import jax.numpy as jnp
 import numpy as np
 from jax import lax
+from jax.experimental import pallas as pl
+from jax.experimental.pallas import tpu as pltpu
 from jax.sharding import PartitionSpec as P
 
 omega_base = 0.25
@@ -167,14 +171,472 @@
     return summed
 
 
+def ceil_to(count, unit):
+    return -(-count // unit) * unit
+
+
+scoped_bytes = 12 * 1024 * 1024
+in_vmem = pl.BlockSpec(memory_space=pltpu.VMEM)
+anywhere = pl.BlockSpec(memory_space=pl.ANY)
+
+
+def lanes_next(value):
+    return pltpu.roll(value, value.shape[1] - 1, 1)
+
+
+def lanes_before(value):
+    return pltpu.roll(value, 1, 1)
+
+
+def rows_next(value, below):
+    count = value.shape[0]
+    row = lax.broadcasted_iota(jnp.int32, value.shape, 0)
+    return jnp.where(row == count - 1, below, pltpu.roll(value, count - 1, 0))
+
+
+def rows_before(value, above):
+    row = lax.broadcasted_iota(jnp.int32, value.shape, 0)
+    return jnp.where(row == 0, above, pltpu.roll(value, 1, 0))
+
+
+class Sizes:
+    def __init__(self, perturbation, groups):
+        self.local, _, self.fields, self.width, self.columns = perturbation.shape
+        self.groups = groups
+        self.total = self.local * groups
+        self.components = self.local * 2 * self.fields
+        self.edge = ceil_to(self.components + 1, 8)
+        cut = self.fields - 1
+        self.moved, self.sent = (0, cut), (cut, self.fields)
+        self.block_rows = self.local * 2 * (self.fields - cut) * self.width
+        self.message_rows = ceil_to(self.block_rows + self.local * 2 * cut * 2, 8)
+
+    def at(self, harmonic, part, field):
+        return (harmonic * 2 + part) * self.fields + field
+
+    def block(self, harmonic, part, field):
+        first, last = self.sent
+        start = ((harmonic * 2 + part) * (last - first) + field - first) * self.width
+        return slice(start, start + self.width)
+
+    def rim(self, harmonic, part, field, side):
+        first, last = self.moved
+        at = ((harmonic * 2 + part) * (last - first) + field - first) * 2 + side
+        return slice(self.block_rows + at, self.block_rows + at + 1)
+
+    def shape(self, harmonics, fields):
+        return (harmonics, 2, fields[1] - fields[0], self.width, self.columns)
+
+    def each(self):
+        for harmonic in range(self.local):
+            for part in range(2):
+                for field in range(self.fields):
+                    yield harmonic, part, field
+
+
+def fetch_kernel(sizes, q_from, visc_from, q_ref, visc_ref, moved_ref, q_sem, visc_sem):
+    copies = (
+        pltpu.make_async_copy(q_from, q_ref, q_sem),
+        pltpu.make_async_copy(visc_from, visc_ref, visc_sem),
+    )
+    for copy in copies:
+        copy.start()
+    for copy in copies:
+        copy.wait()
+    moved_ref[...] = q_ref[:, :, sizes.moved[0] : sizes.moved[1]]
+
+
+def edge_kernel(row):
+    def kernel(sizes, q_ref, visc_ref, *refs):
+        edge_ref = refs[-1]
+        rows = slice(row, row + 1) if row >= 0 else slice(sizes.width - 1, sizes.width)
+        for harmonic, part, field in sizes.each():
+            at = sizes.at(harmonic, part, field)
+            edge_ref[at : at + 1, :] = q_ref[harmonic, part, field, rows, :]
+        at = sizes.components
+        edge_ref[at : at + 1, :] = visc_ref[rows, :]
+        edge_ref[at + 1 :, :] = jnp.zeros((sizes.edge - at - 1, sizes.columns), jnp.float32)
+
+    return kernel
+
+
+def halo(sizes, ref, at):
+    below = sizes.edge + at
+    return ref[at : at + 1, :], ref[below : below + 1, :]
+
+
+def slope_y(value):
+    return 0.5 * (lanes_next(value) - lanes_before(value))
+
+
+def slope_x(value, above, below):
+    return 0.5 * (rows_next(value, below) - rows_before(value, above))
+
+
+def add_products(sums, chosen, moved):
+    real, imag = sums
+    for (c_real, c_imag), (m_real, m_imag) in zip(chosen, moved, strict=True):
+        more_real = c_real * m_real - c_imag * m_imag
+        more_imag = c_real * m_imag + c_imag * m_real
+        real = more_real if real is None else real + more_real
+        imag = more_imag if imag is None else imag + more_imag
+    return real, imag
+
+
+def chosen_rows(sizes, base, target, source, rows):
+    at = lax.rem(target - source + sizes.total, sizes.total)
+    return [[base[at, part, term, rows, :] for part in (0, 1)] for term in range(3)]
+
+
+def result_kernel(
+    sizes, base_a, base_b, base_c, base_d, q_ref, halo_ref, near_ref, far_ref, base
+):
+    me = lax.axis_index("harm")
+    for place, ref in enumerate((base_a, base_b, base_c, base_d)):
+        for harmonic in range(sizes.local):
+            base[lax.bitwise_xor(me, place) * sizes.local + harmonic] = ref[harmonic]
+    targets = [
+        (lax.bitwise_xor(me, place) * sizes.local + harmonic, ref, harmonic)
+        for place, ref in ((2, near_ref), (3, far_ref))
+        for harmonic in range(sizes.local)
+    ]
+    first, last = sizes.sent
+    parts = (0, 1)
+    for field in range(first, last):
+        moved = []
+        for harmonic in range(sizes.local):
+            terms = [[], [], []]
+            for part in parts:
+                value = q_ref[harmonic, part, field]
+                above, below = halo(sizes, halo_ref, sizes.at(harmonic, part, field))
+                for term, what in zip(
+                    terms, (slope_x(value, above, below), slope_y(value), value), strict=True
+                ):
+                    term.append(what)
+            moved.append(terms)
+        for start in range(0, sizes.width, 8):
+            rows = slice(start, start + 8)
+            for target, ref, harmonic in targets:
+                sums = (None, None)
+                for source in range(sizes.local):
+                    chosen = chosen_rows(sizes, base, target, me * sizes.local + source, rows)
+                    cut = [[value[rows] for value in term] for term in moved[source]]
+                    sums = add_products(sums, chosen, cut)
+                for part in parts:
+                    at = sizes.block(harmonic, part, field).start + start
+                    ref[at : at + 8, :] = sums[part]
+    first, last = sizes.moved
+    for side, row, sign in ((0, 0, -0.5), (1, sizes.width - 1, 0.5)):
+        outside = [
+            [
+                jnp.concatenate(
+                    [
+                        halo(sizes, halo_ref, sizes.at(harmonic, part, field))[side]
+                        for field in range(first, last)
+                    ],
+                    axis=0,
+                )
+                for part in parts
+            ]
+            for harmonic in range(sizes.local)
+        ]
+        for target, ref, harmonic in targets:
+            real = imag = 0.0
+            for source in range(sizes.local):
+                at = lax.rem(target - (me * sizes.local + source) + sizes.total, sizes.total)
+                u_real = sign * base[at, 0, 0, row : row + 1, :]
+                u_imag = sign * base[at, 1, 0, row : row + 1, :]
+                q_real, q_imag = outside[source]
+                real = real + u_real * q_real - u_imag * q_imag
+                imag = imag + u_real * q_imag + u_imag * q_real
+            for part, value in zip(parts, (real, imag), strict=True):
+                for field in range(first, last):
+                    at = field - first
+                    ref[sizes.rim(harmonic, part, field, side), :] = value[at : at + 1, :]
+    tail = sizes.block_rows + sizes.local * 2 * (last - first) * 2
+    if tail < sizes.message_rows:
+        for ref in (near_ref, far_ref):
+            ref[tail:, :] = jnp.zeros((sizes.message_rows - tail, sizes.columns), jnp.float32)
+
+
+def own_terms_into(sizes, q_ref, visc_ref, halo_ref, sum_ref):
+    me = lax.axis_index("harm")
+    center = visc_ref[...]
+    above, below = halo(sizes, halo_ref, sizes.components)
+    east = 0.5 * (center + rows_next(center, below))
+    west = 0.5 * (center + rows_before(center, above))
+    north = 0.5 * (center + lanes_next(center))
+    south = 0.5 * (center + lanes_before(center))
+    for harmonic in range(sizes.local):
+        number = me * sizes.local + harmonic
+        signed = jnp.where(number < sizes.total // 2, number, number - sizes.total)
+        frequency = omega_base * signed.astype(jnp.float32)
+        for part in range(2):
+            turn = -frequency if part == 0 else frequency
+            terms = {}
+            for field in range(sizes.fields):
+                value = q_ref[harmonic, part, field]
+                above, below = halo(sizes, halo_ref, sizes.at(harmonic, part, field))
+                x_next, x_before = rows_next(value, below), rows_before(value, above)
+                y_next, y_before = lanes_next(value), lanes_before(value)
+                damping = (
+                    east * (x_next - value)
+                    - west * (value - x_before)
+                    + north * (y_next - value)
+                    - south * (value - y_before)
+                )
+                terms[field] = turn * q_ref[harmonic, 1 - part, field] - damping
+                if field == 1:
+                    dilation = 0.5 * (x_next - x_before)
+                elif field == 2:
+                    dilation = dilation + 0.5 * (y_next - y_before)
+                elif field == 4:
+                    terms[1] = terms[1] + 0.5 * (x_next - x_before)
+                    terms[2] = terms[2] + 0.5 * (y_next - y_before)
+            terms[0] = terms[0] + dilation
+            terms[4] = terms[4] + dilation
+            for field in range(sizes.fields):
+                sum_ref[harmonic, part, field] = terms[field]
+
+
+def couple(sizes, base, place, fields, start_from, q_ref, halo_ref, slopes, store):
+    me = lax.axis_index("harm")
+    slopes_x, slopes_y = slopes
+    group = lax.bitwise_xor(me, place)
+    for field in range(*fields):
+        for harmonic in range(sizes.local):
+            for part in (0, 1):
+                value = q_ref[harmonic, part, field]
+                above = below = 0.0
+                if halo_ref is not None:
+                    above, below = halo(sizes, halo_ref, sizes.at(harmonic, part, field))
+                slopes_x[harmonic, part] = slope_x(value, above, below)
+                slopes_y[harmonic, part] = slope_y(value)
+        for start in range(0, sizes.width, 8):
+            rows = slice(start, start + 8)
+            sums = [
+                [start_from(harmonic, part, field, rows) for part in (0, 1)]
+                for harmonic in range(sizes.local)
+            ]
+            for source in range(sizes.local):
+                moved = [
+                    [slopes_x[source, part, rows, :] for part in (0, 1)],
+                    [slopes_y[source, part, rows, :] for part in (0, 1)],
+                    [q_ref[source, part, field, rows, :] for part in (0, 1)],
+                ]
+                for harmonic in range(sizes.local):
+                    target = me * sizes.local + harmonic
+                    number = group * sizes.local + source
+                    chosen = chosen_rows(sizes, base, target, number, rows)
+                    sums[harmonic] = add_products(sums[harmonic], chosen, moved)
+            for harmonic in range(sizes.local):
+                for part in (0, 1):
+                    store(harmonic, part, field, rows, sums[harmonic][part])
+
+
+def reader(ref):
+    return lambda harmonic, part, field, rows: ref[harmonic, part, field, rows, :]
+
+
+def writer(ref):
+    def store(harmonic, part, field, rows, value):
+        ref[harmonic, part, field, rows, :] = value
+
+    return store
+
+
+def own_kernel(sizes, base, q_ref, halo_ref, visc_ref, _, sum_ref, *slopes):
+    own_terms_into(sizes, q_ref, visc_ref, halo_ref, sum_ref)
+    everything = (0, sizes.fields)
+    couple(
+        sizes, base, 0, everything, reader(sum_ref), q_ref, halo_ref, slopes, writer(sum_ref)
+    )
+
+
+def core_kernel(sizes, base, q_ref, halo_ref, before_ref, sum_ref, *slopes):
+    everything = (0, sizes.fields)
+    couple(
+        sizes, base, 1, everything, reader(before_ref), q_ref, halo_ref, slopes, writer(sum_ref)
+    )
+
+
+def far_kernel(place):
+    def kernel(sizes, base, q_ref, before_ref, sum_ref, *slopes):
+        couple(
+            sizes, base, place, sizes.moved, reader(before_ref), q_ref, None, slopes,
+            writer(sum_ref),
+        )
+
+    return kernel
+
+
+def pass_kernel(sizes, values, after, same):
+    pass
+
+
+def sent_kernel(sizes, near_ref, message, _, sum_ref):
+    first = sizes.sent[0]
+    for field in range(*sizes.sent):
+        for harmonic in range(sizes.local):
+            for part in (0, 1):
+                more = message[sizes.block(harmonic, part, field), :]
+                sum_ref[harmonic, part, field - first] = near_ref[harmonic, part, field] + more
+
+
+def last_kernel(
+    sizes, base, q_diag, sent_ref, far_ref, message, out_ref, slopes_x, slopes_y, result, sems
+):
+    copies = []
+
+    def send(source, field):
+        copies.append(
+            pltpu.make_async_copy(source, out_ref.at[:, :, field], sems.at[field])
+        )
+        copies[-1].start()
+
+    for field in range(*sizes.sent):
+        send(sent_ref.at[:, :, field - sizes.sent[0]], field)
+    for field in range(*sizes.moved):
+        couple(
+            sizes, base, 3, (field, field + 1), reader(far_ref), q_diag, None, (slopes_x, slopes_y),
+            writer(result),
+        )
+        for harmonic in range(sizes.local):
+            for part in (0, 1):
+                for side, row in ((0, 0), (1, sizes.width - 1)):
+                    more = message[sizes.rim(harmonic, part, field, side), :]
+                    result[harmonic, part, field, row : row + 1, :] += more
+        send(result.at[:, :, field], field)
+    for copy in copies:
+        copy.wait()
+
+
+def paired_shards(perturbation, base_flow, viscosity):
+    groups, tiles = lax.axis_size("harm"), lax.axis_size("tile")
+    sizes = Sizes(perturbation, groups)
+
+    def to_chip(value):
+        return lax.ppermute(value, "harm", [(i, i ^ 2) for i in range(groups)])
+
+    def to_core(value):
+        return lax.ppermute(value, "harm", [(i, i ^ 1) for i in range(groups)])
+
+    def along_tile(value, step):
+        return lax.ppermute(value, "tile", [(i, (i + step) % tiles) for i in range(tiles)])
+
+    def array(*shape):
+        return jax.ShapeDtypeStruct(shape, jnp.float32)
+
+    def call(
+        kernel, operands, outs, scratch=(), in_specs=None, out_specs=None, flops=1, aliases=None
+    ):
+        return pl.pallas_call(
+            functools.partial(kernel, sizes),
+            in_specs=in_specs or [in_vmem] * len(operands),
+            out_shape=outs,
+            out_specs=out_specs or [in_vmem] * len(outs),
+            scratch_shapes=scratch,
+            input_output_aliases=aliases or {},
+            cost_estimate=pl.CostEstimate(flops=flops, bytes_accessed=1, transcendentals=0),
+            compiler_params=pltpu.CompilerParams(vmem_limit_bytes=scoped_bytes),
+        )(*operands)
+
+    slopes = [pltpu.VMEM((sizes.local, 2, sizes.width, sizes.columns), jnp.float32)] * 2
+    edges = array(sizes.edge, sizes.columns)
+    message = array(sizes.message_rows, sizes.columns)
+
+    base_chip = to_chip(base_flow)
+    held, visc, moved = call(
+        fetch_kernel,
+        [pltpu.with_memory_space_constraint(x, pltpu.HBM) for x in (perturbation, viscosity)],
+        [
+            array(*perturbation.shape),
+            array(*viscosity.shape),
+            array(*sizes.shape(sizes.local, sizes.moved)),
+        ],
+        [pltpu.SemaphoreType.DMA] * 2,
+        [anywhere] * 2,
+    )
+    up = call(edge_kernel(-1), (held, visc), [edges])[0]
+    base_core = to_core(base_flow)
+    above = along_tile(up, 1)
+    moved_chip = to_chip(moved)
+    down = call(
+        edge_kernel(0), (held, visc, base_core), [edges], in_specs=[in_vmem] * 2 + [anywhere]
+    )[0]
+    below = along_tile(down, -1)
+    halo_own = jnp.concatenate([above, below], axis=0)
+    halo_core = to_core(halo_own)
+    base_diag = to_core(base_chip)
+    near, far, base = call(
+        result_kernel,
+        (base_flow, base_core, base_chip, base_diag, held, halo_own),
+        [message, message, array(sizes.total, *base_flow.shape[1:])],
+    )
+    message_out = near + to_core(far)
+    results = to_chip(message_out)
+    held_core = to_core(lax.optimization_barrier((held, near))[0])
+    own_sum = call(
+        own_kernel,
+        (base, held, halo_own, visc, message_out),
+        [array(*perturbation.shape)],
+        slopes,
+        [in_vmem] * 4 + [anywhere],
+    )[0]
+    near_sum = call(
+        core_kernel, (base, held_core, halo_core, own_sum), [array(*perturbation.shape)], slopes
+    )[0]
+    moved_here = call(
+        pass_kernel,
+        (moved_chip, own_sum),
+        array(*moved_chip.shape),
+        in_specs=[anywhere] * 2,
+        out_specs=anywhere,
+        flops=10**9,
+        aliases={0: 0},
+    )
+    moved_diag = to_core(moved_here)
+    far_sum = call(
+        far_kernel(2),
+        (base, moved_here, near_sum),
+        [array(*sizes.shape(sizes.local, sizes.moved))],
+        slopes,
+    )[0]
+    sent_sum = call(
+        sent_kernel,
+        (near_sum, results, far_sum),
+        [array(*sizes.shape(sizes.local, sizes.sent))],
+        flops=2*10**9,
+        in_specs=[in_vmem, in_vmem, anywhere],
+    )[0]
+    return call(
+        last_kernel,
+        (base, moved_diag, sent_sum, far_sum, results),
+        array(*perturbation.shape),
+        [
+            *slopes,
+            pltpu.VMEM(sizes.shape(sizes.local, sizes.moved), jnp.float32),
+            pltpu.SemaphoreType.DMA((sizes.fields,)),
+        ],
+        out_specs=anywhere,
+    )
+
+
 def solution(mesh):
     placed = (
         P("harm", None, None, ("parts", "tile"), None),
         P("harm", None, None, ("parts", "tile"), None),
         P(("parts", "tile"), None),
     )
+
+    def chosen(perturbation, base_flow, viscosity):
+        two_chips = mesh.shape["harm"] == 2 * 2
+        whole_tiles = perturbation.shape[3] % 8 == 0 and perturbation.shape[4] % 128 == 0
+        body = paired_shards if two_chips and whole_tiles else shards
+        return body(perturbation, base_flow, viscosity)
+
     return jax.shard_map(
-        shards,
+        chosen,
         mesh=mesh,
         in_specs=placed,
         out_specs=P("harm", None, None, ("parts", "tile"), None),

time: 47.9 us -> 18.9 us (0.39)
  waiting for transfers between devices: 22.2 us -> 4.4 us
  blocking collectives: 8.62 us -> 0 us
  local copies, waits for them, and re-layouts: 6.52 us -> 0.01 us
  starting transfers between devices: 5.62 us -> 10.4 us
  other arithmetic: 4.13 us -> 0.01 us
  Pallas kernels: 0 us -> 3.78 us
    ppermute x5 -> x11, waiting for transfers between devices: 22.2 us -> 4.4 us  [the longest x6 2.69 us: to_core(): return lax.ppermute(value, 'harm', [(i, i ^ 1) for i in range(groups)])]
    all_gather x1 -> x0, blocking collectives: 8.62 us -> none  [shards(): whole_base = lax.all_gather(base_flow, 'harm', axis=0, tiled=True)]
    ppermute x5 -> x11, starting transfers between devices: 5.62 us -> 10.4 us  [the longest x3 5.03 us: to_chip(): return lax.ppermute(value, 'harm', [(i, i ^ 2) for i in range(groups)])]
    pallas_call x0 -> x10, Pallas kernels: none -> 3.78 us  [call(): pl.pallas_call(functools.partial(kernel, sizes), in_specs=in_specs or [in...]
    gather x4 -> x0, local copies, waits for them, and re-layouts: 2.3 us -> none  [block_terms(): chosen = blocks[index_table]]
    unnamed x11 -> x3, local copies, waits for them, and re-layouts: 1.54 us -> 0.01 us
    slice x10 -> x0, local copies, waits for them, and re-layouts: 1.24 us -> none  [the longest x8 1.09 us: split_rows(): grad_y = 0.5 * (jnp.roll(middle, -1, -1) - jnp.roll(middle, 1, -1))]
    reduce_sum x4 -> x0, other arithmetic: 1.12 us -> none  [block_terms(): jnp.sum(real_part, axis=1)]
  transfers between devices with their start and end apart: 5 -> 11, of which waited for: 3 -> 6; matrix products, arithmetic and copies ran while one was open for 6% -> 0% of each run, Pallas kernels for 0% -> 15%
where the time goes in v3:
time: 18.9 us; the launch traced here: 18.7 us
  starting transfers between devices  10.4 us (55%)
  waiting for transfers between devices  4.4 us (23%)
  Pallas kernels  3.78 us (20%)
    ppermute x3, starting transfers between devices, to_chip(): return lax.ppermute(value, 'harm', [(i, i ^ 2) for i in range(groups)])  5.03 us
    ppermute x2, starting transfers between devices, along_tile(): lax.ppermute(value, 'tile', [(i, (i + step) % tiles) for i in range(tiles)])  3.8 us
    pallas_call x10, Pallas kernels, call(): pl.pallas_call(functools.partial(kernel, sizes), in_specs=in_specs or [in...  3.78 us
    ppermute x6, waiting for transfers between devices, to_core(): return lax.ppermute(value, 'harm', [(i, i ^ 1) for i in range(groups)])  2.69 us
    ppermute x6, starting transfers between devices, to_core(): return lax.ppermute(value, 'harm', [(i, i ^ 1) for i in range(groups)])  1.6 us
    ppermute x2, waiting for transfers between devices, along_tile(): lax.ppermute(value, 'tile', [(i, (i + step) % tiles) for i in range(tiles)])  1.11 us
    ppermute x3, waiting for transfers between devices, to_chip(): return lax.ppermute(value, 'harm', [(i, i ^ 2) for i in range(groups)])  0.6 us
  transfers between devices with their start and end apart: 11, of which 6 were waited for; matrix products, arithmetic and copies ran while one was open for 0% of the time, Pallas kernels for 15%

profile of v3, /device:TPU:0, one launch (start us, length us, event | category | flops | bytes accessed | tf_op | source)
XLA Modules:
  0.0 18.7 jit_solution(16982747295098477807)
XLA Ops:
  0.0 0.5 %collective-permute-start = (f32[2,2,3,16,256]{4,3,2,1,0:T(8,128)}, f32[2,2,3,16,256]{4,3,2,1,0:T(8,128)S(1)}, u32[]{:S(2)}, u32[]{:S(2)}) collective-permute-start(f32[2,2,3,16,256]{4,3,2,1,0:T(8,128)} %base_a.1), channel_id=1, source_target_pairs={{0,4},{4,0},{8,12},{12,8},{1,5},{5,1},{9,13},{13,9},{2,6},{6,2},{1... | collective-permute-start | bytes 589832 | tf_op jit(solution)/shard_map/ppermute | solution.py:522
  0.5 2.5 %collective-permute-start.1 = (f32[2,2,3,16,256]{4,3,2,1,0:T(8,128)}, f32[2,2,3,16,256]{4,3,2,1,0:T(8,128)S(1)}, u32[]{:S(2)}, u32[]{:S(2)}) collective-permute-start(f32[2,2,3,16,256]{4,3,2,1,0:T(8,128)} %base_a.1), channel_id=1, source_target_pairs={{0,8},{4,12},{8,0},{12,4},{1,9},{5,13},{9,1},{13,5},{2,10},{6,14},... | collective-permute-start | bytes 589832 | tf_op jit(solution)/shard_map/ppermute | solution.py:519
  3.0 1.0 %shard_map.37 = (f32[2,2,5,16,256]{4,3,2,1,0:T(8,128)S(1)}, f32[16,256]{1,0:T(8,128)S(1)}, f32[2,2,4,16,256]{4,3,2,1,0:T(8,128)S(1)}) custom-call(f32[2,2,5,16,256]{4,3,2,1,0:T(8,128)} %q_from.1, f32[16,256]{1,0:T(8,128)} %visc_from.1), custom_call_target="tpu_custom_call" | custom-call | flops 1 | bytes 1 | tf_op jit(solution)/shard_map/pallas_call | solution.py:533
  4.0 1.6 %collective-permute-start.3 = (f32[24,256]{1,0:T(8,128)S(1)}, f32[24,256]{1,0:T(8,128)S(1)}, u32[]{:S(2)}, u32[]{:S(2)}) collective-permute-start(f32[24,256]{1,0:T(8,128)S(1)} %shard_map.38), channel_id=1, source_target_pairs={{0,1},{1,2},{2,3},{3,0},{4,5},{5,6},{6,7},{7,4},{8,9},{9,10},{10,1... | collective-permute-start | bytes 73736 | tf_op jit(solution)/shard_map/ppermute | solution.py:525
  5.6 0.5 %collective-permute-start.5 = (f32[2,2,4,16,256]{4,3,2,1,0:T(8,128)S(1)}, f32[2,2,4,16,256]{4,3,2,1,0:T(8,128)S(1)}, u32[]{:S(2)}, u32[]{:S(2)}) collective-permute-start(f32[2,2,4,16,256]{4,3,2,1,0:T(8,128)S(1)} %get-tuple-element.15), channel_id=1, source_target_pairs={{0,8},{4,12},{8,0},{12,4},{1,9},{5,13},{9,1},{13,5},{2,10},{6,14},... | collective-permute-start | bytes 786440 | tf_op jit(solution)/shard_map/ppermute | solution.py:519
  6.2 2.2 %collective-permute-start.4 = (f32[24,256]{1,0:T(8,128)S(1)}, f32[24,256]{1,0:T(8,128)S(1)}, u32[]{:S(2)}, u32[]{:S(2)}) collective-permute-start(f32[24,256]{1,0:T(8,128)S(1)} %shard_map.39), channel_id=1, source_target_pairs={{0,3},{1,0},{2,1},{3,2},{4,7},{5,4},{6,5},{7,6},{8,11},{9,8},{10,9... | collective-permute-start | bytes 73736 | tf_op jit(solution)/shard_map/ppermute | solution.py:525
  8.3 0.6 %collective-permute-done.1.base_c = f32[2,2,3,16,256]{4,3,2,1,0:T(8,128)S(1)} collective-permute-done((f32[2,2,3,16,256]{4,3,2,1,0:T(8,128)}, f32[2,2,3,16,256]{4,3,2,1,0:T(8,128)S(1)}, u32[]{:S(2)}, u32[]{:S(2)}) %collective-permute-start.1) | collective-permute-done | bytes 196640 | tf_op jit(solution)/shard_map/ppermute | solution.py:519
  8.9 0.0 collective-permute-start.2
  8.9 0.8 %collective-permute-done.3 = f32[24,256]{1,0:T(8,128)S(1)} collective-permute-done((f32[24,256]{1,0:T(8,128)S(1)}, f32[24,256]{1,0:T(8,128)S(1)}, u32[]{:S(2)}, u32[]{:S(2)}) %collective-permute-start.3) | collective-permute-done | bytes 24608 | tf_op jit(solution)/shard_map/ppermute | solution.py:525
  9.7 0.3 %collective-permute-done.4 = f32[24,256]{1,0:T(8,128)S(1)} collective-permute-done((f32[24,256]{1,0:T(8,128)S(1)}, f32[24,256]{1,0:T(8,128)S(1)}, u32[]{:S(2)}, u32[]{:S(2)}) %collective-permute-start.4) | collective-permute-done | bytes 24608 | tf_op jit(solution)/shard_map/ppermute | solution.py:525
  10.1 0.3 %collective-permute-done.2.base_d = f32[2,2,3,16,256]{4,3,2,1,0:T(8,128)S(1)} collective-permute-done((f32[2,2,3,16,256]{4,3,2,1,0:T(8,128)S(1)}, f32[2,2,3,16,256]{4,3,2,1,0:T(8,128)S(1)}, u32[]{:S(2)}, u32[]{:S(2)}) %collective-permute-start.2) | collective-permute-done | bytes 196640 | tf_op jit(solution)/shard_map/ppermute | solution.py:522
  10.4 0.3 %shard_map.40 = (f32[96,256]{1,0:T(8,128)S(1)}, f32[96,256]{1,0:T(8,128)S(1)}, f32[8,2,3,16,256]{4,3,2,1,0:T(8,128)S(1)}) custom-call(f32[2,2,3,16,256]{4,3,2,1,0:T(8,128)S(1)} %copy-done, f32[2,2,3,16,256]{4,3,2,1,0:T(8,128)S(1)} %collective-permute-done.refs_0_.base_b, f32[2,2,3,16,256]{4,3,2,1,0:T(8,128)S(1)} %collective-permute-done.1.base_c, ...), custom_call_target="tpu_custom_call" | custom-call | flops 1 | bytes 1 | tf_op jit(solution)/shard_map/pallas_call | solution.py:533
  10.7 0.2 %collective-permute-start.8 = (f32[2,2,5,16,256]{4,3,2,1,0:T(8,128)S(1)}, f32[2,2,5,16,256]{4,3,2,1,0:T(8,128)S(1)}, u32[]{:S(2)}, u32[]{:S(2)}) collective-permute-start(f32[2,2,5,16,256]{4,3,2,1,0:T(8,128)S(1)} %get-tuple-element.18.q_ref), channel_id=1, source_target_pairs={{0,4},{4,0},{8,12},{12,8},{1,5},{5,1},{9,13},{13,9},{2,6},{6,2},{1... | collective-permute-start | bytes 983048 | tf_op jit(solution)/shard_map/ppermute | solution.py:522
  10.9 0.4 %collective-permute-start.6 = (f32[96,256]{1,0:T(8,128)S(1)}, f32[96,256]{1,0:T(8,128)S(1)}, u32[]{:S(2)}, u32[]{:S(2)}) collective-permute-start(f32[96,256]{1,0:T(8,128)S(1)} %get-tuple-element.17), channel_id=1, source_target_pairs={{0,4},{4,0},{8,12},{12,8},{1,5},{5,1},{9,13},{13,9},{2,6},{6,2},{1... | collective-permute-start | bytes 294920 | tf_op jit(solution)/shard_map/ppermute | solution.py:522
  11.2 1.3 %collective-permute-done.6 = f32[96,256]{1,0:T(8,128)S(1)} collective-permute-done((f32[96,256]{1,0:T(8,128)S(1)}, f32[96,256]{1,0:T(8,128)S(1)}, u32[]{:S(2)}, u32[]{:S(2)}) %collective-permute-start.6) | collective-permute-done | bytes 98336 | tf_op jit(solution)/shard_map/ppermute | solution.py:522
  12.5 2.0 %collective-permute-start.10 = (f32[96,256]{1,0:T(8,128)S(1)}, f32[96,256]{1,0:T(8,128)S(1)}, u32[]{:S(2)}, u32[]{:S(2)}) collective-permute-start(f32[96,256]{1,0:T(8,128)S(1)} %add.3._), channel_id=1, source_target_pairs={{0,8},{4,12},{8,0},{12,4},{1,9},{5,13},{9,1},{13,5},{2,10},{6,14},... | collective-permute-start | bytes 294920 | tf_op jit(solution)/shard_map/ppermute | solution.py:519
  14.5 0.7 %shard_map.41.after.before_ref = f32[2,2,5,16,256]{4,3,2,1,0:T(8,128)S(1)} custom-call(f32[8,2,3,16,256]{4,3,2,1,0:T(8,128)S(1)} %get-tuple-element.14.base, f32[2,2,5,16,256]{4,3,2,1,0:T(8,128)S(1)} %get-tuple-element.18.q_ref, f32[48,256]{1,0:T(8,128)S(1)} %constant_dynamic-update-slice_fusion.halo_ref, f32[16,256]{1,0:T(8,128)S(1)} %get-tuple-element.13.visc_ref, ...), custom_call_target="tpu_custom_call" | custom-call | flops 1 | bytes 1 | tf_op jit(solution)/shard_map/pallas_call | solution.py:533
  15.2 0.0 collective-permute-done.5.values
  15.2 0.1 collective-permute-start.7
  15.3 0.5 %collective-permute-start.9 = (f32[48,256]{1,0:T(8,128)S(1)}, f32[48,256]{1,0:T(8,128)S(1)}, u32[]{:S(2)}, u32[]{:S(2)}) collective-permute-start(f32[48,256]{1,0:T(8,128)S(1)} %constant_dynamic-update-slice_fusion.halo_ref), channel_id=1, source_target_pairs={{0,4},{4,0},{8,12},{12,8},{1,5},{5,1},{9,13},{13,9},{2,6},{6,2},{1... | collective-permute-start | bytes 147464 | tf_op jit(solution)/shard_map/ppermute | solution.py:522
  15.8 1.1 %collective-permute-done.9.halo_ref = f32[48,256]{1,0:T(8,128)S(1)} collective-permute-done((f32[48,256]{1,0:T(8,128)S(1)}, f32[48,256]{1,0:T(8,128)S(1)}, u32[]{:S(2)}, u32[]{:S(2)}) %collective-permute-start.9) | collective-permute-done | bytes 49184 | tf_op jit(solution)/shard_map/ppermute | solution.py:522
  16.9 0.4 %shard_map.43.before_ref.near_ref = f32[2,2,5,16,256]{4,3,2,1,0:T(8,128)S(1)} custom-call(f32[8,2,3,16,256]{4,3,2,1,0:T(8,128)S(1)} %get-tuple-element.14.base, f32[2,2,5,16,256]{4,3,2,1,0:T(8,128)S(1)} %collective-permute-done.8.q_ref, f32[48,256]{1,0:T(8,128)S(1)} %collective-permute-done.9.halo_ref, f32[2,2,5,16,256]{4,3,2,1,0:T(8,128)S(1)} %shard_map.41.after.before_ref), custom_call_target="tpu_custom_call" | custom-call | flops 1 | bytes 1 | tf_op jit(solution)/shard_map/pallas_call | solution.py:533
  17.3 0.3 %shard_map.44._.far_ref = f32[2,2,4,16,256]{4,3,2,1,0:T(8,128)S(1)} custom-call(f32[8,2,3,16,256]{4,3,2,1,0:T(8,128)S(1)} %get-tuple-element.14.base, f32[2,2,4,16,256]{4,3,2,1,0:T(8,128)S(1)} %shard_map.42.q_ref, f32[2,2,5,16,256]{4,3,2,1,0:T(8,128)S(1)} %shard_map.43.before_ref.near_ref), custom_call_target="tpu_custom_call" | custom-call | flops 1 | bytes 1 | tf_op jit(solution)/shard_map/pallas_call | solution.py:533
  17.7 1.0 %shard_map.46 = f32[2,2,5,16,256]{4,3,2,1,0:T(8,128)} custom-call(f32[8,2,3,16,256]{4,3,2,1,0:T(8,128)S(1)} %get-tuple-element.14.base, f32[2,2,4,16,256]{4,3,2,1,0:T(8,128)S(1)} %collective-permute-done.7.q_diag, f32[2,2,1,16,256]{4,3,2,1,0:T(8,128)S(1)} %shard_map.45.sent_ref, f32[2,2,4,16,256]{4,3,2,1,0:T(8,128)S(1)} %shard_map.44._.far_ref, ...), custom_call_target="tpu_custom_call" | custom-call | flops 1 | bytes 1 | tf_op jit(solution)/shard_map/pallas_call | solution.py:533
  (13 shorter events, 0.1 us)
Async XLA Ops:
  0.0 6.1 %collective-permute-start = (f32[2,2,3,16,256]{4,3,2,1,0:T(8,128)}, f32[2,2,3,16,256]{4,3,2,1,0:T(8,128)S(1)}, u32[]{:S(2)}, u32[]{:S(2)}) collective-permute-start(f32[2,2,3,16,256]{4,3,2,1,0:T(8,128)} %base_a.1), channel_id=1, source_target_pairs={{0,4},{4,0},{8,12},{12,8},{1,5},{5,1},{9,13},{13,9},{2,6},{6,2},{1... | collective-permute-start | bytes 589832 | tf_op jit(solution)/shard_map/ppermute | solution.py:522
  0.5 8.5 %collective-permute-start.1 = (f32[2,2,3,16,256]{4,3,2,1,0:T(8,128)}, f32[2,2,3,16,256]{4,3,2,1,0:T(8,128)S(1)}, u32[]{:S(2)}, u32[]{:S(2)}) collective-permute-start(f32[2,2,3,16,256]{4,3,2,1,0:T(8,128)} %base_a.1), channel_id=1, source_target_pairs={{0,8},{4,12},{8,0},{12,4},{1,9},{5,13},{9,1},{13,5},{2,10},{6,14},... | collective-permute-start | bytes 589832 | tf_op jit(solution)/shard_map/ppermute | solution.py:519
  4.0 5.7 %collective-permute-start.3 = (f32[24,256]{1,0:T(8,128)S(1)}, f32[24,256]{1,0:T(8,128)S(1)}, u32[]{:S(2)}, u32[]{:S(2)}) collective-permute-start(f32[24,256]{1,0:T(8,128)S(1)} %shard_map.38), channel_id=1, source_target_pairs={{0,1},{1,2},{2,3},{3,0},{4,5},{5,6},{6,7},{7,4},{8,9},{9,10},{10,1... | collective-permute-start | bytes 73736 | tf_op jit(solution)/shard_map/ppermute | solution.py:525
  5.6 4.7 %copy-start = (f32[2,2,3,16,256]{4,3,2,1,0:T(8,128)S(1)}, f32[2,2,3,16,256]{4,3,2,1,0:T(8,128)}, u32[]{:S(2)}) copy-start(f32[2,2,3,16,256]{4,3,2,1,0:T(8,128)} %base_a.1) | copy-start | bytes 589828
  5.6 9.6 %collective-permute-start.5 = (f32[2,2,4,16,256]{4,3,2,1,0:T(8,128)S(1)}, f32[2,2,4,16,256]{4,3,2,1,0:T(8,128)S(1)}, u32[]{:S(2)}, u32[]{:S(2)}) collective-permute-start(f32[2,2,4,16,256]{4,3,2,1,0:T(8,128)S(1)} %get-tuple-element.15), channel_id=1, source_target_pairs={{0,8},{4,12},{8,0},{12,4},{1,9},{5,13},{9,1},{13,5},{2,10},{6,14},... | collective-permute-start | bytes 786440 | tf_op jit(solution)/shard_map/ppermute | solution.py:519
  6.2 3.9 %collective-permute-start.4 = (f32[24,256]{1,0:T(8,128)S(1)}, f32[24,256]{1,0:T(8,128)S(1)}, u32[]{:S(2)}, u32[]{:S(2)}) collective-permute-start(f32[24,256]{1,0:T(8,128)S(1)} %shard_map.39), channel_id=1, source_target_pairs={{0,3},{1,0},{2,1},{3,2},{4,7},{5,4},{6,5},{7,6},{8,11},{9,8},{10,9... | collective-permute-start | bytes 73736 | tf_op jit(solution)/shard_map/ppermute | solution.py:525
  8.9 1.4 %collective-permute-start.2 = (f32[2,2,3,16,256]{4,3,2,1,0:T(8,128)S(1)}, f32[2,2,3,16,256]{4,3,2,1,0:T(8,128)S(1)}, u32[]{:S(2)}, u32[]{:S(2)}) collective-permute-start(f32[2,2,3,16,256]{4,3,2,1,0:T(8,128)S(1)} %collective-permute-done.1.base_c), channel_id=1, source_target_pairs={{0,4},{4,0},{8,12},{12,8},{1,5},{5,1},{9,13},{13,9},{2,6},{6,2},{1... | collective-permute-start | bytes 589832 | tf_op jit(solution)/shard_map/ppermute | solution.py:522
  10.7 6.3 %collective-permute-start.8 = (f32[2,2,5,16,256]{4,3,2,1,0:T(8,128)S(1)}, f32[2,2,5,16,256]{4,3,2,1,0:T(8,128)S(1)}, u32[]{:S(2)}, u32[]{:S(2)}) collective-permute-start(f32[2,2,5,16,256]{4,3,2,1,0:T(8,128)S(1)} %get-tuple-element.18.q_ref), channel_id=1, source_target_pairs={{0,4},{4,0},{8,12},{12,8},{1,5},{5,1},{9,13},{13,9},{2,6},{6,2},{1... | collective-permute-start | bytes 983048 | tf_op jit(solution)/shard_map/ppermute | solution.py:522
  10.9 1.6 %collective-permute-start.6 = (f32[96,256]{1,0:T(8,128)S(1)}, f32[96,256]{1,0:T(8,128)S(1)}, u32[]{:S(2)}, u32[]{:S(2)}) collective-permute-start(f32[96,256]{1,0:T(8,128)S(1)} %get-tuple-element.17), channel_id=1, source_target_pairs={{0,4},{4,0},{8,12},{12,8},{1,5},{5,1},{9,13},{13,9},{2,6},{6,2},{1... | collective-permute-start | bytes 294920 | tf_op jit(solution)/shard_map/ppermute | solution.py:522
  12.5 5.2 %collective-permute-start.10 = (f32[96,256]{1,0:T(8,128)S(1)}, f32[96,256]{1,0:T(8,128)S(1)}, u32[]{:S(2)}, u32[]{:S(2)}) collective-permute-start(f32[96,256]{1,0:T(8,128)S(1)} %add.3._), channel_id=1, source_target_pairs={{0,8},{4,12},{8,0},{12,4},{1,9},{5,13},{9,1},{13,5},{2,10},{6,14},... | collective-permute-start | bytes 294920 | tf_op jit(solution)/shard_map/ppermute | solution.py:519
  15.2 2.5 %collective-permute-start.7 = (f32[2,2,4,16,256]{4,3,2,1,0:T(8,128)S(1)}, f32[2,2,4,16,256]{4,3,2,1,0:T(8,128)S(1)}, u32[]{:S(2)}, u32[]{:S(2)}) collective-permute-start(f32[2,2,4,16,256]{4,3,2,1,0:T(8,128)S(1)} %shard_map.42.q_ref), channel_id=1, source_target_pairs={{0,4},{4,0},{8,12},{12,8},{1,5},{5,1},{9,13},{13,9},{2,6},{6,2},{1... | collective-permute-start | bytes 786440 | tf_op jit(solution)/shard_map/ppermute | solution.py:522
  15.3 1.6 %collective-permute-start.9 = (f32[48,256]{1,0:T(8,128)S(1)}, f32[48,256]{1,0:T(8,128)S(1)}, u32[]{:S(2)}, u32[]{:S(2)}) collective-permute-start(f32[48,256]{1,0:T(8,128)S(1)} %constant_dynamic-update-slice_fusion.halo_ref), channel_id=1, source_target_pairs={{0,4},{4,0},{8,12},{12,8},{1,5},{5,1},{9,13},{13,9},{2,6},{6,2},{1... | collective-permute-start | bytes 147464 | tf_op jit(solution)/shard_map/ppermute | solution.py:522

commit v4 on v3

--- a/solution.py
+++ b/solution.py
@@ -289,22 +289,23 @@
 
 
 def result_kernel(
-    sizes, base_a, base_b, base_c, base_d, q_ref, halo_ref, near_ref, far_ref, base
+    sizes, base_a, base_b, base_c, base_d, q_own, q_core, halo_own, halo_core, out_ref, base
 ):
     me = lax.axis_index("harm")
     for place, ref in enumerate((base_a, base_b, base_c, base_d)):
         for harmonic in range(sizes.local):
             base[lax.bitwise_xor(me, place) * sizes.local + harmonic] = ref[harmonic]
-    targets = [
-        (lax.bitwise_xor(me, place) * sizes.local + harmonic, ref, harmonic)
-        for place, ref in ((2, near_ref), (3, far_ref))
+    targets = [lax.bitwise_xor(me, 2) * sizes.local + harmonic for harmonic in range(sizes.local)]
+    sources = [
+        (lax.bitwise_xor(me, place) * sizes.local + harmonic, q_ref, halo_ref, harmonic)
+        for place, q_ref, halo_ref in ((0, q_own, halo_own), (1, q_core, halo_core))
         for harmonic in range(sizes.local)
     ]
     first, last = sizes.sent
     parts = (0, 1)
     for field in range(first, last):
         moved = []
-        for harmonic in range(sizes.local):
+        for _, q_ref, halo_ref, harmonic in sources:
             terms = [[], [], []]
             for part in parts:
                 value = q_ref[harmonic, part, field]
@@ -316,15 +317,15 @@
             moved.append(terms)
         for start in range(0, sizes.width, 8):
             rows = slice(start, start + 8)
-            for target, ref, harmonic in targets:
+            for harmonic, target in enumerate(targets):
                 sums = (None, None)
-                for source in range(sizes.local):
-                    chosen = chosen_rows(sizes, base, target, me * sizes.local + source, rows)
-                    cut = [[value[rows] for value in term] for term in moved[source]]
+                for terms, (source, _, _, _) in zip(moved, sources, strict=True):
+                    chosen = chosen_rows(sizes, base, target, source, rows)
+                    cut = [[value[rows] for value in term] for term in terms]
                     sums = add_products(sums, chosen, cut)
                 for part in parts:
                     at = sizes.block(harmonic, part, field).start + start
-                    ref[at : at + 8, :] = sums[part]
+                    out_ref[at : at + 8, :] = sums[part]
     first, last = sizes.moved
     for side, row, sign in ((0, 0, -0.5), (1, sizes.width - 1, 0.5)):
         outside = [
@@ -338,25 +339,23 @@
                 )
                 for part in parts
             ]
-            for harmonic in range(sizes.local)
+            for _, _, halo_ref, harmonic in sources
         ]
-        for target, ref, harmonic in targets:
+        for harmonic, target in enumerate(targets):
             real = imag = 0.0
-            for source in range(sizes.local):
-                at = lax.rem(target - (me * sizes.local + source) + sizes.total, sizes.total)
+            for (q_real, q_imag), (source, _, _, _) in zip(outside, sources, strict=True):
+                at = lax.rem(target - source + sizes.total, sizes.total)
                 u_real = sign * base[at, 0, 0, row : row + 1, :]
                 u_imag = sign * base[at, 1, 0, row : row + 1, :]
-                q_real, q_imag = outside[source]
                 real = real + u_real * q_real - u_imag * q_imag
                 imag = imag + u_real * q_imag + u_imag * q_real
             for part, value in zip(parts, (real, imag), strict=True):
                 for field in range(first, last):
                     at = field - first
-                    ref[sizes.rim(harmonic, part, field, side), :] = value[at : at + 1, :]
+                    out_ref[sizes.rim(harmonic, part, field, side), :] = value[at : at + 1, :]
     tail = sizes.block_rows + sizes.local * 2 * (last - first) * 2
     if tail < sizes.message_rows:
-        for ref in (near_ref, far_ref):
-            ref[tail:, :] = jnp.zeros((sizes.message_rows - tail, sizes.columns), jnp.float32)
+        out_ref[tail:, :] = jnp.zeros((sizes.message_rows - tail, sizes.columns), jnp.float32)
 
 
 def own_terms_into(sizes, q_ref, visc_ref, halo_ref, sum_ref):
@@ -445,7 +444,7 @@
     return store
 
 
-def own_kernel(sizes, base, q_ref, halo_ref, visc_ref, _, sum_ref, *slopes):
+def own_kernel(sizes, base, q_ref, halo_ref, visc_ref, sum_ref, *slopes):
     own_terms_into(sizes, q_ref, visc_ref, halo_ref, sum_ref)
     everything = (0, sizes.fields)
     couple(
@@ -543,7 +542,6 @@
 
     slopes = [pltpu.VMEM((sizes.local, 2, sizes.width, sizes.columns), jnp.float32)] * 2
     edges = array(sizes.edge, sizes.columns)
-    message = array(sizes.message_rows, sizes.columns)
 
     base_chip = to_chip(base_flow)
     held, visc, moved = call(
@@ -567,21 +565,16 @@
     below = along_tile(down, -1)
     halo_own = jnp.concatenate([above, below], axis=0)
     halo_core = to_core(halo_own)
+    held_core = to_core(lax.optimization_barrier((held, base_core))[0])
     base_diag = to_core(base_chip)
-    near, far, base = call(
+    message, base = call(
         result_kernel,
-        (base_flow, base_core, base_chip, base_diag, held, halo_own),
-        [message, message, array(sizes.total, *base_flow.shape[1:])],
-    )
-    message_out = near + to_core(far)
-    results = to_chip(message_out)
-    held_core = to_core(lax.optimization_barrier((held, near))[0])
+        (base_flow, base_core, base_chip, base_diag, held, held_core, halo_own, halo_core),
+        [array(sizes.message_rows, sizes.columns), array(sizes.total, *base_flow.shape[1:])],
+    )
+    results = to_chip(message)
     own_sum = call(
-        own_kernel,
-        (base, held, halo_own, visc, message_out),
-        [array(*perturbation.shape)],
-        slopes,
-        [in_vmem] * 4 + [anywhere],
+        own_kernel, (base, held, halo_own, visc), [array(*perturbation.shape)], slopes
     )[0]
     near_sum = call(
         core_kernel, (base, held_core, halo_core, own_sum), [array(*perturbation.shape)], slopes
@@ -606,7 +599,7 @@
         sent_kernel,
         (near_sum, results, far_sum),
         [array(*sizes.shape(sizes.local, sizes.sent))],
-        flops=2*10**9,
+        flops=3*10**9,
         in_specs=[in_vmem, in_vmem, anywhere],
     )[0]
     return call(

time: 18.9 us -> 18 us (0.952)
  starting transfers between devices: 10.4 us -> 9.34 us
  waiting for transfers between devices: 4.4 us -> 4.61 us
    ppermute x6 -> x5, waiting for transfers between devices: 2.69 us -> 1.24 us  [to_core(): return lax.ppermute(value, 'harm', [(i, i ^ 1) for i in range(groups)])]
    ppermute x3, waiting for transfers between devices: 0.6 us -> 1.98 us  [to_chip(): return lax.ppermute(value, 'harm', [(i, i ^ 2) for i in range(groups)])]
    ppermute x6 -> x5, starting transfers between devices: 1.6 us -> 0.82 us  [to_core(): return lax.ppermute(value, 'harm', [(i, i ^ 1) for i in range(groups)])]
    ppermute x3, starting transfers between devices: 5.03 us -> 4.61 us  [to_chip(): return lax.ppermute(value, 'harm', [(i, i ^ 2) for i in range(groups)])]
    ppermute x2, waiting for transfers between devices: 1.11 us -> 1.4 us  [along_tile(): lax.ppermute(value, 'tile', [(i, (i + step) % tiles) for i in range(tiles)])]
  transfers between devices with their start and end apart: 11 -> 10, of which waited for: 6 -> 5; matrix products, arithmetic and copies ran while one was open for 0% -> 0% of each run, Pallas kernels for 15% -> 16%
where the time goes in v4:
time: 18 us; the launch traced here: 17.9 us
  starting transfers between devices  9.34 us (52%)
  waiting for transfers between devices  4.61 us (26%)
  Pallas kernels  3.81 us (21%)
    ppermute x3, starting transfers between devices, to_chip(): return lax.ppermute(value, 'harm', [(i, i ^ 2) for i in range(groups)])  4.61 us
    ppermute x2, starting transfers between devices, along_tile(): lax.ppermute(value, 'tile', [(i, (i + step) % tiles) for i in range(tiles)])  3.91 us
    pallas_call x10, Pallas kernels, call(): pl.pallas_call(functools.partial(kernel, sizes), in_specs=in_specs or [in...  3.81 us
    ppermute x3, waiting for transfers between devices, to_chip(): return lax.ppermute(value, 'harm', [(i, i ^ 2) for i in range(groups)])  1.98 us
    ppermute x2, waiting for transfers between devices, along_tile(): lax.ppermute(value, 'tile', [(i, (i + step) % tiles) for i in range(tiles)])  1.4 us
    ppermute x5, waiting for transfers between devices, to_core(): return lax.ppermute(value, 'harm', [(i, i ^ 1) for i in range(groups)])  1.24 us
    ppermute x5, starting transfers between devices, to_core(): return lax.ppermute(value, 'harm', [(i, i ^ 1) for i in range(groups)])  0.82 us
  transfers between devices with their start and end apart: 10, of which 5 were waited for; matrix products, arithmetic and copies ran while one was open for 0% of the time, Pallas kernels for 16%

profile of v4, /device:TPU:0, one launch (start us, length us, event | category | flops | bytes accessed | tf_op | source)
XLA Modules:
  0.0 17.9 jit_solution(5872816756954997148)
XLA Ops:
  0.0 0.5 %collective-permute-start = (f32[2,2,3,16,256]{4,3,2,1,0:T(8,128)}, f32[2,2,3,16,256]{4,3,2,1,0:T(8,128)S(1)}, u32[]{:S(2)}, u32[]{:S(2)}) collective-permute-start(f32[2,2,3,16,256]{4,3,2,1,0:T(8,128)} %base_a.1), channel_id=1, source_target_pairs={{0,4},{4,0},{8,12},{12,8},{1,5},{5,1},{9,13},{13,9},{2,6},{6,2},{1... | collective-permute-start | bytes 589832 | tf_op jit(solution)/shard_map/ppermute | solution.py:521
  0.5 2.5 %collective-permute-start.1 = (f32[2,2,3,16,256]{4,3,2,1,0:T(8,128)}, f32[2,2,3,16,256]{4,3,2,1,0:T(8,128)S(1)}, u32[]{:S(2)}, u32[]{:S(2)}) collective-permute-start(f32[2,2,3,16,256]{4,3,2,1,0:T(8,128)} %base_a.1), channel_id=1, source_target_pairs={{0,8},{4,12},{8,0},{12,4},{1,9},{5,13},{9,1},{13,5},{2,10},{6,14},... | collective-permute-start | bytes 589832 | tf_op jit(solution)/shard_map/ppermute | solution.py:518
  3.0 1.0 %shard_map.37 = (f32[2,2,5,16,256]{4,3,2,1,0:T(8,128)S(1)}, f32[16,256]{1,0:T(8,128)S(1)}, f32[2,2,4,16,256]{4,3,2,1,0:T(8,128)S(1)}) custom-call(f32[2,2,5,16,256]{4,3,2,1,0:T(8,128)} %q_from.1, f32[16,256]{1,0:T(8,128)} %visc_from.1), custom_call_target="tpu_custom_call" | custom-call | flops 1 | bytes 1 | tf_op jit(solution)/shard_map/pallas_call | solution.py:532
  4.0 0.0 collective-permute-done.refs_0_.base_b
  4.0 0.3 %collective-permute-start.3 = (f32[2,2,5,16,256]{4,3,2,1,0:T(8,128)S(1)}, f32[2,2,5,16,256]{4,3,2,1,0:T(8,128)S(1)}, u32[]{:S(2)}, u32[]{:S(2)}) collective-permute-start(f32[2,2,5,16,256]{4,3,2,1,0:T(8,128)S(1)} %get-tuple-element.12.q_ref.q_own), channel_id=1, source_target_pairs={{0,4},{4,0},{8,12},{12,8},{1,5},{5,1},{9,13},{13,9},{2,6},{6,2},{1... | collective-permute-start | bytes 983048 | tf_op jit(solution)/shard_map/ppermute | solution.py:521
  4.3 1.6 %collective-permute-start.4 = (f32[24,256]{1,0:T(8,128)S(1)}, f32[24,256]{1,0:T(8,128)S(1)}, u32[]{:S(2)}, u32[]{:S(2)}) collective-permute-start(f32[24,256]{1,0:T(8,128)S(1)} %shard_map.38), channel_id=1, source_target_pairs={{0,1},{1,2},{2,3},{3,0},{4,5},{5,6},{6,7},{7,4},{8,9},{9,10},{10,1... | collective-permute-start | bytes 73736 | tf_op jit(solution)/shard_map/ppermute | solution.py:524
  5.9 0.5 %collective-permute-start.7 = (f32[2,2,4,16,256]{4,3,2,1,0:T(8,128)S(1)}, f32[2,2,4,16,256]{4,3,2,1,0:T(8,128)S(1)}, u32[]{:S(2)}, u32[]{:S(2)}) collective-permute-start(f32[2,2,4,16,256]{4,3,2,1,0:T(8,128)S(1)} %get-tuple-element.15), channel_id=1, source_target_pairs={{0,8},{4,12},{8,0},{12,4},{1,9},{5,13},{9,1},{13,5},{2,10},{6,14},... | collective-permute-start | bytes 786440 | tf_op jit(solution)/shard_map/ppermute | solution.py:518
  6.5 2.3 %collective-permute-start.5 = (f32[24,256]{1,0:T(8,128)S(1)}, f32[24,256]{1,0:T(8,128)S(1)}, u32[]{:S(2)}, u32[]{:S(2)}) collective-permute-start(f32[24,256]{1,0:T(8,128)S(1)} %shard_map.39), channel_id=1, source_target_pairs={{0,3},{1,0},{2,1},{3,2},{4,7},{5,4},{6,5},{7,6},{8,11},{9,8},{10,9... | collective-permute-start | bytes 73736 | tf_op jit(solution)/shard_map/ppermute | solution.py:524
  8.7 0.2 %collective-permute-done.1.base_c = f32[2,2,3,16,256]{4,3,2,1,0:T(8,128)S(1)} collective-permute-done((f32[2,2,3,16,256]{4,3,2,1,0:T(8,128)}, f32[2,2,3,16,256]{4,3,2,1,0:T(8,128)S(1)}, u32[]{:S(2)}, u32[]{:S(2)}) %collective-permute-start.1) | collective-permute-done | bytes 196640 | tf_op jit(solution)/shard_map/ppermute | solution.py:518
  8.9 0.0 collective-permute-start.2
  8.9 1.1 %collective-permute-done.4 = f32[24,256]{1,0:T(8,128)S(1)} collective-permute-done((f32[24,256]{1,0:T(8,128)S(1)}, f32[24,256]{1,0:T(8,128)S(1)}, u32[]{:S(2)}, u32[]{:S(2)}) %collective-permute-start.4) | collective-permute-done | bytes 24608 | tf_op jit(solution)/shard_map/ppermute | solution.py:524
  10.0 0.3 %collective-permute-done.5 = f32[24,256]{1,0:T(8,128)S(1)} collective-permute-done((f32[24,256]{1,0:T(8,128)S(1)}, f32[24,256]{1,0:T(8,128)S(1)}, u32[]{:S(2)}, u32[]{:S(2)}) %collective-permute-start.5) | collective-permute-done | bytes 24608 | tf_op jit(solution)/shard_map/ppermute | solution.py:524
  10.3 0.0 collective-permute-start.6
  10.3 1.2 %collective-permute-done.6.halo_core.halo_ref = f32[48,256]{1,0:T(8,128)S(1)} collective-permute-done((f32[48,256]{1,0:T(8,128)S(1)}, f32[48,256]{1,0:T(8,128)S(1)}, u32[]{:S(2)}, u32[]{:S(2)}) %collective-permute-start.6) | collective-permute-done | bytes 49184 | tf_op jit(solution)/shard_map/ppermute | solution.py:521
  11.6 0.0 collective-permute-done.2.base_d
  11.6 0.0 collective-permute-done.3.q_core.q_ref
  11.6 0.3 %shard_map.40 = (f32[96,256]{1,0:T(8,128)S(1)}, f32[8,2,3,16,256]{4,3,2,1,0:T(8,128)S(1)}) custom-call(f32[2,2,3,16,256]{4,3,2,1,0:T(8,128)S(1)} %copy-done, f32[2,2,3,16,256]{4,3,2,1,0:T(8,128)S(1)} %collective-permute-done.refs_0_.base_b, f32[2,2,3,16,256]{4,3,2,1,0:T(8,128)S(1)} %collective-permute-done.1.base_c, ...), custom_call_target="tpu_custom_call" | custom-call | flops 1 | bytes 1 | tf_op jit(solution)/shard_map/pallas_call | solution.py:532
  11.9 1.6 %collective-permute-start.9 = (f32[96,256]{1,0:T(8,128)S(1)}, f32[96,256]{1,0:T(8,128)S(1)}, u32[]{:S(2)}, u32[]{:S(2)}) collective-permute-start(f32[96,256]{1,0:T(8,128)S(1)} %get-tuple-element.16), channel_id=1, source_target_pairs={{0,8},{4,12},{8,0},{12,4},{1,9},{5,13},{9,1},{13,5},{2,10},{6,14},... | collective-permute-start | bytes 294920 | tf_op jit(solution)/shard_map/ppermute | solution.py:518
  13.5 0.7 %shard_map.41.after.before_ref = f32[2,2,5,16,256]{4,3,2,1,0:T(8,128)S(1)} custom-call(f32[8,2,3,16,256]{4,3,2,1,0:T(8,128)S(1)} %get-tuple-element.14.base, f32[2,2,5,16,256]{4,3,2,1,0:T(8,128)S(1)} %get-tuple-element.12.q_ref.q_own, f32[48,256]{1,0:T(8,128)S(1)} %constant_dynamic-update-slice_fusion.halo_own.halo_ref, f32[16,256]{1,0:T(8,128)S(1)} %get-tuple-element.13.visc_ref), custom_call_target="tpu_custom_call" | custom-call | flops 1 | bytes 1 | tf_op jit(solution)/shard_map/pallas_call | solution.py:532
  14.2 0.4 %shard_map.43.before_ref.near_ref = f32[2,2,5,16,256]{4,3,2,1,0:T(8,128)S(1)} custom-call(f32[8,2,3,16,256]{4,3,2,1,0:T(8,128)S(1)} %get-tuple-element.14.base, f32[2,2,5,16,256]{4,3,2,1,0:T(8,128)S(1)} %collective-permute-done.3.q_core.q_ref, f32[48,256]{1,0:T(8,128)S(1)} %collective-permute-done.6.halo_core.halo_ref, ...), custom_call_target="tpu_custom_call" | custom-call | flops 1 | bytes 1 | tf_op jit(solution)/shard_map/pallas_call | solution.py:532
  14.6 0.1 collective-permute-start.8
  14.7 0.3 %shard_map.44._.far_ref = f32[2,2,4,16,256]{4,3,2,1,0:T(8,128)S(1)} custom-call(f32[8,2,3,16,256]{4,3,2,1,0:T(8,128)S(1)} %get-tuple-element.14.base, f32[2,2,4,16,256]{4,3,2,1,0:T(8,128)S(1)} %shard_map.42.q_ref, f32[2,2,5,16,256]{4,3,2,1,0:T(8,128)S(1)} %shard_map.43.before_ref.near_ref), custom_call_target="tpu_custom_call" | custom-call | flops 1 | bytes 1 | tf_op jit(solution)/shard_map/pallas_call | solution.py:532
  15.0 1.8 %collective-permute-done.9.message = f32[96,256]{1,0:T(8,128)S(1)} collective-permute-done((f32[96,256]{1,0:T(8,128)S(1)}, f32[96,256]{1,0:T(8,128)S(1)}, u32[]{:S(2)}, u32[]{:S(2)}) %collective-permute-start.9) | collective-permute-done | bytes 98336 | tf_op jit(solution)/shard_map/ppermute | solution.py:518
  16.8 1.0 %shard_map.46 = f32[2,2,5,16,256]{4,3,2,1,0:T(8,128)} custom-call(f32[8,2,3,16,256]{4,3,2,1,0:T(8,128)S(1)} %get-tuple-element.14.base, f32[2,2,4,16,256]{4,3,2,1,0:T(8,128)S(1)} %collective-permute-done.8.q_diag, f32[2,2,1,16,256]{4,3,2,1,0:T(8,128)S(1)} %shard_map.45.sent_ref, f32[2,2,4,16,256]{4,3,2,1,0:T(8,128)S(1)} %shard_map.44._.far_ref, ...), custom_call_target="tpu_custom_call" | custom-call | flops 1 | bytes 1 | tf_op jit(solution)/shard_map/pallas_call | solution.py:532
  (10 shorter events, 0.1 us)
Async XLA Ops:
  0.0 4.0 %collective-permute-start = (f32[2,2,3,16,256]{4,3,2,1,0:T(8,128)}, f32[2,2,3,16,256]{4,3,2,1,0:T(8,128)S(1)}, u32[]{:S(2)}, u32[]{:S(2)}) collective-permute-start(f32[2,2,3,16,256]{4,3,2,1,0:T(8,128)} %base_a.1), channel_id=1, source_target_pairs={{0,4},{4,0},{8,12},{12,8},{1,5},{5,1},{9,13},{13,9},{2,6},{6,2},{1... | collective-permute-start | bytes 589832 | tf_op jit(solution)/shard_map/ppermute | solution.py:521
  0.5 8.5 %collective-permute-start.1 = (f32[2,2,3,16,256]{4,3,2,1,0:T(8,128)}, f32[2,2,3,16,256]{4,3,2,1,0:T(8,128)S(1)}, u32[]{:S(2)}, u32[]{:S(2)}) collective-permute-start(f32[2,2,3,16,256]{4,3,2,1,0:T(8,128)} %base_a.1), channel_id=1, source_target_pairs={{0,8},{4,12},{8,0},{12,4},{1,9},{5,13},{9,1},{13,5},{2,10},{6,14},... | collective-permute-start | bytes 589832 | tf_op jit(solution)/shard_map/ppermute | solution.py:518
  4.0 7.6 %collective-permute-start.3 = (f32[2,2,5,16,256]{4,3,2,1,0:T(8,128)S(1)}, f32[2,2,5,16,256]{4,3,2,1,0:T(8,128)S(1)}, u32[]{:S(2)}, u32[]{:S(2)}) collective-permute-start(f32[2,2,5,16,256]{4,3,2,1,0:T(8,128)S(1)} %get-tuple-element.12.q_ref.q_own), channel_id=1, source_target_pairs={{0,4},{4,0},{8,12},{12,8},{1,5},{5,1},{9,13},{13,9},{2,6},{6,2},{1... | collective-permute-start | bytes 983048 | tf_op jit(solution)/shard_map/ppermute | solution.py:521
  4.3 5.7 %collective-permute-start.4 = (f32[24,256]{1,0:T(8,128)S(1)}, f32[24,256]{1,0:T(8,128)S(1)}, u32[]{:S(2)}, u32[]{:S(2)}) collective-permute-start(f32[24,256]{1,0:T(8,128)S(1)} %shard_map.38), channel_id=1, source_target_pairs={{0,1},{1,2},{2,3},{3,0},{4,5},{5,6},{6,7},{7,4},{8,9},{9,10},{10,1... | collective-permute-start | bytes 73736 | tf_op jit(solution)/shard_map/ppermute | solution.py:524
  5.9 5.6 %copy-start = (f32[2,2,3,16,256]{4,3,2,1,0:T(8,128)S(1)}, f32[2,2,3,16,256]{4,3,2,1,0:T(8,128)}, u32[]{:S(2)}) copy-start(f32[2,2,3,16,256]{4,3,2,1,0:T(8,128)} %base_a.1) | copy-start | bytes 589828
  5.9 8.7 %collective-permute-start.7 = (f32[2,2,4,16,256]{4,3,2,1,0:T(8,128)S(1)}, f32[2,2,4,16,256]{4,3,2,1,0:T(8,128)S(1)}, u32[]{:S(2)}, u32[]{:S(2)}) collective-permute-start(f32[2,2,4,16,256]{4,3,2,1,0:T(8,128)S(1)} %get-tuple-element.15), channel_id=1, source_target_pairs={{0,8},{4,12},{8,0},{12,4},{1,9},{5,13},{9,1},{13,5},{2,10},{6,14},... | collective-permute-start | bytes 786440 | tf_op jit(solution)/shard_map/ppermute | solution.py:518
  6.5 3.9 %collective-permute-start.5 = (f32[24,256]{1,0:T(8,128)S(1)}, f32[24,256]{1,0:T(8,128)S(1)}, u32[]{:S(2)}, u32[]{:S(2)}) collective-permute-start(f32[24,256]{1,0:T(8,128)S(1)} %shard_map.39), channel_id=1, source_target_pairs={{0,3},{1,0},{2,1},{3,2},{4,7},{5,4},{6,5},{7,6},{8,11},{9,8},{10,9... | collective-permute-start | bytes 73736 | tf_op jit(solution)/shard_map/ppermute | solution.py:524
  8.9 2.6 %collective-permute-start.2 = (f32[2,2,3,16,256]{4,3,2,1,0:T(8,128)S(1)}, f32[2,2,3,16,256]{4,3,2,1,0:T(8,128)S(1)}, u32[]{:S(2)}, u32[]{:S(2)}) collective-permute-start(f32[2,2,3,16,256]{4,3,2,1,0:T(8,128)S(1)} %collective-permute-done.1.base_c), channel_id=1, source_target_pairs={{0,4},{4,0},{8,12},{12,8},{1,5},{5,1},{9,13},{13,9},{2,6},{6,2},{1... | collective-permute-start | bytes 589832 | tf_op jit(solution)/shard_map/ppermute | solution.py:521
  10.3 1.2 %collective-permute-start.6 = (f32[48,256]{1,0:T(8,128)S(1)}, f32[48,256]{1,0:T(8,128)S(1)}, u32[]{:S(2)}, u32[]{:S(2)}) collective-permute-start(f32[48,256]{1,0:T(8,128)S(1)} %constant_dynamic-update-slice_fusion.halo_own.halo_ref), channel_id=1, source_target_pairs={{0,4},{4,0},{8,12},{12,8},{1,5},{5,1},{9,13},{13,9},{2,6},{6,2},{1... | collective-permute-start | bytes 147464 | tf_op jit(solution)/shard_map/ppermute | solution.py:521
  11.9 4.9 %collective-permute-start.9 = (f32[96,256]{1,0:T(8,128)S(1)}, f32[96,256]{1,0:T(8,128)S(1)}, u32[]{:S(2)}, u32[]{:S(2)}) collective-permute-start(f32[96,256]{1,0:T(8,128)S(1)} %get-tuple-element.16), channel_id=1, source_target_pairs={{0,8},{4,12},{8,0},{12,4},{1,9},{5,13},{9,1},{13,5},{2,10},{6,14},... | collective-permute-start | bytes 294920 | tf_op jit(solution)/shard_map/ppermute | solution.py:518
  14.6 2.2 %collective-permute-start.8 = (f32[2,2,4,16,256]{4,3,2,1,0:T(8,128)S(1)}, f32[2,2,4,16,256]{4,3,2,1,0:T(8,128)S(1)}, u32[]{:S(2)}, u32[]{:S(2)}) collective-permute-start(f32[2,2,4,16,256]{4,3,2,1,0:T(8,128)S(1)} %shard_map.42.q_ref), channel_id=1, source_target_pairs={{0,4},{4,0},{8,12},{12,8},{1,5},{5,1},{9,13},{13,9},{2,6},{6,2},{1... | collective-permute-start | bytes 786440 | tf_op jit(solution)/shard_map/ppermute | solution.py:521

commit v5 on v4

--- a/solution.py
+++ b/solution.py
@@ -288,13 +288,8 @@
     return [[base[at, part, term, rows, :] for part in (0, 1)] for term in range(3)]
 
 
-def result_kernel(
-    sizes, base_a, base_b, base_c, base_d, q_own, q_core, halo_own, halo_core, out_ref, base
-):
+def result_kernel(sizes, base, q_own, q_core, halo_own, halo_core, out_ref):
     me = lax.axis_index("harm")
-    for place, ref in enumerate((base_a, base_b, base_c, base_d)):
-        for harmonic in range(sizes.local):
-            base[lax.bitwise_xor(me, place) * sizes.local + harmonic] = ref[harmonic]
     targets = [lax.bitwise_xor(me, 2) * sizes.local + harmonic for harmonic in range(sizes.local)]
     sources = [
         (lax.bitwise_xor(me, place) * sizes.local + harmonic, q_ref, halo_ref, harmonic)
@@ -444,7 +439,13 @@
     return store
 
 
-def own_kernel(sizes, base, q_ref, halo_ref, visc_ref, sum_ref, *slopes):
+def own_kernel(
+    sizes, base_a, base_b, base_c, base_d, q_ref, halo_ref, visc_ref, sum_ref, base, *slopes
+):
+    me = lax.axis_index("harm")
+    for place, ref in enumerate((base_a, base_b, base_c, base_d)):
+        for harmonic in range(sizes.local):
+            base[lax.bitwise_xor(me, place) * sizes.local + harmonic] = ref[harmonic]
     own_terms_into(sizes, q_ref, visc_ref, halo_ref, sum_ref)
     everything = (0, sizes.fields)
     couple(
@@ -459,14 +460,29 @@
     )
 
 
-def far_kernel(place):
-    def kernel(sizes, base, q_ref, before_ref, sum_ref, *slopes):
-        couple(
-            sizes, base, place, sizes.moved, reader(before_ref), q_ref, None, slopes,
-            writer(sum_ref),
-        )
-
-    return kernel
+class Pieces:
+    def __init__(self, sizes, refs):
+        self.fields = sizes.moved[1]
+        self.planes = [(ref, plane) for ref in refs for plane in range(ref.shape[0])]
+
+    def __getitem__(self, at):
+        harmonic, part, field, *rest = at
+        ref, plane = self.planes[(harmonic * 2 + part) * self.fields + field]
+        return ref[(plane, *rest)]
+
+
+def chip_kernel(sizes, base, q_ref, before_ref, sum_ref, *slopes):
+    couple(
+        sizes, base, 2, sizes.moved, reader(before_ref), q_ref, None, slopes, writer(sum_ref)
+    )
+
+
+def diag_kernel(sizes, base, before_ref, *refs):
+    *values, sum_ref, slopes_x, slopes_y = refs
+    values, slopes = Pieces(sizes, values), (slopes_x, slopes_y)
+    couple(
+        sizes, base, 3, sizes.moved, reader(before_ref), values, None, slopes, writer(sum_ref)
+    )
 
 
 def pass_kernel(sizes, values, after, same):
@@ -482,26 +498,19 @@
                 sum_ref[harmonic, part, field - first] = near_ref[harmonic, part, field] + more
 
 
-def last_kernel(
-    sizes, base, q_diag, sent_ref, far_ref, message, out_ref, slopes_x, slopes_y, result, sems
-):
+def last_kernel(sizes, sent_ref, far_ref, message, out_ref, result, sems):
     copies = []
 
     def send(source, field):
-        copies.append(
-            pltpu.make_async_copy(source, out_ref.at[:, :, field], sems.at[field])
-        )
+        copies.append(pltpu.make_async_copy(source, out_ref.at[:, :, field], sems.at[field]))
         copies[-1].start()
 
     for field in range(*sizes.sent):
         send(sent_ref.at[:, :, field - sizes.sent[0]], field)
     for field in range(*sizes.moved):
-        couple(
-            sizes, base, 3, (field, field + 1), reader(far_ref), q_diag, None, (slopes_x, slopes_y),
-            writer(result),
-        )
         for harmonic in range(sizes.local):
             for part in (0, 1):
+                result[harmonic, part, field] = far_ref[harmonic, part, field]
                 for side, row in ((0, 0), (1, sizes.width - 1)):
                     more = message[sizes.rim(harmonic, part, field, side), :]
                     result[harmonic, part, field, row : row + 1, :] += more
@@ -565,33 +574,44 @@
     below = along_tile(down, -1)
     halo_own = jnp.concatenate([above, below], axis=0)
     halo_core = to_core(halo_own)
-    held_core = to_core(lax.optimization_barrier((held, base_core))[0])
+    held_core = to_core(perturbation)
     base_diag = to_core(base_chip)
-    message, base = call(
+    own_sum, base = call(
+        own_kernel,
+        (base_flow, base_core, base_chip, base_diag, held, halo_own, visc),
+        [array(*perturbation.shape), array(sizes.total, *base_flow.shape[1:])],
+        slopes,
+    )
+    message = call(
         result_kernel,
-        (base_flow, base_core, base_chip, base_diag, held, held_core, halo_own, halo_core),
-        [array(sizes.message_rows, sizes.columns), array(sizes.total, *base_flow.shape[1:])],
-    )
+        (base, held, held_core, halo_own, halo_core),
+        [array(sizes.message_rows, sizes.columns)],
+    )[0]
     results = to_chip(message)
-    own_sum = call(
-        own_kernel, (base, held, halo_own, visc), [array(*perturbation.shape)], slopes
-    )[0]
     near_sum = call(
         core_kernel, (base, held_core, halo_core, own_sum), [array(*perturbation.shape)], slopes
     )[0]
     moved_here = call(
         pass_kernel,
-        (moved_chip, own_sum),
+        (moved_chip, near_sum),
         array(*moved_chip.shape),
         in_specs=[anywhere] * 2,
         out_specs=anywhere,
-        flops=10**9,
+        flops=1,
         aliases={0: 0},
     )
-    moved_diag = to_core(moved_here)
+    flat = moved_here.reshape(-1, sizes.width, sizes.columns)
+    starts = [len(flat) * place // 3 for place in range(3 + 1)]
+    pieces = [to_core(flat[begin:end]) for begin, end in zip(starts, starts[1:])]
     far_sum = call(
-        far_kernel(2),
+        chip_kernel,
         (base, moved_here, near_sum),
+        [array(*sizes.shape(sizes.local, sizes.moved))],
+        slopes,
+    )[0]
+    far_sum = call(
+        diag_kernel,
+        (base, far_sum, *pieces),
         [array(*sizes.shape(sizes.local, sizes.moved))],
         slopes,
     )[0]
@@ -604,10 +624,9 @@
     )[0]
     return call(
         last_kernel,
-        (base, moved_diag, sent_sum, far_sum, results),
+        (sent_sum, far_sum, results),
         array(*perturbation.shape),
         [
-            *slopes,
             pltpu.VMEM(sizes.shape(sizes.local, sizes.moved), jnp.float32),
             pltpu.SemaphoreType.DMA((sizes.fields,)),
         ],

time: 18 us -> 17.6 us (0.978)
  waiting for transfers between devices: 4.61 us -> 3.68 us
  starting transfers between devices: 9.34 us -> 9.84 us
    ppermute x3, waiting for transfers between devices: 1.98 us -> 0.97 us  [to_chip(): return lax.ppermute(value, 'harm', [(i, i ^ 2) for i in range(groups)])]
    ppermute x5 -> x7, starting transfers between devices: 0.82 us -> 1.39 us  [to_core(): return lax.ppermute(value, 'harm', [(i, i ^ 1) for i in range(groups)])]
    ppermute x5 -> x7, waiting for transfers between devices: 1.24 us -> 1.37 us  [to_core(): return lax.ppermute(value, 'harm', [(i, i ^ 1) for i in range(groups)])]
    pallas_call x10 -> x11, Pallas kernels: 3.81 us -> 3.85 us  [call(): pl.pallas_call(functools.partial(kernel, sizes), in_specs=in_specs or [in...]
  transfers between devices with their start and end apart: 10 -> 12, of which waited for: 5 -> 9; matrix products, arithmetic and copies ran while one was open for 0% -> 0% of each run, Pallas kernels for 16% -> 18%
where the time goes in v5:
time: 17.6 us; the launch traced here: 17.5 us
  starting transfers between devices  9.84 us (56%)
  Pallas kernels  3.85 us (22%)
  waiting for transfers between devices  3.68 us (21%)
    ppermute x3, starting transfers between devices, to_chip(): return lax.ppermute(value, 'harm', [(i, i ^ 2) for i in range(groups)])  4.66 us
    pallas_call x11, Pallas kernels, call(): pl.pallas_call(functools.partial(kernel, sizes), in_specs=in_specs or [in...  3.85 us
    ppermute x2, starting transfers between devices, along_tile(): lax.ppermute(value, 'tile', [(i, (i + step) % tiles) for i in range(tiles)])  3.8 us
    ppermute x7, starting transfers between devices, to_core(): return lax.ppermute(value, 'harm', [(i, i ^ 1) for i in range(groups)])  1.39 us
    ppermute x7, waiting for transfers between devices, to_core(): return lax.ppermute(value, 'harm', [(i, i ^ 1) for i in range(groups)])  1.37 us
    ppermute x2, waiting for transfers between devices, along_tile(): lax.ppermute(value, 'tile', [(i, (i + step) % tiles) for i in range(tiles)])  1.33 us
    ppermute x3, waiting for transfers between devices, to_chip(): return lax.ppermute(value, 'harm', [(i, i ^ 2) for i in range(groups)])  0.97 us
  transfers between devices with their start and end apart: 12, of which 9 were waited for; matrix products, arithmetic and copies ran while one was open for 0% of the time, Pallas kernels for 18%

profile of v5, /device:TPU:0, one launch (start us, length us, event | category | flops | bytes accessed | tf_op | source)
XLA Modules:
  0.0 17.5 jit_solution(17706455631972154671)
XLA Ops:
  0.0 0.5 %collective-permute-start = (f32[2,2,3,16,256]{4,3,2,1,0:T(8,128)}, f32[2,2,3,16,256]{4,3,2,1,0:T(8,128)S(1)}, u32[]{:S(2)}, u32[]{:S(2)}) collective-permute-start(f32[2,2,3,16,256]{4,3,2,1,0:T(8,128)} %base_a.1), channel_id=1, source_target_pairs={{0,4},{4,0},{8,12},{12,8},{1,5},{5,1},{9,13},{13,9},{2,6},{6,2},{1... | collective-permute-start | bytes 589832 | tf_op jit(solution)/shard_map/ppermute | solution.py:530
  0.5 2.5 %collective-permute-start.1 = (f32[2,2,3,16,256]{4,3,2,1,0:T(8,128)}, f32[2,2,3,16,256]{4,3,2,1,0:T(8,128)S(1)}, u32[]{:S(2)}, u32[]{:S(2)}) collective-permute-start(f32[2,2,3,16,256]{4,3,2,1,0:T(8,128)} %base_a.1), channel_id=1, source_target_pairs={{0,8},{4,12},{8,0},{12,4},{1,9},{5,13},{9,1},{13,5},{2,10},{6,14},... | collective-permute-start | bytes 589832 | tf_op jit(solution)/shard_map/ppermute | solution.py:527
  3.0 0.2 %collective-permute-start.5 = (f32[2,2,5,16,256]{4,3,2,1,0:T(8,128)}, f32[2,2,5,16,256]{4,3,2,1,0:T(8,128)S(1)}, u32[]{:S(2)}, u32[]{:S(2)}) collective-permute-start(f32[2,2,5,16,256]{4,3,2,1,0:T(8,128)} %q_from.1), channel_id=1, source_target_pairs={{0,4},{4,0},{8,12},{12,8},{1,5},{5,1},{9,13},{13,9},{2,6},{6,2},{1... | collective-permute-start | bytes 983048 | tf_op jit(solution)/shard_map/ppermute | solution.py:530
  3.2 1.0 %shard_map.37 = (f32[2,2,5,16,256]{4,3,2,1,0:T(8,128)S(1)}, f32[16,256]{1,0:T(8,128)S(1)}, f32[2,2,4,16,256]{4,3,2,1,0:T(8,128)S(1)}) custom-call(f32[2,2,5,16,256]{4,3,2,1,0:T(8,128)} %q_from.1, f32[16,256]{1,0:T(8,128)} %visc_from.1), custom_call_target="tpu_custom_call" | custom-call | flops 1 | bytes 1 | tf_op jit(solution)/shard_map/pallas_call | solution.py:541
  4.2 1.6 %collective-permute-start.3 = (f32[24,256]{1,0:T(8,128)S(1)}, f32[24,256]{1,0:T(8,128)S(1)}, u32[]{:S(2)}, u32[]{:S(2)}) collective-permute-start(f32[24,256]{1,0:T(8,128)S(1)} %shard_map.38), channel_id=1, source_target_pairs={{0,1},{1,2},{2,3},{3,0},{4,5},{5,6},{6,7},{7,4},{8,9},{9,10},{10,1... | collective-permute-start | bytes 73736 | tf_op jit(solution)/shard_map/ppermute | solution.py:533
  5.9 0.5 %collective-permute-start.8 = (f32[2,2,4,16,256]{4,3,2,1,0:T(8,128)S(1)}, f32[2,2,4,16,256]{4,3,2,1,0:T(8,128)S(1)}, u32[]{:S(2)}, u32[]{:S(2)}) collective-permute-start(f32[2,2,4,16,256]{4,3,2,1,0:T(8,128)S(1)} %get-tuple-element.14), channel_id=1, source_target_pairs={{0,8},{4,12},{8,0},{12,4},{1,9},{5,13},{9,1},{13,5},{2,10},{6,14},... | collective-permute-start | bytes 786440 | tf_op jit(solution)/shard_map/ppermute | solution.py:527
  6.4 2.2 %collective-permute-start.4 = (f32[24,256]{1,0:T(8,128)S(1)}, f32[24,256]{1,0:T(8,128)S(1)}, u32[]{:S(2)}, u32[]{:S(2)}) collective-permute-start(f32[24,256]{1,0:T(8,128)S(1)} %shard_map.39), channel_id=1, source_target_pairs={{0,3},{1,0},{2,1},{3,2},{4,7},{5,4},{6,5},{7,6},{8,11},{9,8},{10,9... | collective-permute-start | bytes 73736 | tf_op jit(solution)/shard_map/ppermute | solution.py:533
  8.6 0.4 %collective-permute-done.1.base_c = f32[2,2,3,16,256]{4,3,2,1,0:T(8,128)S(1)} collective-permute-done((f32[2,2,3,16,256]{4,3,2,1,0:T(8,128)}, f32[2,2,3,16,256]{4,3,2,1,0:T(8,128)S(1)}, u32[]{:S(2)}, u32[]{:S(2)}) %collective-permute-start.1) | collective-permute-done | bytes 196640 | tf_op jit(solution)/shard_map/ppermute | solution.py:527
  8.9 1.0 %collective-permute-done.3 = f32[24,256]{1,0:T(8,128)S(1)} collective-permute-done((f32[24,256]{1,0:T(8,128)S(1)}, f32[24,256]{1,0:T(8,128)S(1)}, u32[]{:S(2)}, u32[]{:S(2)}) %collective-permute-start.3) | collective-permute-done | bytes 24608 | tf_op jit(solution)/shard_map/ppermute | solution.py:533
  9.9 0.3 %collective-permute-done.4 = f32[24,256]{1,0:T(8,128)S(1)} collective-permute-done((f32[24,256]{1,0:T(8,128)S(1)}, f32[24,256]{1,0:T(8,128)S(1)}, u32[]{:S(2)}, u32[]{:S(2)}) %collective-permute-start.4) | collective-permute-done | bytes 24608 | tf_op jit(solution)/shard_map/ppermute | solution.py:533
  10.3 0.1 collective-permute-done.2.base_d
  10.4 0.7 %shard_map.40 = (f32[2,2,5,16,256]{4,3,2,1,0:T(8,128)S(1)}, f32[8,2,3,16,256]{4,3,2,1,0:T(8,128)S(1)}) custom-call(f32[2,2,3,16,256]{4,3,2,1,0:T(8,128)S(1)} %copy-done, f32[2,2,3,16,256]{4,3,2,1,0:T(8,128)S(1)} %collective-permute-done.refs_0_.base_b, f32[2,2,3,16,256]{4,3,2,1,0:T(8,128)S(1)} %collective-permute-done.1.base_c, ...), custom_call_target="tpu_custom_call" | custom-call | flops 1 | bytes 1 | tf_op jit(solution)/shard_map/pallas_call | solution.py:541
  11.1 0.4 %collective-permute-done.6.halo_ref.halo_core = f32[48,256]{1,0:T(8,128)S(1)} collective-permute-done((f32[48,256]{1,0:T(8,128)S(1)}, f32[48,256]{1,0:T(8,128)S(1)}, u32[]{:S(2)}, u32[]{:S(2)}) %collective-permute-start.6) | collective-permute-done | bytes 49184 | tf_op jit(solution)/shard_map/ppermute | solution.py:530
  11.5 0.3 %shard_map.42 = f32[96,256]{1,0:T(8,128)S(1)} custom-call(f32[8,2,3,16,256]{4,3,2,1,0:T(8,128)S(1)} %get-tuple-element.12.base, f32[2,2,5,16,256]{4,3,2,1,0:T(8,128)S(1)} %get-tuple-element.10.q_ref.q_own, f32[2,2,5,16,256]{4,3,2,1,0:T(8,128)S(1)} %collective-permute-done.5.q_ref.q_core, f32[48,256]{1,0:T(8,128)S(1)} %constant_dynamic-update-slice_fusion.halo_ref.halo_own, ...), custom_call_target="tpu_custom_call" | custom-call | flops 1 | bytes 1 | tf_op jit(solution)/shard_map/pallas_call | solution.py:541
  11.8 1.6 %collective-permute-start.7 = (f32[96,256]{1,0:T(8,128)S(1)}, f32[96,256]{1,0:T(8,128)S(1)}, u32[]{:S(2)}, u32[]{:S(2)}) collective-permute-start(f32[96,256]{1,0:T(8,128)S(1)} %shard_map.42), channel_id=1, source_target_pairs={{0,8},{4,12},{8,0},{12,4},{1,9},{5,13},{9,1},{13,5},{2,10},{6,14},... | collective-permute-start | bytes 294920 | tf_op jit(solution)/shard_map/ppermute | solution.py:527
  13.4 0.4 %shard_map.41.after.before_ref.near_ref = f32[2,2,5,16,256]{4,3,2,1,0:T(8,128)S(1)} custom-call(f32[8,2,3,16,256]{4,3,2,1,0:T(8,128)S(1)} %get-tuple-element.12.base, f32[2,2,5,16,256]{4,3,2,1,0:T(8,128)S(1)} %collective-permute-done.5.q_ref.q_core, f32[48,256]{1,0:T(8,128)S(1)} %collective-permute-done.6.halo_ref.halo_core, ...), custom_call_target="tpu_custom_call" | custom-call | flops 1 | bytes 1 | tf_op jit(solution)/shard_map/pallas_call | solution.py:541
  13.8 0.5 %collective-permute-done.8.values = f32[2,2,4,16,256]{4,3,2,1,0:T(8,128)S(1)} collective-permute-done((f32[2,2,4,16,256]{4,3,2,1,0:T(8,128)S(1)}, f32[2,2,4,16,256]{4,3,2,1,0:T(8,128)S(1)}, u32[]{:S(2)}, u32[]{:S(2)}) %collective-permute-start.8) | collective-permute-done | bytes 262176 | tf_op jit(solution)/shard_map/ppermute | solution.py:527
  14.5 0.6 %collective-permute-start.9 = (f32[5,16,256]{2,1,0:T(8,128)S(1)}, f32[5,16,256]{2,1,0:T(8,128)S(1)}, u32[]{:S(2)}, u32[]{:S(2)}) collective-permute-start(f32[5,16,256]{2,1,0:T(8,128)S(1)} %get-tuple-element.16), channel_id=1, source_target_pairs={{0,4},{4,0},{8,12},{12,8},{1,5},{5,1},{9,13},{13,9},{2,6},{6,2},{1... | collective-permute-start | bytes 245768 | tf_op jit(solution)/shard_map/ppermute | solution.py:530
  15.0 0.1 collective-permute-start.10
  15.1 0.3 %shard_map.44.before_ref = f32[2,2,4,16,256]{4,3,2,1,0:T(8,128)S(1)} custom-call(f32[8,2,3,16,256]{4,3,2,1,0:T(8,128)S(1)} %get-tuple-element.12.base, f32[2,2,4,16,256]{4,3,2,1,0:T(8,128)S(1)} %shard_map.43.q_ref, f32[2,2,5,16,256]{4,3,2,1,0:T(8,128)S(1)} %shard_map.41.after.before_ref.near_ref), custom_call_target="tpu_custom_call" | custom-call | flops 1 | bytes 1 | tf_op jit(solution)/shard_map/pallas_call | solution.py:541
  15.4 0.5 %collective-permute-done.9.refs_0_ = f32[5,16,256]{2,1,0:T(8,128)S(1)} collective-permute-done((f32[5,16,256]{2,1,0:T(8,128)S(1)}, f32[5,16,256]{2,1,0:T(8,128)S(1)}, u32[]{:S(2)}, u32[]{:S(2)}) %collective-permute-start.9) | collective-permute-done | bytes 81952 | tf_op jit(solution)/shard_map/ppermute | solution.py:530
  16.0 0.4 %collective-permute-done.10.refs_1_ = f32[5,16,256]{2,1,0:T(8,128)S(1)} collective-permute-done((f32[5,16,256]{2,1,0:T(8,128)S(1)}, f32[5,16,256]{2,1,0:T(8,128)S(1)}, u32[]{:S(2)}, u32[]{:S(2)}) %collective-permute-start.10) | collective-permute-done | bytes 81952 | tf_op jit(solution)/shard_map/ppermute | solution.py:530
  16.3 0.3 %shard_map.45._.far_ref = f32[2,2,4,16,256]{4,3,2,1,0:T(8,128)S(1)} custom-call(f32[8,2,3,16,256]{4,3,2,1,0:T(8,128)S(1)} %get-tuple-element.12.base, f32[2,2,4,16,256]{4,3,2,1,0:T(8,128)S(1)} %shard_map.44.before_ref, f32[5,16,256]{2,1,0:T(8,128)S(1)} %collective-permute-done.9.refs_0_, f32[5,16,256]{2,1,0:T(8,128)S(1)} %collective-permute-done.10.refs_1_, ...), custom_call_target="tpu_custom_call" | custom-call | flops 1 | bytes 1 | tf_op jit(solution)/shard_map/pallas_call | solution.py:541
  16.7 0.8 %shard_map.47 = f32[2,2,5,16,256]{4,3,2,1,0:T(8,128)} custom-call(f32[2,2,1,16,256]{4,3,2,1,0:T(8,128)S(1)} %shard_map.46.sent_ref, f32[2,2,4,16,256]{4,3,2,1,0:T(8,128)S(1)} %shard_map.45._.far_ref, f32[96,256]{1,0:T(8,128)S(1)} %collective-permute-done.7.message), custom_call_target="tpu_custom_call" | custom-call | flops 1 | bytes 1 | tf_op jit(solution)/shard_map/pallas_call | solution.py:541
  (17 shorter events, 0.2 us)
Async XLA Ops:
  0.0 6.4 %collective-permute-start = (f32[2,2,3,16,256]{4,3,2,1,0:T(8,128)}, f32[2,2,3,16,256]{4,3,2,1,0:T(8,128)S(1)}, u32[]{:S(2)}, u32[]{:S(2)}) collective-permute-start(f32[2,2,3,16,256]{4,3,2,1,0:T(8,128)} %base_a.1), channel_id=1, source_target_pairs={{0,4},{4,0},{8,12},{12,8},{1,5},{5,1},{9,13},{13,9},{2,6},{6,2},{1... | collective-permute-start | bytes 589832 | tf_op jit(solution)/shard_map/ppermute | solution.py:530
  0.5 8.5 %collective-permute-start.1 = (f32[2,2,3,16,256]{4,3,2,1,0:T(8,128)}, f32[2,2,3,16,256]{4,3,2,1,0:T(8,128)S(1)}, u32[]{:S(2)}, u32[]{:S(2)}) collective-permute-start(f32[2,2,3,16,256]{4,3,2,1,0:T(8,128)} %base_a.1), channel_id=1, source_target_pairs={{0,8},{4,12},{8,0},{12,4},{1,9},{5,13},{9,1},{13,5},{2,10},{6,14},... | collective-permute-start | bytes 589832 | tf_op jit(solution)/shard_map/ppermute | solution.py:527
  3.0 8.5 %collective-permute-start.5 = (f32[2,2,5,16,256]{4,3,2,1,0:T(8,128)}, f32[2,2,5,16,256]{4,3,2,1,0:T(8,128)S(1)}, u32[]{:S(2)}, u32[]{:S(2)}) collective-permute-start(f32[2,2,5,16,256]{4,3,2,1,0:T(8,128)} %q_from.1), channel_id=1, source_target_pairs={{0,4},{4,0},{8,12},{12,8},{1,5},{5,1},{9,13},{13,9},{2,6},{6,2},{1... | collective-permute-start | bytes 983048 | tf_op jit(solution)/shard_map/ppermute | solution.py:530
  4.2 5.7 %collective-permute-start.3 = (f32[24,256]{1,0:T(8,128)S(1)}, f32[24,256]{1,0:T(8,128)S(1)}, u32[]{:S(2)}, u32[]{:S(2)}) collective-permute-start(f32[24,256]{1,0:T(8,128)S(1)} %shard_map.38), channel_id=1, source_target_pairs={{0,1},{1,2},{2,3},{3,0},{4,5},{5,6},{6,7},{7,4},{8,9},{9,10},{10,1... | collective-permute-start | bytes 73736 | tf_op jit(solution)/shard_map/ppermute | solution.py:533
  5.9 4.5 %copy-start = (f32[2,2,3,16,256]{4,3,2,1,0:T(8,128)S(1)}, f32[2,2,3,16,256]{4,3,2,1,0:T(8,128)}, u32[]{:S(2)}) copy-start(f32[2,2,3,16,256]{4,3,2,1,0:T(8,128)} %base_a.1) | copy-start | bytes 589828
  5.9 8.5 %collective-permute-start.8 = (f32[2,2,4,16,256]{4,3,2,1,0:T(8,128)S(1)}, f32[2,2,4,16,256]{4,3,2,1,0:T(8,128)S(1)}, u32[]{:S(2)}, u32[]{:S(2)}) collective-permute-start(f32[2,2,4,16,256]{4,3,2,1,0:T(8,128)S(1)} %get-tuple-element.14), channel_id=1, source_target_pairs={{0,8},{4,12},{8,0},{12,4},{1,9},{5,13},{9,1},{13,5},{2,10},{6,14},... | collective-permute-start | bytes 786440 | tf_op jit(solution)/shard_map/ppermute | solution.py:527
  6.4 3.9 %collective-permute-start.4 = (f32[24,256]{1,0:T(8,128)S(1)}, f32[24,256]{1,0:T(8,128)S(1)}, u32[]{:S(2)}, u32[]{:S(2)}) collective-permute-start(f32[24,256]{1,0:T(8,128)S(1)} %shard_map.39), channel_id=1, source_target_pairs={{0,3},{1,0},{2,1},{3,2},{4,7},{5,4},{6,5},{7,6},{8,11},{9,8},{10,9... | collective-permute-start | bytes 73736 | tf_op jit(solution)/shard_map/ppermute | solution.py:533
  8.9 1.4 %collective-permute-start.2 = (f32[2,2,3,16,256]{4,3,2,1,0:T(8,128)S(1)}, f32[2,2,3,16,256]{4,3,2,1,0:T(8,128)S(1)}, u32[]{:S(2)}, u32[]{:S(2)}) collective-permute-start(f32[2,2,3,16,256]{4,3,2,1,0:T(8,128)S(1)} %collective-permute-done.1.base_c), channel_id=1, source_target_pairs={{0,4},{4,0},{8,12},{12,8},{1,5},{5,1},{9,13},{13,9},{2,6},{6,2},{1... | collective-permute-start | bytes 589832 | tf_op jit(solution)/shard_map/ppermute | solution.py:530
  10.3 1.2 %collective-permute-start.6 = (f32[48,256]{1,0:T(8,128)S(1)}, f32[48,256]{1,0:T(8,128)S(1)}, u32[]{:S(2)}, u32[]{:S(2)}) collective-permute-start(f32[48,256]{1,0:T(8,128)S(1)} %constant_dynamic-update-slice_fusion.halo_ref.halo_own), channel_id=1, source_target_pairs={{0,4},{4,0},{8,12},{12,8},{1,5},{5,1},{9,13},{13,9},{2,6},{6,2},{1... | collective-permute-start | bytes 147464 | tf_op jit(solution)/shard_map/ppermute | solution.py:530
  11.8 4.9 %collective-permute-start.7 = (f32[96,256]{1,0:T(8,128)S(1)}, f32[96,256]{1,0:T(8,128)S(1)}, u32[]{:S(2)}, u32[]{:S(2)}) collective-permute-start(f32[96,256]{1,0:T(8,128)S(1)} %shard_map.42), channel_id=1, source_target_pairs={{0,8},{4,12},{8,0},{12,4},{1,9},{5,13},{9,1},{13,5},{2,10},{6,14},... | collective-permute-start | bytes 294920 | tf_op jit(solution)/shard_map/ppermute | solution.py:527
  14.4 1.9 %collective-permute-start.11 = (f32[6,16,256]{2,1,0:T(8,128)S(1)}, f32[6,16,256]{2,1,0:T(8,128)S(1)}, u32[]{:S(2)}, u32[]{:S(2)}) collective-permute-start(f32[6,16,256]{2,1,0:T(8,128)S(1)} %slice.14), channel_id=1, source_target_pairs={{0,4},{4,0},{8,12},{12,8},{1,5},{5,1},{9,13},{13,9},{2,6},{6,2},{1... | collective-permute-start | bytes 294920 | tf_op jit(solution)/shard_map/ppermute | solution.py:530
  14.5 1.5 %collective-permute-start.9 = (f32[5,16,256]{2,1,0:T(8,128)S(1)}, f32[5,16,256]{2,1,0:T(8,128)S(1)}, u32[]{:S(2)}, u32[]{:S(2)}) collective-permute-start(f32[5,16,256]{2,1,0:T(8,128)S(1)} %get-tuple-element.16), channel_id=1, source_target_pairs={{0,4},{4,0},{8,12},{12,8},{1,5},{5,1},{9,13},{13,9},{2,6},{6,2},{1... | collective-permute-start | bytes 245768 | tf_op jit(solution)/shard_map/ppermute | solution.py:530
  15.0 1.3 %collective-permute-start.10 = (f32[5,16,256]{2,1,0:T(8,128)S(1)}, f32[5,16,256]{2,1,0:T(8,128)S(1)}, u32[]{:S(2)}, u32[]{:S(2)}) collective-permute-start(f32[5,16,256]{2,1,0:T(8,128)S(1)} %get-tuple-element.15), channel_id=1, source_target_pairs={{0,4},{4,0},{8,12},{12,8},{1,5},{5,1},{9,13},{13,9},{2,6},{6,2},{1... | collective-permute-start | bytes 245768 | tf_op jit(solution)/shard_map/ppermute | solution.py:530

commit v6 on v5

--- a/solution.py
+++ b/solution.py
@@ -176,6 +176,8 @@
 
 
 scoped_bytes = 12 * 1024 * 1024
+results_flops = 3 * 10**9
+hand_on_pieces = 3
 in_vmem = pl.BlockSpec(memory_space=pltpu.VMEM)
 anywhere = pl.BlockSpec(memory_space=pl.ANY)
 
@@ -260,9 +262,13 @@
     return kernel
 
 
-def halo(sizes, ref, at):
-    below = sizes.edge + at
-    return ref[at : at + 1, :], ref[below : below + 1, :]
+def halo(ref, sizes, harmonic, part, field):
+    at = sizes.at(harmonic, part, field)
+    return halo_rows(ref, sizes, at)
+
+
+def halo_rows(ref, sizes, at):
+    return tuple(ref[start : start + 1, :] for start in (at, sizes.edge + at))
 
 
 def slope_y(value):
@@ -288,67 +294,80 @@
     return [[base[at, part, term, rows, :] for part in (0, 1)] for term in range(3)]
 
 
-def result_kernel(sizes, base, q_own, q_core, halo_own, halo_core, out_ref):
+def chip_sources(sizes):
     me = lax.axis_index("harm")
-    targets = [lax.bitwise_xor(me, 2) * sizes.local + harmonic for harmonic in range(sizes.local)]
-    sources = [
-        (lax.bitwise_xor(me, place) * sizes.local + harmonic, q_ref, halo_ref, harmonic)
-        for place, q_ref, halo_ref in ((0, q_own, halo_own), (1, q_core, halo_core))
+    return [
+        (lax.bitwise_xor(me, place) * sizes.local + harmonic, place, harmonic)
+        for place in (0, 1)
         for harmonic in range(sizes.local)
     ]
-    first, last = sizes.sent
-    parts = (0, 1)
-    for field in range(first, last):
+
+
+def far_targets(sizes):
+    me = lax.axis_index("harm")
+    return [lax.bitwise_xor(me, 2) * sizes.local + harmonic for harmonic in range(sizes.local)]
+
+
+def block_into(sizes, base, q_own, q_core, block_ref):
+    sources = chip_sources(sizes)
+    for field in range(*sizes.sent):
         moved = []
-        for _, q_ref, halo_ref, harmonic in sources:
-            terms = [[], [], []]
-            for part in parts:
-                value = q_ref[harmonic, part, field]
-                above, below = halo(sizes, halo_ref, sizes.at(harmonic, part, field))
-                for term, what in zip(
-                    terms, (slope_x(value, above, below), slope_y(value), value), strict=True
-                ):
-                    term.append(what)
-            moved.append(terms)
+        for _, place, harmonic in sources:
+            parts = [(q_own, q_core)[place][harmonic, part, field] for part in (0, 1)]
+            moved.append(
+                [
+                    [slope_x(value, 0.0, 0.0) for value in parts],
+                    [slope_y(value) for value in parts],
+                    parts,
+                ]
+            )
         for start in range(0, sizes.width, 8):
             rows = slice(start, start + 8)
-            for harmonic, target in enumerate(targets):
+            for harmonic, target in enumerate(far_targets(sizes)):
                 sums = (None, None)
-                for terms, (source, _, _, _) in zip(moved, sources, strict=True):
+                for terms, (source, _, _) in zip(moved, sources, strict=True):
                     chosen = chosen_rows(sizes, base, target, source, rows)
                     cut = [[value[rows] for value in term] for term in terms]
                     sums = add_products(sums, chosen, cut)
-                for part in parts:
+                for part in (0, 1):
                     at = sizes.block(harmonic, part, field).start + start
-                    out_ref[at : at + 8, :] = sums[part]
-    first, last = sizes.moved
+                    block_ref[at : at + 8, :] = sums[part]
+
+
+def result_kernel(sizes, base, block_ref, halo_own, halo_core, out_ref):
+    out_ref[: sizes.block_rows, :] = block_ref[...]
+    sources = chip_sources(sizes)
     for side, row, sign in ((0, 0, -0.5), (1, sizes.width - 1, 0.5)):
         outside = [
             [
                 jnp.concatenate(
                     [
-                        halo(sizes, halo_ref, sizes.at(harmonic, part, field))[side]
-                        for field in range(first, last)
+                        halo((halo_own, halo_core)[place], sizes, harmonic, part, field)[side]
+                        for field in range(sizes.fields)
                     ],
                     axis=0,
                 )
-                for part in parts
+                for part in (0, 1)
             ]
-            for _, _, halo_ref, harmonic in sources
+            for _, place, harmonic in sources
         ]
-        for harmonic, target in enumerate(targets):
+        for harmonic, target in enumerate(far_targets(sizes)):
             real = imag = 0.0
-            for (q_real, q_imag), (source, _, _, _) in zip(outside, sources, strict=True):
+            for (q_real, q_imag), (source, _, _) in zip(outside, sources, strict=True):
                 at = lax.rem(target - source + sizes.total, sizes.total)
                 u_real = sign * base[at, 0, 0, row : row + 1, :]
                 u_imag = sign * base[at, 1, 0, row : row + 1, :]
                 real = real + u_real * q_real - u_imag * q_imag
                 imag = imag + u_real * q_imag + u_imag * q_real
-            for part, value in zip(parts, (real, imag), strict=True):
-                for field in range(first, last):
-                    at = field - first
-                    out_ref[sizes.rim(harmonic, part, field, side), :] = value[at : at + 1, :]
-    tail = sizes.block_rows + sizes.local * 2 * (last - first) * 2
+            for part, value in zip((0, 1), (real, imag), strict=True):
+                for field in range(sizes.fields):
+                    more = value[field : field + 1, :]
+                    if field < sizes.moved[1]:
+                        out_ref[sizes.rim(harmonic, part, field, side), :] = more
+                    else:
+                        at = sizes.block(harmonic, part, field).start + row
+                        out_ref[at : at + 1, :] += more
+    tail = sizes.block_rows + sizes.local * 2 * (sizes.moved[1] - sizes.moved[0]) * 2
     if tail < sizes.message_rows:
         out_ref[tail:, :] = jnp.zeros((sizes.message_rows - tail, sizes.columns), jnp.float32)
 
@@ -356,7 +375,7 @@
 def own_terms_into(sizes, q_ref, visc_ref, halo_ref, sum_ref):
     me = lax.axis_index("harm")
     center = visc_ref[...]
-    above, below = halo(sizes, halo_ref, sizes.components)
+    above, below = halo_rows(halo_ref, sizes, sizes.components)
     east = 0.5 * (center + rows_next(center, below))
     west = 0.5 * (center + rows_before(center, above))
     north = 0.5 * (center + lanes_next(center))
@@ -370,7 +389,7 @@
             terms = {}
             for field in range(sizes.fields):
                 value = q_ref[harmonic, part, field]
-                above, below = halo(sizes, halo_ref, sizes.at(harmonic, part, field))
+                above, below = halo(halo_ref, sizes, harmonic, part, field)
                 x_next, x_before = rows_next(value, below), rows_before(value, above)
                 y_next, y_before = lanes_next(value), lanes_before(value)
                 damping = (
@@ -403,7 +422,7 @@
                 value = q_ref[harmonic, part, field]
                 above = below = 0.0
                 if halo_ref is not None:
-                    above, below = halo(sizes, halo_ref, sizes.at(harmonic, part, field))
+                    above, below = halo(halo_ref, sizes, harmonic, part, field)
                 slopes_x[harmonic, part] = slope_x(value, above, below)
                 slopes_y[harmonic, part] = slope_y(value)
         for start in range(0, sizes.width, 8):
@@ -440,35 +459,38 @@
 
 
 def own_kernel(
-    sizes, base_a, base_b, base_c, base_d, q_ref, halo_ref, visc_ref, sum_ref, base, *slopes
+    sizes, base_a, base_b, base_c, base_d, q_own, q_core, halo_ref, visc_ref, sum_ref, base, block_ref,
+    *slopes,
 ):
     me = lax.axis_index("harm")
     for place, ref in enumerate((base_a, base_b, base_c, base_d)):
         for harmonic in range(sizes.local):
             base[lax.bitwise_xor(me, place) * sizes.local + harmonic] = ref[harmonic]
-    own_terms_into(sizes, q_ref, visc_ref, halo_ref, sum_ref)
+    block_into(sizes, base, q_own, q_core, block_ref)
+    own_terms_into(sizes, q_own, visc_ref, halo_ref, sum_ref)
     everything = (0, sizes.fields)
-    couple(
-        sizes, base, 0, everything, reader(sum_ref), q_ref, halo_ref, slopes, writer(sum_ref)
-    )
+    couple(sizes, base, 0, everything, reader(sum_ref), q_own, halo_ref, slopes, writer(sum_ref))
 
 
 def core_kernel(sizes, base, q_ref, halo_ref, before_ref, sum_ref, *slopes):
     everything = (0, sizes.fields)
-    couple(
-        sizes, base, 1, everything, reader(before_ref), q_ref, halo_ref, slopes, writer(sum_ref)
-    )
+    couple(sizes, base, 1, everything, reader(before_ref), q_ref, halo_ref, slopes, writer(sum_ref))
 
 
 class Pieces:
     def __init__(self, sizes, refs):
-        self.fields = sizes.moved[1]
-        self.planes = [(ref, plane) for ref in refs for plane in range(ref.shape[0])]
+        self.sizes = sizes
+        self.blocks = [
+            (ref, slice(start, start + 8)) for ref in refs for start in range(0, ref.shape[0], 8)
+        ]
 
     def __getitem__(self, at):
         harmonic, part, field, *rest = at
-        ref, plane = self.planes[(harmonic * 2 + part) * self.fields + field]
-        return ref[(plane, *rest)]
+        plane = (harmonic * 2 + part) * self.sizes.moved[1] + field
+        count = self.sizes.width // 8
+        chosen = range(rest[0].start // 8, rest[0].stop // 8) if rest else range(count)
+        blocks = [self.blocks[plane * count + block] for block in chosen]
+        return jnp.concatenate([ref[rows, :] for ref, rows in blocks], axis=0)
 
 
 def chip_kernel(sizes, base, q_ref, before_ref, sum_ref, *slopes):
@@ -576,15 +598,19 @@
     halo_core = to_core(halo_own)
     held_core = to_core(perturbation)
     base_diag = to_core(base_chip)
-    own_sum, base = call(
+    own_sum, base, block = call(
         own_kernel,
-        (base_flow, base_core, base_chip, base_diag, held, halo_own, visc),
-        [array(*perturbation.shape), array(sizes.total, *base_flow.shape[1:])],
+        (base_flow, base_core, base_chip, base_diag, held, held_core, halo_own, visc),
+        [
+            array(*perturbation.shape),
+            array(sizes.total, *base_flow.shape[1:]),
+            array(sizes.block_rows, sizes.columns),
+        ],
         slopes,
     )
     message = call(
         result_kernel,
-        (base, held, held_core, halo_own, halo_core),
+        (base, block, halo_own, halo_core),
         [array(sizes.message_rows, sizes.columns)],
     )[0]
     results = to_chip(message)
@@ -600,8 +626,8 @@
         flops=1,
         aliases={0: 0},
     )
-    flat = moved_here.reshape(-1, sizes.width, sizes.columns)
-    starts = [len(flat) * place // 3 for place in range(3 + 1)]
+    flat = moved_here.reshape(-1, sizes.columns)
+    starts = [len(flat) // 8 * place // hand_on_pieces * 8 for place in range(hand_on_pieces + 1)]
     pieces = [to_core(flat[begin:end]) for begin, end in zip(starts, starts[1:])]
     far_sum = call(
         chip_kernel,
@@ -619,7 +645,7 @@
         sent_kernel,
         (near_sum, results, far_sum),
         [array(*sizes.shape(sizes.local, sizes.sent))],
-        flops=3*10**9,
+        flops=results_flops,
         in_specs=[in_vmem, in_vmem, anywhere],
     )[0]
     return call(

time: 17.6 us -> 17.5 us (level)
  waiting for transfers between devices: 3.68 us -> 3.41 us
    ppermute x7, waiting for transfers between devices: 1.37 us -> 1.15 us  [to_core(): return lax.ppermute(value, 'harm', [(i, i ^ 1) for i in range(groups)])]
    ppermute x3, starting transfers between devices: 4.66 us -> 4.84 us  [to_chip(): return lax.ppermute(value, 'harm', [(i, i ^ 2) for i in range(groups)])]
  transfers between devices with their start and end apart: 12 -> 12, of which waited for: 9 -> 7; matrix products, arithmetic and copies ran while one was open for 0% -> 0% of each run, Pallas kernels for 18% -> 18%
where the time goes in v6:
time: 17.5 us; the launch traced here: 17.4 us
  starting transfers between devices  9.99 us (57%)
  Pallas kernels  3.88 us (22%)
  waiting for transfers between devices  3.41 us (19%)
    ppermute x3, starting transfers between devices, to_chip(): return lax.ppermute(value, 'harm', [(i, i ^ 2) for i in range(groups)])  4.84 us
    pallas_call x11, Pallas kernels, call(): pl.pallas_call(functools.partial(kernel, sizes), in_specs=in_specs or [in...  3.88 us
    ppermute x2, starting transfers between devices, along_tile(): lax.ppermute(value, 'tile', [(i, (i + step) % tiles) for i in range(tiles)])  3.8 us
    ppermute x7, starting transfers between devices, to_core(): return lax.ppermute(value, 'harm', [(i, i ^ 1) for i in range(groups)])  1.36 us
    ppermute x2, waiting for transfers between devices, along_tile(): lax.ppermute(value, 'tile', [(i, (i + step) % tiles) for i in range(tiles)])  1.33 us
    ppermute x7, waiting for transfers between devices, to_core(): return lax.ppermute(value, 'harm', [(i, i ^ 1) for i in range(groups)])  1.15 us
    ppermute x3, waiting for transfers between devices, to_chip(): return lax.ppermute(value, 'harm', [(i, i ^ 2) for i in range(groups)])  0.92 us
  transfers between devices with their start and end apart: 12, of which 7 were waited for; matrix products, arithmetic and copies ran while one was open for 0% of the time, Pallas kernels for 18%

profile of v6, /device:TPU:0, one launch (start us, length us, event | category | flops | bytes accessed | tf_op | source)
XLA Modules:
  0.0 17.4 jit_solution(9426010841577569592)
XLA Ops:
  0.0 0.5 %collective-permute-start = (f32[2,2,3,16,256]{4,3,2,1,0:T(8,128)}, f32[2,2,3,16,256]{4,3,2,1,0:T(8,128)S(1)}, u32[]{:S(2)}, u32[]{:S(2)}) collective-permute-start(f32[2,2,3,16,256]{4,3,2,1,0:T(8,128)} %base_a.1), channel_id=1, source_target_pairs={{0,4},{4,0},{8,12},{12,8},{1,5},{5,1},{9,13},{13,9},{2,6},{6,2},{1... | collective-permute-start | bytes 589832 | tf_op jit(solution)/shard_map/ppermute | solution.py:552
  0.5 2.5 %collective-permute-start.1 = (f32[2,2,3,16,256]{4,3,2,1,0:T(8,128)}, f32[2,2,3,16,256]{4,3,2,1,0:T(8,128)S(1)}, u32[]{:S(2)}, u32[]{:S(2)}) collective-permute-start(f32[2,2,3,16,256]{4,3,2,1,0:T(8,128)} %base_a.1), channel_id=1, source_target_pairs={{0,8},{4,12},{8,0},{12,4},{1,9},{5,13},{9,1},{13,5},{2,10},{6,14},... | collective-permute-start | bytes 589832 | tf_op jit(solution)/shard_map/ppermute | solution.py:549
  3.0 0.2 %collective-permute-start.3 = (f32[2,2,5,16,256]{4,3,2,1,0:T(8,128)}, f32[2,2,5,16,256]{4,3,2,1,0:T(8,128)S(1)}, u32[]{:S(2)}, u32[]{:S(2)}) collective-permute-start(f32[2,2,5,16,256]{4,3,2,1,0:T(8,128)} %q_from.1), channel_id=1, source_target_pairs={{0,4},{4,0},{8,12},{12,8},{1,5},{5,1},{9,13},{13,9},{2,6},{6,2},{1... | collective-permute-start | bytes 983048 | tf_op jit(solution)/shard_map/ppermute | solution.py:552
  3.2 1.0 %shard_map.37 = (f32[2,2,5,16,256]{4,3,2,1,0:T(8,128)S(1)}, f32[16,256]{1,0:T(8,128)S(1)}, f32[2,2,4,16,256]{4,3,2,1,0:T(8,128)S(1)}) custom-call(f32[2,2,5,16,256]{4,3,2,1,0:T(8,128)} %q_from.1, f32[16,256]{1,0:T(8,128)} %visc_from.1), custom_call_target="tpu_custom_call" | custom-call | flops 1 | bytes 1 | tf_op jit(solution)/shard_map/pallas_call | solution.py:563
  4.2 1.6 %collective-permute-start.4 = (f32[24,256]{1,0:T(8,128)S(1)}, f32[24,256]{1,0:T(8,128)S(1)}, u32[]{:S(2)}, u32[]{:S(2)}) collective-permute-start(f32[24,256]{1,0:T(8,128)S(1)} %shard_map.38), channel_id=1, source_target_pairs={{0,1},{1,2},{2,3},{3,0},{4,5},{5,6},{6,7},{7,4},{8,9},{9,10},{10,1... | collective-permute-start | bytes 73736 | tf_op jit(solution)/shard_map/ppermute | solution.py:555
  5.9 0.5 %collective-permute-start.8 = (f32[2,2,4,16,256]{4,3,2,1,0:T(8,128)S(1)}, f32[2,2,4,16,256]{4,3,2,1,0:T(8,128)S(1)}, u32[]{:S(2)}, u32[]{:S(2)}) collective-permute-start(f32[2,2,4,16,256]{4,3,2,1,0:T(8,128)S(1)} %get-tuple-element.16), channel_id=1, source_target_pairs={{0,8},{4,12},{8,0},{12,4},{1,9},{5,13},{9,1},{13,5},{2,10},{6,14},... | collective-permute-start | bytes 786440 | tf_op jit(solution)/shard_map/ppermute | solution.py:549
  6.4 2.2 %collective-permute-start.5 = (f32[24,256]{1,0:T(8,128)S(1)}, f32[24,256]{1,0:T(8,128)S(1)}, u32[]{:S(2)}, u32[]{:S(2)}) collective-permute-start(f32[24,256]{1,0:T(8,128)S(1)} %shard_map.39), channel_id=1, source_target_pairs={{0,3},{1,0},{2,1},{3,2},{4,7},{5,4},{6,5},{7,6},{8,11},{9,8},{10,9... | collective-permute-start | bytes 73736 | tf_op jit(solution)/shard_map/ppermute | solution.py:555
  8.6 0.4 %collective-permute-done.1.base_c = f32[2,2,3,16,256]{4,3,2,1,0:T(8,128)S(1)} collective-permute-done((f32[2,2,3,16,256]{4,3,2,1,0:T(8,128)}, f32[2,2,3,16,256]{4,3,2,1,0:T(8,128)S(1)}, u32[]{:S(2)}, u32[]{:S(2)}) %collective-permute-start.1) | collective-permute-done | bytes 196640 | tf_op jit(solution)/shard_map/ppermute | solution.py:549
  8.9 1.0 %collective-permute-done.4 = f32[24,256]{1,0:T(8,128)S(1)} collective-permute-done((f32[24,256]{1,0:T(8,128)S(1)}, f32[24,256]{1,0:T(8,128)S(1)}, u32[]{:S(2)}, u32[]{:S(2)}) %collective-permute-start.4) | collective-permute-done | bytes 24608 | tf_op jit(solution)/shard_map/ppermute | solution.py:555
  9.9 0.3 %collective-permute-done.5 = f32[24,256]{1,0:T(8,128)S(1)} collective-permute-done((f32[24,256]{1,0:T(8,128)S(1)}, f32[24,256]{1,0:T(8,128)S(1)}, u32[]{:S(2)}, u32[]{:S(2)}) %collective-permute-start.5) | collective-permute-done | bytes 24608 | tf_op jit(solution)/shard_map/ppermute | solution.py:555
  10.3 0.1 collective-permute-done.2.base_d
  10.4 0.9 %shard_map.40 = (f32[2,2,5,16,256]{4,3,2,1,0:T(8,128)S(1)}, f32[8,2,3,16,256]{4,3,2,1,0:T(8,128)S(1)}, f32[64,256]{1,0:T(8,128)S(1)}) custom-call(f32[2,2,3,16,256]{4,3,2,1,0:T(8,128)S(1)} %copy-done, f32[2,2,3,16,256]{4,3,2,1,0:T(8,128)S(1)} %collective-permute-done.refs_0_.base_b, f32[2,2,3,16,256]{4,3,2,1,0:T(8,128)S(1)} %collective-permute-done.1.base_c, ...), custom_call_target="tpu_custom_call" | custom-call | flops 1 | bytes 1 | tf_op jit(solution)/shard_map/pallas_call | solution.py:563
  11.3 0.2 %collective-permute-done.6.halo_ref.halo_core = f32[48,256]{1,0:T(8,128)S(1)} collective-permute-done((f32[48,256]{1,0:T(8,128)S(1)}, f32[48,256]{1,0:T(8,128)S(1)}, u32[]{:S(2)}, u32[]{:S(2)}) %collective-permute-start.6) | collective-permute-done | bytes 49184 | tf_op jit(solution)/shard_map/ppermute | solution.py:552
  11.5 0.1 shard_map.42
  11.6 1.8 %collective-permute-start.7 = (f32[96,256]{1,0:T(8,128)S(1)}, f32[96,256]{1,0:T(8,128)S(1)}, u32[]{:S(2)}, u32[]{:S(2)}) collective-permute-start(f32[96,256]{1,0:T(8,128)S(1)} %shard_map.42), channel_id=1, source_target_pairs={{0,8},{4,12},{8,0},{12,4},{1,9},{5,13},{9,1},{13,5},{2,10},{6,14},... | collective-permute-start | bytes 294920 | tf_op jit(solution)/shard_map/ppermute | solution.py:549
  13.4 0.4 %shard_map.41.after.before_ref.near_ref = f32[2,2,5,16,256]{4,3,2,1,0:T(8,128)S(1)} custom-call(f32[8,2,3,16,256]{4,3,2,1,0:T(8,128)S(1)} %get-tuple-element.13.base, f32[2,2,5,16,256]{4,3,2,1,0:T(8,128)S(1)} %collective-permute-done.3.q_core.q_ref, f32[48,256]{1,0:T(8,128)S(1)} %collective-permute-done.6.halo_ref.halo_core, ...), custom_call_target="tpu_custom_call" | custom-call | flops 1 | bytes 1 | tf_op jit(solution)/shard_map/pallas_call | solution.py:563
  13.8 0.5 %collective-permute-done.8.values = f32[2,2,4,16,256]{4,3,2,1,0:T(8,128)S(1)} collective-permute-done((f32[2,2,4,16,256]{4,3,2,1,0:T(8,128)S(1)}, f32[2,2,4,16,256]{4,3,2,1,0:T(8,128)S(1)}, u32[]{:S(2)}, u32[]{:S(2)}) %collective-permute-start.8) | collective-permute-done | bytes 262176 | tf_op jit(solution)/shard_map/ppermute | solution.py:549
  14.4 0.1 collective-permute-start.10
  14.5 0.5 %collective-permute-start.11 = (f32[88,256]{1,0:T(8,128)S(1)}, f32[88,256]{1,0:T(8,128)S(1)}, u32[]{:S(2)}, u32[]{:S(2)}) collective-permute-start(f32[88,256]{1,0:T(8,128)S(1)} %get-tuple-element.17), channel_id=1, source_target_pairs={{0,4},{4,0},{8,12},{12,8},{1,5},{5,1},{9,13},{13,9},{2,6},{6,2},{1... | collective-permute-start | bytes 270344 | tf_op jit(solution)/shard_map/ppermute | solution.py:552
  15.0 0.1 collective-permute-start.9
  15.1 0.3 %shard_map.44.before_ref = f32[2,2,4,16,256]{4,3,2,1,0:T(8,128)S(1)} custom-call(f32[8,2,3,16,256]{4,3,2,1,0:T(8,128)S(1)} %get-tuple-element.13.base, f32[2,2,4,16,256]{4,3,2,1,0:T(8,128)S(1)} %shard_map.43.q_ref, f32[2,2,5,16,256]{4,3,2,1,0:T(8,128)S(1)} %shard_map.41.after.before_ref.near_ref), custom_call_target="tpu_custom_call" | custom-call | flops 1 | bytes 1 | tf_op jit(solution)/shard_map/pallas_call | solution.py:563
  15.4 0.8 %collective-permute-done.9.refs_0_ = f32[80,256]{1,0:T(8,128)S(1)} collective-permute-done((f32[80,256]{1,0:T(8,128)S(1)}, f32[80,256]{1,0:T(8,128)S(1)}, u32[]{:S(2)}, u32[]{:S(2)}) %collective-permute-start.9) | collective-permute-done | bytes 81952 | tf_op jit(solution)/shard_map/ppermute | solution.py:552
  16.3 0.3 %shard_map.45._.far_ref = f32[2,2,4,16,256]{4,3,2,1,0:T(8,128)S(1)} custom-call(f32[8,2,3,16,256]{4,3,2,1,0:T(8,128)S(1)} %get-tuple-element.13.base, f32[2,2,4,16,256]{4,3,2,1,0:T(8,128)S(1)} %shard_map.44.before_ref, f32[80,256]{1,0:T(8,128)S(1)} %collective-permute-done.9.refs_0_, f32[88,256]{1,0:T(8,128)S(1)} %collective-permute-done.10.refs_1_, ...), custom_call_target="tpu_custom_call" | custom-call | flops 1 | bytes 1 | tf_op jit(solution)/shard_map/pallas_call | solution.py:563
  16.6 0.8 %shard_map.47 = f32[2,2,5,16,256]{4,3,2,1,0:T(8,128)} custom-call(f32[2,2,1,16,256]{4,3,2,1,0:T(8,128)S(1)} %shard_map.46.sent_ref, f32[2,2,4,16,256]{4,3,2,1,0:T(8,128)S(1)} %shard_map.45._.far_ref, f32[96,256]{1,0:T(8,128)S(1)} %collective-permute-done.7.message), custom_call_target="tpu_custom_call" | custom-call | flops 1 | bytes 1 | tf_op jit(solution)/shard_map/pallas_call | solution.py:563
  (17 shorter events, 0.1 us)
Async XLA Ops:
  0.0 6.4 %collective-permute-start = (f32[2,2,3,16,256]{4,3,2,1,0:T(8,128)}, f32[2,2,3,16,256]{4,3,2,1,0:T(8,128)S(1)}, u32[]{:S(2)}, u32[]{:S(2)}) collective-permute-start(f32[2,2,3,16,256]{4,3,2,1,0:T(8,128)} %base_a.1), channel_id=1, source_target_pairs={{0,4},{4,0},{8,12},{12,8},{1,5},{5,1},{9,13},{13,9},{2,6},{6,2},{1... | collective-permute-start | bytes 589832 | tf_op jit(solution)/shard_map/ppermute | solution.py:552
  0.5 8.5 %collective-permute-start.1 = (f32[2,2,3,16,256]{4,3,2,1,0:T(8,128)}, f32[2,2,3,16,256]{4,3,2,1,0:T(8,128)S(1)}, u32[]{:S(2)}, u32[]{:S(2)}) collective-permute-start(f32[2,2,3,16,256]{4,3,2,1,0:T(8,128)} %base_a.1), channel_id=1, source_target_pairs={{0,8},{4,12},{8,0},{12,4},{1,9},{5,13},{9,1},{13,5},{2,10},{6,14},... | collective-permute-start | bytes 589832 | tf_op jit(solution)/shard_map/ppermute | solution.py:549
  3.0 7.3 %collective-permute-start.3 = (f32[2,2,5,16,256]{4,3,2,1,0:T(8,128)}, f32[2,2,5,16,256]{4,3,2,1,0:T(8,128)S(1)}, u32[]{:S(2)}, u32[]{:S(2)}) collective-permute-start(f32[2,2,5,16,256]{4,3,2,1,0:T(8,128)} %q_from.1), channel_id=1, source_target_pairs={{0,4},{4,0},{8,12},{12,8},{1,5},{5,1},{9,13},{13,9},{2,6},{6,2},{1... | collective-permute-start | bytes 983048 | tf_op jit(solution)/shard_map/ppermute | solution.py:552
  4.2 5.7 %collective-permute-start.4 = (f32[24,256]{1,0:T(8,128)S(1)}, f32[24,256]{1,0:T(8,128)S(1)}, u32[]{:S(2)}, u32[]{:S(2)}) collective-permute-start(f32[24,256]{1,0:T(8,128)S(1)} %shard_map.38), channel_id=1, source_target_pairs={{0,1},{1,2},{2,3},{3,0},{4,5},{5,6},{6,7},{7,4},{8,9},{9,10},{10,1... | collective-permute-start | bytes 73736 | tf_op jit(solution)/shard_map/ppermute | solution.py:555
  5.9 4.5 %copy-start = (f32[2,2,3,16,256]{4,3,2,1,0:T(8,128)S(1)}, f32[2,2,3,16,256]{4,3,2,1,0:T(8,128)}, u32[]{:S(2)}) copy-start(f32[2,2,3,16,256]{4,3,2,1,0:T(8,128)} %base_a.1) | copy-start | bytes 589828
  5.9 8.5 %collective-permute-start.8 = (f32[2,2,4,16,256]{4,3,2,1,0:T(8,128)S(1)}, f32[2,2,4,16,256]{4,3,2,1,0:T(8,128)S(1)}, u32[]{:S(2)}, u32[]{:S(2)}) collective-permute-start(f32[2,2,4,16,256]{4,3,2,1,0:T(8,128)S(1)} %get-tuple-element.16), channel_id=1, source_target_pairs={{0,8},{4,12},{8,0},{12,4},{1,9},{5,13},{9,1},{13,5},{2,10},{6,14},... | collective-permute-start | bytes 786440 | tf_op jit(solution)/shard_map/ppermute | solution.py:549
  6.4 3.9 %collective-permute-start.5 = (f32[24,256]{1,0:T(8,128)S(1)}, f32[24,256]{1,0:T(8,128)S(1)}, u32[]{:S(2)}, u32[]{:S(2)}) collective-permute-start(f32[24,256]{1,0:T(8,128)S(1)} %shard_map.39), channel_id=1, source_target_pairs={{0,3},{1,0},{2,1},{3,2},{4,7},{5,4},{6,5},{7,6},{8,11},{9,8},{10,9... | collective-permute-start | bytes 73736 | tf_op jit(solution)/shard_map/ppermute | solution.py:555
  8.9 1.4 %collective-permute-start.2 = (f32[2,2,3,16,256]{4,3,2,1,0:T(8,128)S(1)}, f32[2,2,3,16,256]{4,3,2,1,0:T(8,128)S(1)}, u32[]{:S(2)}, u32[]{:S(2)}) collective-permute-start(f32[2,2,3,16,256]{4,3,2,1,0:T(8,128)S(1)} %collective-permute-done.1.base_c), channel_id=1, source_target_pairs={{0,4},{4,0},{8,12},{12,8},{1,5},{5,1},{9,13},{13,9},{2,6},{6,2},{1... | collective-permute-start | bytes 589832 | tf_op jit(solution)/shard_map/ppermute | solution.py:552
  10.3 1.2 %collective-permute-start.6 = (f32[48,256]{1,0:T(8,128)S(1)}, f32[48,256]{1,0:T(8,128)S(1)}, u32[]{:S(2)}, u32[]{:S(2)}) collective-permute-start(f32[48,256]{1,0:T(8,128)S(1)} %constant_dynamic-update-slice_fusion.halo_ref.halo_own), channel_id=1, source_target_pairs={{0,4},{4,0},{8,12},{12,8},{1,5},{5,1},{9,13},{13,9},{2,6},{6,2},{1... | collective-permute-start | bytes 147464 | tf_op jit(solution)/shard_map/ppermute | solution.py:552
  11.6 5.0 %collective-permute-start.7 = (f32[96,256]{1,0:T(8,128)S(1)}, f32[96,256]{1,0:T(8,128)S(1)}, u32[]{:S(2)}, u32[]{:S(2)}) collective-permute-start(f32[96,256]{1,0:T(8,128)S(1)} %shard_map.42), channel_id=1, source_target_pairs={{0,8},{4,12},{8,0},{12,4},{1,9},{5,13},{9,1},{13,5},{2,10},{6,14},... | collective-permute-start | bytes 294920 | tf_op jit(solution)/shard_map/ppermute | solution.py:549
  14.4 1.9 %collective-permute-start.10 = (f32[88,256]{1,0:T(8,128)S(1)}, f32[88,256]{1,0:T(8,128)S(1)}, u32[]{:S(2)}, u32[]{:S(2)}) collective-permute-start(f32[88,256]{1,0:T(8,128)S(1)} %get-tuple-element.18), channel_id=1, source_target_pairs={{0,4},{4,0},{8,12},{12,8},{1,5},{5,1},{9,13},{13,9},{2,6},{6,2},{1... | collective-permute-start | bytes 270344 | tf_op jit(solution)/shard_map/ppermute | solution.py:552
  14.5 1.8 %collective-permute-start.11 = (f32[88,256]{1,0:T(8,128)S(1)}, f32[88,256]{1,0:T(8,128)S(1)}, u32[]{:S(2)}, u32[]{:S(2)}) collective-permute-start(f32[88,256]{1,0:T(8,128)S(1)} %get-tuple-element.17), channel_id=1, source_target_pairs={{0,4},{4,0},{8,12},{12,8},{1,5},{5,1},{9,13},{13,9},{2,6},{6,2},{1... | collective-permute-start | bytes 270344 | tf_op jit(solution)/shard_map/ppermute | solution.py:552
  15.0 1.3 %collective-permute-start.9 = (f32[80,256]{1,0:T(8,128)S(1)}, f32[80,256]{1,0:T(8,128)S(1)}, u32[]{:S(2)}, u32[]{:S(2)}) collective-permute-start(f32[80,256]{1,0:T(8,128)S(1)} %slice.12), channel_id=1, source_target_pairs={{0,4},{4,0},{8,12},{12,8},{1,5},{5,1},{9,13},{13,9},{2,6},{6,2},{1... | collective-permute-start | bytes 245768 | tf_op jit(solution)/shard_map/ppermute | solution.py:552

commit v7 on v6

--- a/solution.py
+++ b/solution.py
@@ -177,6 +177,7 @@
 
 scoped_bytes = 12 * 1024 * 1024
 results_flops = 3 * 10**9
+fetch_flops = 10**9
 hand_on_pieces = 3
 in_vmem = pl.BlockSpec(memory_space=pltpu.VMEM)
 anywhere = pl.BlockSpec(memory_space=pl.ANY)
@@ -236,30 +237,32 @@
                     yield harmonic, part, field
 
 
-def fetch_kernel(sizes, q_from, visc_from, q_ref, visc_ref, moved_ref, q_sem, visc_sem):
-    copies = (
-        pltpu.make_async_copy(q_from, q_ref, q_sem),
-        pltpu.make_async_copy(visc_from, visc_ref, visc_sem),
-    )
-    for copy in copies:
-        copy.start()
-    for copy in copies:
-        copy.wait()
-    moved_ref[...] = q_ref[:, :, sizes.moved[0] : sizes.moved[1]]
-
-
-def edge_kernel(row):
-    def kernel(sizes, q_ref, visc_ref, *refs):
-        edge_ref = refs[-1]
-        rows = slice(row, row + 1) if row >= 0 else slice(sizes.width - 1, sizes.width)
-        for harmonic, part, field in sizes.each():
-            at = sizes.at(harmonic, part, field)
-            edge_ref[at : at + 1, :] = q_ref[harmonic, part, field, rows, :]
-        at = sizes.components
-        edge_ref[at : at + 1, :] = visc_ref[rows, :]
-        edge_ref[at + 1 :, :] = jnp.zeros((sizes.edge - at - 1, sizes.columns), jnp.float32)
-
-    return kernel
+def edge_rows(sizes, q_ref, visc_ref, row, edge_ref):
+    rows = slice(row, row + 1)
+    for harmonic, part, field in sizes.each():
+        at = sizes.at(harmonic, part, field)
+        edge_ref[at : at + 1, :] = q_ref[harmonic, part, field, rows, :]
+    at = sizes.components
+    edge_ref[at : at + 1, :] = visc_ref[rows, :]
+    edge_ref[at + 1 :, :] = jnp.zeros((sizes.edge - at - 1, sizes.columns), jnp.float32)
+
+
+def visc_kernel(sizes, visc_from, visc_ref, sem):
+    copy = pltpu.make_async_copy(visc_from, visc_ref, sem)
+    copy.start()
+    copy.wait()
+
+
+def up_kernel(sizes, q_ref, visc_ref, edge_ref):
+    edge_rows(sizes, q_ref, visc_ref, sizes.width - 1, edge_ref)
+
+
+def down_kernel(sizes, q_ref, visc_ref, _, edge_ref):
+    edge_rows(sizes, q_ref, visc_ref, 0, edge_ref)
+
+
+def moved_kernel(sizes, q_ref, moved_ref):
+    moved_ref[...] = q_ref[:, :, slice(*sizes.moved)]
 
 
 def halo(ref, sizes, harmonic, part, field):
@@ -458,23 +461,21 @@
     return store
 
 
-def own_kernel(
-    sizes, base_a, base_b, base_c, base_d, q_own, q_core, halo_ref, visc_ref, sum_ref, base, block_ref,
-    *slopes,
-):
+def block_kernel(sizes, base_a, base_b, base_c, base_d, q_own, q_core, base, block_ref):
     me = lax.axis_index("harm")
     for place, ref in enumerate((base_a, base_b, base_c, base_d)):
         for harmonic in range(sizes.local):
             base[lax.bitwise_xor(me, place) * sizes.local + harmonic] = ref[harmonic]
     block_into(sizes, base, q_own, q_core, block_ref)
-    own_terms_into(sizes, q_own, visc_ref, halo_ref, sum_ref)
+
+
+def near_kernel(sizes, base, q_own, q_core, halo_own, halo_core, visc_ref, sum_ref, *slopes):
+    own_terms_into(sizes, q_own, visc_ref, halo_own, sum_ref)
     everything = (0, sizes.fields)
-    couple(sizes, base, 0, everything, reader(sum_ref), q_own, halo_ref, slopes, writer(sum_ref))
-
-
-def core_kernel(sizes, base, q_ref, halo_ref, before_ref, sum_ref, *slopes):
-    everything = (0, sizes.fields)
-    couple(sizes, base, 1, everything, reader(before_ref), q_ref, halo_ref, slopes, writer(sum_ref))
+    for place, q_ref, halo_ref in ((0, q_own, halo_own), (1, q_core, halo_core)):
+        couple(
+            sizes, base, place, everything, reader(sum_ref), q_ref, halo_ref, slopes, writer(sum_ref)
+        )
 
 
 class Pieces:
@@ -575,38 +576,32 @@
     edges = array(sizes.edge, sizes.columns)
 
     base_chip = to_chip(base_flow)
-    held, visc, moved = call(
-        fetch_kernel,
-        [pltpu.with_memory_space_constraint(x, pltpu.HBM) for x in (perturbation, viscosity)],
-        [
-            array(*perturbation.shape),
-            array(*viscosity.shape),
-            array(*sizes.shape(sizes.local, sizes.moved)),
-        ],
-        [pltpu.SemaphoreType.DMA] * 2,
-        [anywhere] * 2,
-    )
-    up = call(edge_kernel(-1), (held, visc), [edges])[0]
+    held = perturbation
+    visc = call(
+        visc_kernel,
+        [pltpu.with_memory_space_constraint(viscosity, pltpu.HBM)],
+        [array(*viscosity.shape)],
+        [pltpu.SemaphoreType.DMA],
+        [anywhere],
+        flops=fetch_flops,
+    )[0]
+    up = call(up_kernel, (held, visc), [edges])[0]
     base_core = to_core(base_flow)
     above = along_tile(up, 1)
+    moved = call(moved_kernel, (held,), [array(*sizes.shape(sizes.local, sizes.moved))])[0]
     moved_chip = to_chip(moved)
     down = call(
-        edge_kernel(0), (held, visc, base_core), [edges], in_specs=[in_vmem] * 2 + [anywhere]
+        down_kernel, (held, visc, base_core), [edges], in_specs=[in_vmem] * 2 + [anywhere]
     )[0]
     below = along_tile(down, -1)
     halo_own = jnp.concatenate([above, below], axis=0)
     halo_core = to_core(halo_own)
     held_core = to_core(perturbation)
     base_diag = to_core(base_chip)
-    own_sum, base, block = call(
-        own_kernel,
-        (base_flow, base_core, base_chip, base_diag, held, held_core, halo_own, visc),
-        [
-            array(*perturbation.shape),
-            array(sizes.total, *base_flow.shape[1:]),
-            array(sizes.block_rows, sizes.columns),
-        ],
-        slopes,
+    base, block = call(
+        block_kernel,
+        (base_flow, base_core, base_chip, base_diag, held, held_core),
+        [array(sizes.total, *base_flow.shape[1:]), array(sizes.block_rows, sizes.columns)],
     )
     message = call(
         result_kernel,
@@ -615,7 +610,10 @@
     )[0]
     results = to_chip(message)
     near_sum = call(
-        core_kernel, (base, held_core, halo_core, own_sum), [array(*perturbation.shape)], slopes
+        near_kernel,
+        (base, held, held_core, halo_own, halo_core, visc),
+        [array(*perturbation.shape)],
+        slopes,
     )[0]
     moved_here = call(
         pass_kernel,

time: 17.5 us -> 17.7 us (1.011)
  waiting for transfers between devices: 3.41 us -> 3.92 us
  Pallas kernels: 3.88 us -> 3.62 us
  starting transfers between devices: 9.99 us -> 9.76 us
    ppermute x7, waiting for transfers between devices: 1.15 us -> 1.85 us  [to_core(): return lax.ppermute(value, 'harm', [(i, i ^ 1) for i in range(groups)])]
    pallas_call x11 -> x12, Pallas kernels: 3.88 us -> 3.62 us  [call(): pl.pallas_call(functools.partial(kernel, sizes), in_specs=in_specs or [in...]
    ppermute x2, waiting for transfers between devices: 1.33 us -> 1.1 us  [along_tile(): lax.ppermute(value, 'tile', [(i, (i + step) % tiles) for i in range(tiles)])]
  transfers between devices with their start and end apart: 12 -> 12, of which waited for: 7 -> 7; matrix products, arithmetic and copies ran while one was open for 0% -> 0% of each run, Pallas kernels for 18% -> 16%
where the time goes in v7:
time: 17.7 us; the launch traced here: 17.4 us
  starting transfers between devices  9.76 us (55%)
  waiting for transfers between devices  3.92 us (22%)
  Pallas kernels  3.62 us (20%)
    ppermute x3, starting transfers between devices, to_chip(): return lax.ppermute(value, 'harm', [(i, i ^ 2) for i in range(groups)])  4.73 us
    ppermute x2, starting transfers between devices, along_tile(): lax.ppermute(value, 'tile', [(i, (i + step) % tiles) for i in range(tiles)])  3.73 us
    pallas_call x12, Pallas kernels, call(): pl.pallas_call(functools.partial(kernel, sizes), in_specs=in_specs or [in...  3.62 us
    ppermute x7, waiting for transfers between devices, to_core(): return lax.ppermute(value, 'harm', [(i, i ^ 1) for i in range(groups)])  1.85 us
    ppermute x7, starting transfers between devices, to_core(): return lax.ppermute(value, 'harm', [(i, i ^ 1) for i in range(groups)])  1.3 us
    ppermute x2, waiting for transfers between devices, along_tile(): lax.ppermute(value, 'tile', [(i, (i + step) % tiles) for i in range(tiles)])  1.1 us
    ppermute x3, waiting for transfers between devices, to_chip(): return lax.ppermute(value, 'harm', [(i, i ^ 2) for i in range(groups)])  0.97 us
  transfers between devices with their start and end apart: 12, of which 7 were waited for; matrix products, arithmetic and copies ran while one was open for 0% of the time, Pallas kernels for 16%

profile of v7, /device:TPU:0, one launch (start us, length us, event | category | flops | bytes accessed | tf_op | source)
XLA Modules:
  0.0 17.4 jit_solution(17187116331817514194)
XLA Ops:
  0.0 0.5 %collective-permute-start = (f32[2,2,3,16,256]{4,3,2,1,0:T(8,128)}, f32[2,2,3,16,256]{4,3,2,1,0:T(8,128)S(1)}, u32[]{:S(2)}, u32[]{:S(2)}) collective-permute-start(f32[2,2,3,16,256]{4,3,2,1,0:T(8,128)} %base_a.1), channel_id=1, source_target_pairs={{0,4},{4,0},{8,12},{12,8},{1,5},{5,1},{9,13},{13,9},{2,6},{6,2},{1... | collective-permute-start | bytes 589832 | tf_op jit(solution)/shard_map/ppermute | solution.py:553
  0.5 2.6 %collective-permute-start.1 = (f32[2,2,3,16,256]{4,3,2,1,0:T(8,128)}, f32[2,2,3,16,256]{4,3,2,1,0:T(8,128)S(1)}, u32[]{:S(2)}, u32[]{:S(2)}) collective-permute-start(f32[2,2,3,16,256]{4,3,2,1,0:T(8,128)} %base_a.1), channel_id=1, source_target_pairs={{0,8},{4,12},{8,0},{12,4},{1,9},{5,13},{9,1},{13,5},{2,10},{6,14},... | collective-permute-start | bytes 589832 | tf_op jit(solution)/shard_map/ppermute | solution.py:550
  3.0 0.2 collective-permute-start.3
  3.2 0.7 %shard_map.38.visc_ref = f32[16,256]{1,0:T(8,128)S(1)} custom-call(f32[16,256]{1,0:T(8,128)} %visc_from.1), custom_call_target="tpu_custom_call" | custom-call | flops 1000000000 | bytes 1 | tf_op jit(solution)/shard_map/pallas_call | solution.py:564
  4.0 1.6 %collective-permute-start.4 = (f32[24,256]{1,0:T(8,128)S(1)}, f32[24,256]{1,0:T(8,128)S(1)}, u32[]{:S(2)}, u32[]{:S(2)}) collective-permute-start(f32[24,256]{1,0:T(8,128)S(1)} %shard_map.39), channel_id=1, source_target_pairs={{0,1},{1,2},{2,3},{3,0},{4,5},{5,6},{6,7},{7,4},{8,9},{9,10},{10,1... | collective-permute-start | bytes 73736 | tf_op jit(solution)/shard_map/ppermute | solution.py:556
  5.6 0.6 %collective-permute-start.8 = (f32[2,2,4,16,256]{4,3,2,1,0:T(8,128)S(1)}, f32[2,2,4,16,256]{4,3,2,1,0:T(8,128)S(1)}, u32[]{:S(2)}, u32[]{:S(2)}) collective-permute-start(f32[2,2,4,16,256]{4,3,2,1,0:T(8,128)S(1)} %shard_map.43), channel_id=1, source_target_pairs={{0,8},{4,12},{8,0},{12,4},{1,9},{5,13},{9,1},{13,5},{2,10},{6,14},... | collective-permute-start | bytes 786440 | tf_op jit(solution)/shard_map/ppermute | solution.py:550
  6.2 2.1 %collective-permute-start.5 = (f32[24,256]{1,0:T(8,128)S(1)}, f32[24,256]{1,0:T(8,128)S(1)}, u32[]{:S(2)}, u32[]{:S(2)}) collective-permute-start(f32[24,256]{1,0:T(8,128)S(1)} %shard_map.40), channel_id=1, source_target_pairs={{0,3},{1,0},{2,1},{3,2},{4,7},{5,4},{6,5},{7,6},{8,11},{9,8},{10,9... | collective-permute-start | bytes 73736 | tf_op jit(solution)/shard_map/ppermute | solution.py:556
  8.3 0.7 %collective-permute-done.1.base_c = f32[2,2,3,16,256]{4,3,2,1,0:T(8,128)S(1)} collective-permute-done((f32[2,2,3,16,256]{4,3,2,1,0:T(8,128)}, f32[2,2,3,16,256]{4,3,2,1,0:T(8,128)S(1)}, u32[]{:S(2)}, u32[]{:S(2)}) %collective-permute-start.1) | collective-permute-done | bytes 196640 | tf_op jit(solution)/shard_map/ppermute | solution.py:550
  9.0 0.6 %collective-permute-done.4 = f32[24,256]{1,0:T(8,128)S(1)} collective-permute-done((f32[24,256]{1,0:T(8,128)S(1)}, f32[24,256]{1,0:T(8,128)S(1)}, u32[]{:S(2)}, u32[]{:S(2)}) %collective-permute-start.4) | collective-permute-done | bytes 24608 | tf_op jit(solution)/shard_map/ppermute | solution.py:556
  9.6 0.5 %collective-permute-done.5 = f32[24,256]{1,0:T(8,128)S(1)} collective-permute-done((f32[24,256]{1,0:T(8,128)S(1)}, f32[24,256]{1,0:T(8,128)S(1)}, u32[]{:S(2)}, u32[]{:S(2)}) %collective-permute-start.5) | collective-permute-done | bytes 24608 | tf_op jit(solution)/shard_map/ppermute | solution.py:556
  10.1 0.3 %collective-permute-done.2.base_d = f32[2,2,3,16,256]{4,3,2,1,0:T(8,128)S(1)} collective-permute-done((f32[2,2,3,16,256]{4,3,2,1,0:T(8,128)S(1)}, f32[2,2,3,16,256]{4,3,2,1,0:T(8,128)S(1)}, u32[]{:S(2)}, u32[]{:S(2)}) %collective-permute-start.2) | collective-permute-done | bytes 196640 | tf_op jit(solution)/shard_map/ppermute | solution.py:553
  10.4 0.2 %shard_map.37 = (f32[8,2,3,16,256]{4,3,2,1,0:T(8,128)S(1)}, f32[64,256]{1,0:T(8,128)S(1)}) custom-call(f32[2,2,3,16,256]{4,3,2,1,0:T(8,128)S(1)} %copy-done.1, f32[2,2,3,16,256]{4,3,2,1,0:T(8,128)S(1)} %collective-permute-done.base_b._, f32[2,2,3,16,256]{4,3,2,1,0:T(8,128)S(1)} %collective-permute-done.1.base_c, ...), custom_call_target="tpu_custom_call" | custom-call | flops 1 | bytes 1 | tf_op jit(solution)/shard_map/pallas_call | solution.py:564
  10.7 0.7 %collective-permute-done.6.halo_core = f32[48,256]{1,0:T(8,128)S(1)} collective-permute-done((f32[48,256]{1,0:T(8,128)S(1)}, f32[48,256]{1,0:T(8,128)S(1)}, u32[]{:S(2)}, u32[]{:S(2)}) %collective-permute-start.6) | collective-permute-done | bytes 49184 | tf_op jit(solution)/shard_map/ppermute | solution.py:553
  11.3 0.1 shard_map.42
  11.4 1.6 %collective-permute-start.7 = (f32[96,256]{1,0:T(8,128)S(1)}, f32[96,256]{1,0:T(8,128)S(1)}, u32[]{:S(2)}, u32[]{:S(2)}) collective-permute-start(f32[96,256]{1,0:T(8,128)S(1)} %shard_map.42), channel_id=1, source_target_pairs={{0,8},{4,12},{8,0},{12,4},{1,9},{5,13},{9,1},{13,5},{2,10},{6,14},... | collective-permute-start | bytes 294920 | tf_op jit(solution)/shard_map/ppermute | solution.py:550
  13.0 1.1 %shard_map.41.after.before_ref.near_ref = f32[2,2,5,16,256]{4,3,2,1,0:T(8,128)S(1)} custom-call(f32[8,2,3,16,256]{4,3,2,1,0:T(8,128)S(1)} %get-tuple-element.7.base, f32[2,2,5,16,256]{4,3,2,1,0:T(8,128)S(1)} %copy-done, f32[2,2,5,16,256]{4,3,2,1,0:T(8,128)S(1)} %collective-permute-done.3.q_core, f32[48,256]{1,0:T(8,128)S(1)} %constant_dynamic-update-slice_fusion.halo_own, ...), custom_call_target="tpu_custom_call" | custom-call | flops 1 | bytes 1 | tf_op jit(solution)/shard_map/pallas_call | solution.py:564
  14.1 0.3 %collective-permute-done.8.values = f32[2,2,4,16,256]{4,3,2,1,0:T(8,128)S(1)} collective-permute-done((f32[2,2,4,16,256]{4,3,2,1,0:T(8,128)S(1)}, f32[2,2,4,16,256]{4,3,2,1,0:T(8,128)S(1)}, u32[]{:S(2)}, u32[]{:S(2)}) %collective-permute-start.8) | collective-permute-done | bytes 262176 | tf_op jit(solution)/shard_map/ppermute | solution.py:550
  14.4 0.1 collective-permute-start.10
  14.5 0.5 %collective-permute-start.11 = (f32[88,256]{1,0:T(8,128)S(1)}, f32[88,256]{1,0:T(8,128)S(1)}, u32[]{:S(2)}, u32[]{:S(2)}) collective-permute-start(f32[88,256]{1,0:T(8,128)S(1)} %get-tuple-element.9), channel_id=1, source_target_pairs={{0,4},{4,0},{8,12},{12,8},{1,5},{5,1},{9,13},{13,9},{2,6},{6,2},{1... | collective-permute-start | bytes 270344 | tf_op jit(solution)/shard_map/ppermute | solution.py:553
  15.0 0.1 collective-permute-start.9
  15.1 0.3 %shard_map.45.before_ref = f32[2,2,4,16,256]{4,3,2,1,0:T(8,128)S(1)} custom-call(f32[8,2,3,16,256]{4,3,2,1,0:T(8,128)S(1)} %get-tuple-element.7.base, f32[2,2,4,16,256]{4,3,2,1,0:T(8,128)S(1)} %shard_map.44.q_ref, f32[2,2,5,16,256]{4,3,2,1,0:T(8,128)S(1)} %shard_map.41.after.before_ref.near_ref), custom_call_target="tpu_custom_call" | custom-call | flops 1 | bytes 1 | tf_op jit(solution)/shard_map/pallas_call | solution.py:564
  15.5 0.8 %collective-permute-done.9.refs_0_ = f32[80,256]{1,0:T(8,128)S(1)} collective-permute-done((f32[80,256]{1,0:T(8,128)S(1)}, f32[80,256]{1,0:T(8,128)S(1)}, u32[]{:S(2)}, u32[]{:S(2)}) %collective-permute-start.9) | collective-permute-done | bytes 81952 | tf_op jit(solution)/shard_map/ppermute | solution.py:553
  16.3 0.3 %shard_map.46._.far_ref = f32[2,2,4,16,256]{4,3,2,1,0:T(8,128)S(1)} custom-call(f32[8,2,3,16,256]{4,3,2,1,0:T(8,128)S(1)} %get-tuple-element.7.base, f32[2,2,4,16,256]{4,3,2,1,0:T(8,128)S(1)} %shard_map.45.before_ref, f32[80,256]{1,0:T(8,128)S(1)} %collective-permute-done.9.refs_0_, f32[88,256]{1,0:T(8,128)S(1)} %collective-permute-done.10.refs_1_, ...), custom_call_target="tpu_custom_call" | custom-call | flops 1 | bytes 1 | tf_op jit(solution)/shard_map/pallas_call | solution.py:564
  16.7 0.8 %shard_map.48 = f32[2,2,5,16,256]{4,3,2,1,0:T(8,128)} custom-call(f32[2,2,1,16,256]{4,3,2,1,0:T(8,128)S(1)} %shard_map.47.sent_ref, f32[2,2,4,16,256]{4,3,2,1,0:T(8,128)S(1)} %shard_map.46._.far_ref, f32[96,256]{1,0:T(8,128)S(1)} %collective-permute-done.7.message), custom_call_target="tpu_custom_call" | custom-call | flops 1 | bytes 1 | tf_op jit(solution)/shard_map/pallas_call | solution.py:564
  (20 shorter events, 0.1 us)
Async XLA Ops:
  0.0 3.9 %copy-start = (f32[2,2,5,16,256]{4,3,2,1,0:T(8,128)S(1)}, f32[2,2,5,16,256]{4,3,2,1,0:T(8,128)}, u32[]{:S(2)}) copy-start(f32[2,2,5,16,256]{4,3,2,1,0:T(8,128)} %q_ref.5) | copy-start | bytes 983044
  0.0 6.2 %collective-permute-start = (f32[2,2,3,16,256]{4,3,2,1,0:T(8,128)}, f32[2,2,3,16,256]{4,3,2,1,0:T(8,128)S(1)}, u32[]{:S(2)}, u32[]{:S(2)}) collective-permute-start(f32[2,2,3,16,256]{4,3,2,1,0:T(8,128)} %base_a.1), channel_id=1, source_target_pairs={{0,4},{4,0},{8,12},{12,8},{1,5},{5,1},{9,13},{13,9},{2,6},{6,2},{1... | collective-permute-start | bytes 589832 | tf_op jit(solution)/shard_map/ppermute | solution.py:553
  0.5 8.5 %collective-permute-start.1 = (f32[2,2,3,16,256]{4,3,2,1,0:T(8,128)}, f32[2,2,3,16,256]{4,3,2,1,0:T(8,128)S(1)}, u32[]{:S(2)}, u32[]{:S(2)}) collective-permute-start(f32[2,2,3,16,256]{4,3,2,1,0:T(8,128)} %base_a.1), channel_id=1, source_target_pairs={{0,8},{4,12},{8,0},{12,4},{1,9},{5,13},{9,1},{13,5},{2,10},{6,14},... | collective-permute-start | bytes 589832 | tf_op jit(solution)/shard_map/ppermute | solution.py:550
  3.0 7.1 %collective-permute-start.3 = (f32[2,2,5,16,256]{4,3,2,1,0:T(8,128)}, f32[2,2,5,16,256]{4,3,2,1,0:T(8,128)S(1)}, u32[]{:S(2)}, u32[]{:S(2)}) collective-permute-start(f32[2,2,5,16,256]{4,3,2,1,0:T(8,128)} %q_ref.5), channel_id=1, source_target_pairs={{0,4},{4,0},{8,12},{12,8},{1,5},{5,1},{9,13},{13,9},{2,6},{6,2},{1... | collective-permute-start | bytes 983048 | tf_op jit(solution)/shard_map/ppermute | solution.py:553
  4.0 5.7 %collective-permute-start.4 = (f32[24,256]{1,0:T(8,128)S(1)}, f32[24,256]{1,0:T(8,128)S(1)}, u32[]{:S(2)}, u32[]{:S(2)}) collective-permute-start(f32[24,256]{1,0:T(8,128)S(1)} %shard_map.39), channel_id=1, source_target_pairs={{0,1},{1,2},{2,3},{3,0},{4,5},{5,6},{6,7},{7,4},{8,9},{9,10},{10,1... | collective-permute-start | bytes 73736 | tf_op jit(solution)/shard_map/ppermute | solution.py:556
  5.6 4.8 %copy-start.1 = (f32[2,2,3,16,256]{4,3,2,1,0:T(8,128)S(1)}, f32[2,2,3,16,256]{4,3,2,1,0:T(8,128)}, u32[]{:S(2)}) copy-start(f32[2,2,3,16,256]{4,3,2,1,0:T(8,128)} %base_a.1) | copy-start | bytes 589828
  5.6 8.8 %collective-permute-start.8 = (f32[2,2,4,16,256]{4,3,2,1,0:T(8,128)S(1)}, f32[2,2,4,16,256]{4,3,2,1,0:T(8,128)S(1)}, u32[]{:S(2)}, u32[]{:S(2)}) collective-permute-start(f32[2,2,4,16,256]{4,3,2,1,0:T(8,128)S(1)} %shard_map.43), channel_id=1, source_target_pairs={{0,8},{4,12},{8,0},{12,4},{1,9},{5,13},{9,1},{13,5},{2,10},{6,14},... | collective-permute-start | bytes 786440 | tf_op jit(solution)/shard_map/ppermute | solution.py:550
  6.2 3.9 %collective-permute-start.5 = (f32[24,256]{1,0:T(8,128)S(1)}, f32[24,256]{1,0:T(8,128)S(1)}, u32[]{:S(2)}, u32[]{:S(2)}) collective-permute-start(f32[24,256]{1,0:T(8,128)S(1)} %shard_map.40), channel_id=1, source_target_pairs={{0,3},{1,0},{2,1},{3,2},{4,7},{5,4},{6,5},{7,6},{8,11},{9,8},{10,9... | collective-permute-start | bytes 73736 | tf_op jit(solution)/shard_map/ppermute | solution.py:556
  9.0 1.4 %collective-permute-start.2 = (f32[2,2,3,16,256]{4,3,2,1,0:T(8,128)S(1)}, f32[2,2,3,16,256]{4,3,2,1,0:T(8,128)S(1)}, u32[]{:S(2)}, u32[]{:S(2)}) collective-permute-start(f32[2,2,3,16,256]{4,3,2,1,0:T(8,128)S(1)} %collective-permute-done.1.base_c), channel_id=1, source_target_pairs={{0,4},{4,0},{8,12},{12,8},{1,5},{5,1},{9,13},{13,9},{2,6},{6,2},{1... | collective-permute-start | bytes 589832 | tf_op jit(solution)/shard_map/ppermute | solution.py:553
  10.1 1.2 %collective-permute-start.6 = (f32[48,256]{1,0:T(8,128)S(1)}, f32[48,256]{1,0:T(8,128)S(1)}, u32[]{:S(2)}, u32[]{:S(2)}) collective-permute-start(f32[48,256]{1,0:T(8,128)S(1)} %constant_dynamic-update-slice_fusion.halo_own), channel_id=1, source_target_pairs={{0,4},{4,0},{8,12},{12,8},{1,5},{5,1},{9,13},{13,9},{2,6},{6,2},{1... | collective-permute-start | bytes 147464 | tf_op jit(solution)/shard_map/ppermute | solution.py:553
  11.4 5.2 %collective-permute-start.7 = (f32[96,256]{1,0:T(8,128)S(1)}, f32[96,256]{1,0:T(8,128)S(1)}, u32[]{:S(2)}, u32[]{:S(2)}) collective-permute-start(f32[96,256]{1,0:T(8,128)S(1)} %shard_map.42), channel_id=1, source_target_pairs={{0,8},{4,12},{8,0},{12,4},{1,9},{5,13},{9,1},{13,5},{2,10},{6,14},... | collective-permute-start | bytes 294920 | tf_op jit(solution)/shard_map/ppermute | solution.py:550
  14.4 1.9 %collective-permute-start.10 = (f32[88,256]{1,0:T(8,128)S(1)}, f32[88,256]{1,0:T(8,128)S(1)}, u32[]{:S(2)}, u32[]{:S(2)}) collective-permute-start(f32[88,256]{1,0:T(8,128)S(1)} %get-tuple-element.10), channel_id=1, source_target_pairs={{0,4},{4,0},{8,12},{12,8},{1,5},{5,1},{9,13},{13,9},{2,6},{6,2},{1... | collective-permute-start | bytes 270344 | tf_op jit(solution)/shard_map/ppermute | solution.py:553
  14.5 1.8 %collective-permute-start.11 = (f32[88,256]{1,0:T(8,128)S(1)}, f32[88,256]{1,0:T(8,128)S(1)}, u32[]{:S(2)}, u32[]{:S(2)}) collective-permute-start(f32[88,256]{1,0:T(8,128)S(1)} %get-tuple-element.9), channel_id=1, source_target_pairs={{0,4},{4,0},{8,12},{12,8},{1,5},{5,1},{9,13},{13,9},{2,6},{6,2},{1... | collective-permute-start | bytes 270344 | tf_op jit(solution)/shard_map/ppermute | solution.py:553
  15.0 1.3 %collective-permute-start.9 = (f32[80,256]{1,0:T(8,128)S(1)}, f32[80,256]{1,0:T(8,128)S(1)}, u32[]{:S(2)}, u32[]{:S(2)}) collective-permute-start(f32[80,256]{1,0:T(8,128)S(1)} %slice.12), channel_id=1, source_target_pairs={{0,4},{4,0},{8,12},{12,8},{1,5},{5,1},{9,13},{13,9},{2,6},{6,2},{1... | collective-permute-start | bytes 245768 | tf_op jit(solution)/shard_map/ppermute | solution.py:553

commit v8 on v6

--- a/solution.py
+++ b/solution.py
@@ -619,7 +619,7 @@
     )[0]
     moved_here = call(
         pass_kernel,
-        (moved_chip, near_sum),
+        (moved_chip, message),
         array(*moved_chip.shape),
         in_specs=[anywhere] * 2,
         out_specs=anywhere,

time: 17.5 us -> 17.5 us (level)
    ppermute x7, waiting for transfers between devices: 1.15 us -> 0.74 us  [to_core(): return lax.ppermute(value, 'harm', [(i, i ^ 1) for i in range(groups)])]
    ppermute x3, waiting for transfers between devices: 0.92 us -> 1.33 us  [to_chip(): return lax.ppermute(value, 'harm', [(i, i ^ 2) for i in range(groups)])]
where the time goes in v8:
time: 17.5 us; the launch traced here: 17.4 us
  starting transfers between devices  9.99 us (57%)
  Pallas kernels  3.88 us (22%)
  waiting for transfers between devices  3.4 us (19%)
    ppermute x3, starting transfers between devices, to_chip(): return lax.ppermute(value, 'harm', [(i, i ^ 2) for i in range(groups)])  4.84 us
    pallas_call x11, Pallas kernels, call(): pl.pallas_call(functools.partial(kernel, sizes), in_specs=in_specs or [in...  3.88 us
    ppermute x2, starting transfers between devices, along_tile(): lax.ppermute(value, 'tile', [(i, (i + step) % tiles) for i in range(tiles)])  3.8 us
    ppermute x7, starting transfers between devices, to_core(): return lax.ppermute(value, 'harm', [(i, i ^ 1) for i in range(groups)])  1.36 us
    ppermute x2, waiting for transfers between devices, along_tile(): lax.ppermute(value, 'tile', [(i, (i + step) % tiles) for i in range(tiles)])  1.33 us
    ppermute x3, waiting for transfers between devices, to_chip(): return lax.ppermute(value, 'harm', [(i, i ^ 2) for i in range(groups)])  1.33 us
    ppermute x7, waiting for transfers between devices, to_core(): return lax.ppermute(value, 'harm', [(i, i ^ 1) for i in range(groups)])  0.74 us
  transfers between devices with their start and end apart: 12, of which 7 were waited for; matrix products, arithmetic and copies ran while one was open for 0% of the time, Pallas kernels for 18%

profile of v8, /device:TPU:0, one launch (start us, length us, event | category | flops | bytes accessed | tf_op | source)
XLA Modules:
  0.0 17.4 jit_solution(4468654364022403740)
XLA Ops:
  0.0 0.5 %collective-permute-start = (f32[2,2,3,16,256]{4,3,2,1,0:T(8,128)}, f32[2,2,3,16,256]{4,3,2,1,0:T(8,128)S(1)}, u32[]{:S(2)}, u32[]{:S(2)}) collective-permute-start(f32[2,2,3,16,256]{4,3,2,1,0:T(8,128)} %base_a.1), channel_id=1, source_target_pairs={{0,4},{4,0},{8,12},{12,8},{1,5},{5,1},{9,13},{13,9},{2,6},{6,2},{1... | collective-permute-start | bytes 589832 | tf_op jit(solution)/shard_map/ppermute | solution.py:552
  0.5 2.5 %collective-permute-start.1 = (f32[2,2,3,16,256]{4,3,2,1,0:T(8,128)}, f32[2,2,3,16,256]{4,3,2,1,0:T(8,128)S(1)}, u32[]{:S(2)}, u32[]{:S(2)}) collective-permute-start(f32[2,2,3,16,256]{4,3,2,1,0:T(8,128)} %base_a.1), channel_id=1, source_target_pairs={{0,8},{4,12},{8,0},{12,4},{1,9},{5,13},{9,1},{13,5},{2,10},{6,14},... | collective-permute-start | bytes 589832 | tf_op jit(solution)/shard_map/ppermute | solution.py:549
  3.0 0.2 %collective-permute-start.3 = (f32[2,2,5,16,256]{4,3,2,1,0:T(8,128)}, f32[2,2,5,16,256]{4,3,2,1,0:T(8,128)S(1)}, u32[]{:S(2)}, u32[]{:S(2)}) collective-permute-start(f32[2,2,5,16,256]{4,3,2,1,0:T(8,128)} %q_from.1), channel_id=1, source_target_pairs={{0,4},{4,0},{8,12},{12,8},{1,5},{5,1},{9,13},{13,9},{2,6},{6,2},{1... | collective-permute-start | bytes 983048 | tf_op jit(solution)/shard_map/ppermute | solution.py:552
  3.2 1.0 %shard_map.37 = (f32[2,2,5,16,256]{4,3,2,1,0:T(8,128)S(1)}, f32[16,256]{1,0:T(8,128)S(1)}, f32[2,2,4,16,256]{4,3,2,1,0:T(8,128)S(1)}) custom-call(f32[2,2,5,16,256]{4,3,2,1,0:T(8,128)} %q_from.1, f32[16,256]{1,0:T(8,128)} %visc_from.1), custom_call_target="tpu_custom_call" | custom-call | flops 1 | bytes 1 | tf_op jit(solution)/shard_map/pallas_call | solution.py:563
  4.2 1.6 %collective-permute-start.4 = (f32[24,256]{1,0:T(8,128)S(1)}, f32[24,256]{1,0:T(8,128)S(1)}, u32[]{:S(2)}, u32[]{:S(2)}) collective-permute-start(f32[24,256]{1,0:T(8,128)S(1)} %shard_map.38), channel_id=1, source_target_pairs={{0,1},{1,2},{2,3},{3,0},{4,5},{5,6},{6,7},{7,4},{8,9},{9,10},{10,1... | collective-permute-start | bytes 73736 | tf_op jit(solution)/shard_map/ppermute | solution.py:555
  5.9 0.5 %collective-permute-start.8 = (f32[2,2,4,16,256]{4,3,2,1,0:T(8,128)S(1)}, f32[2,2,4,16,256]{4,3,2,1,0:T(8,128)S(1)}, u32[]{:S(2)}, u32[]{:S(2)}) collective-permute-start(f32[2,2,4,16,256]{4,3,2,1,0:T(8,128)S(1)} %get-tuple-element.16), channel_id=1, source_target_pairs={{0,8},{4,12},{8,0},{12,4},{1,9},{5,13},{9,1},{13,5},{2,10},{6,14},... | collective-permute-start | bytes 786440 | tf_op jit(solution)/shard_map/ppermute | solution.py:549
  6.4 2.2 %collective-permute-start.5 = (f32[24,256]{1,0:T(8,128)S(1)}, f32[24,256]{1,0:T(8,128)S(1)}, u32[]{:S(2)}, u32[]{:S(2)}) collective-permute-start(f32[24,256]{1,0:T(8,128)S(1)} %shard_map.39), channel_id=1, source_target_pairs={{0,3},{1,0},{2,1},{3,2},{4,7},{5,4},{6,5},{7,6},{8,11},{9,8},{10,9... | collective-permute-start | bytes 73736 | tf_op jit(solution)/shard_map/ppermute | solution.py:555
  8.6 0.4 %collective-permute-done.1.base_c = f32[2,2,3,16,256]{4,3,2,1,0:T(8,128)S(1)} collective-permute-done((f32[2,2,3,16,256]{4,3,2,1,0:T(8,128)}, f32[2,2,3,16,256]{4,3,2,1,0:T(8,128)S(1)}, u32[]{:S(2)}, u32[]{:S(2)}) %collective-permute-start.1) | collective-permute-done | bytes 196640 | tf_op jit(solution)/shard_map/ppermute | solution.py:549
  8.9 1.0 %collective-permute-done.4 = f32[24,256]{1,0:T(8,128)S(1)} collective-permute-done((f32[24,256]{1,0:T(8,128)S(1)}, f32[24,256]{1,0:T(8,128)S(1)}, u32[]{:S(2)}, u32[]{:S(2)}) %collective-permute-start.4) | collective-permute-done | bytes 24608 | tf_op jit(solution)/shard_map/ppermute | solution.py:555
  9.9 0.3 %collective-permute-done.5 = f32[24,256]{1,0:T(8,128)S(1)} collective-permute-done((f32[24,256]{1,0:T(8,128)S(1)}, f32[24,256]{1,0:T(8,128)S(1)}, u32[]{:S(2)}, u32[]{:S(2)}) %collective-permute-start.5) | collective-permute-done | bytes 24608 | tf_op jit(solution)/shard_map/ppermute | solution.py:555
  10.3 0.1 collective-permute-done.2.base_d
  10.4 0.9 %shard_map.40 = (f32[2,2,5,16,256]{4,3,2,1,0:T(8,128)S(1)}, f32[8,2,3,16,256]{4,3,2,1,0:T(8,128)S(1)}, f32[64,256]{1,0:T(8,128)S(1)}) custom-call(f32[2,2,3,16,256]{4,3,2,1,0:T(8,128)S(1)} %copy-done, f32[2,2,3,16,256]{4,3,2,1,0:T(8,128)S(1)} %collective-permute-done.refs_0_.base_b, f32[2,2,3,16,256]{4,3,2,1,0:T(8,128)S(1)} %collective-permute-done.1.base_c, ...), custom_call_target="tpu_custom_call" | custom-call | flops 1 | bytes 1 | tf_op jit(solution)/shard_map/pallas_call | solution.py:563
  11.3 0.2 %collective-permute-done.6.halo_ref.halo_core = f32[48,256]{1,0:T(8,128)S(1)} collective-permute-done((f32[48,256]{1,0:T(8,128)S(1)}, f32[48,256]{1,0:T(8,128)S(1)}, u32[]{:S(2)}, u32[]{:S(2)}) %collective-permute-start.6) | collective-permute-done | bytes 49184 | tf_op jit(solution)/shard_map/ppermute | solution.py:552
  11.5 0.1 shard_map.42.after
  11.6 1.8 %collective-permute-start.7 = (f32[96,256]{1,0:T(8,128)S(1)}, f32[96,256]{1,0:T(8,128)S(1)}, u32[]{:S(2)}, u32[]{:S(2)}) collective-permute-start(f32[96,256]{1,0:T(8,128)S(1)} %shard_map.42.after), channel_id=1, source_target_pairs={{0,8},{4,12},{8,0},{12,4},{1,9},{5,13},{9,1},{13,5},{2,10},{6,14},... | collective-permute-start | bytes 294920 | tf_op jit(solution)/shard_map/ppermute | solution.py:549
  13.4 0.9 %collective-permute-done.8.values = f32[2,2,4,16,256]{4,3,2,1,0:T(8,128)S(1)} collective-permute-done((f32[2,2,4,16,256]{4,3,2,1,0:T(8,128)S(1)}, f32[2,2,4,16,256]{4,3,2,1,0:T(8,128)S(1)}, u32[]{:S(2)}, u32[]{:S(2)}) %collective-permute-start.8) | collective-permute-done | bytes 262176 | tf_op jit(solution)/shard_map/ppermute | solution.py:549
  14.4 0.1 collective-permute-start.10
  14.5 0.5 %collective-permute-start.11 = (f32[88,256]{1,0:T(8,128)S(1)}, f32[88,256]{1,0:T(8,128)S(1)}, u32[]{:S(2)}, u32[]{:S(2)}) collective-permute-start(f32[88,256]{1,0:T(8,128)S(1)} %get-tuple-element.17), channel_id=1, source_target_pairs={{0,4},{4,0},{8,12},{12,8},{1,5},{5,1},{9,13},{13,9},{2,6},{6,2},{1... | collective-permute-start | bytes 270344 | tf_op jit(solution)/shard_map/ppermute | solution.py:552
  15.0 0.1 collective-permute-start.9
  15.1 0.4 %shard_map.41.before_ref.near_ref = f32[2,2,5,16,256]{4,3,2,1,0:T(8,128)S(1)} custom-call(f32[8,2,3,16,256]{4,3,2,1,0:T(8,128)S(1)} %get-tuple-element.13.base, f32[2,2,5,16,256]{4,3,2,1,0:T(8,128)S(1)} %collective-permute-done.3.q_core.q_ref, f32[48,256]{1,0:T(8,128)S(1)} %collective-permute-done.6.halo_ref.halo_core, ...), custom_call_target="tpu_custom_call" | custom-call | flops 1 | bytes 1 | tf_op jit(solution)/shard_map/pallas_call | solution.py:563
  15.5 0.3 %shard_map.44.before_ref = f32[2,2,4,16,256]{4,3,2,1,0:T(8,128)S(1)} custom-call(f32[8,2,3,16,256]{4,3,2,1,0:T(8,128)S(1)} %get-tuple-element.13.base, f32[2,2,4,16,256]{4,3,2,1,0:T(8,128)S(1)} %shard_map.43.q_ref, f32[2,2,5,16,256]{4,3,2,1,0:T(8,128)S(1)} %shard_map.41.before_ref.near_ref), custom_call_target="tpu_custom_call" | custom-call | flops 1 | bytes 1 | tf_op jit(solution)/shard_map/pallas_call | solution.py:563
  15.8 0.4 %collective-permute-done.9.refs_0_ = f32[80,256]{1,0:T(8,128)S(1)} collective-permute-done((f32[80,256]{1,0:T(8,128)S(1)}, f32[80,256]{1,0:T(8,128)S(1)}, u32[]{:S(2)}, u32[]{:S(2)}) %collective-permute-start.9) | collective-permute-done | bytes 81952 | tf_op jit(solution)/shard_map/ppermute | solution.py:552
  16.3 0.3 %shard_map.45._.far_ref = f32[2,2,4,16,256]{4,3,2,1,0:T(8,128)S(1)} custom-call(f32[8,2,3,16,256]{4,3,2,1,0:T(8,128)S(1)} %get-tuple-element.13.base, f32[2,2,4,16,256]{4,3,2,1,0:T(8,128)S(1)} %shard_map.44.before_ref, f32[80,256]{1,0:T(8,128)S(1)} %collective-permute-done.9.refs_0_, f32[88,256]{1,0:T(8,128)S(1)} %collective-permute-done.10.refs_1_, ...), custom_call_target="tpu_custom_call" | custom-call | flops 1 | bytes 1 | tf_op jit(solution)/shard_map/pallas_call | solution.py:563
  16.6 0.8 %shard_map.47 = f32[2,2,5,16,256]{4,3,2,1,0:T(8,128)} custom-call(f32[2,2,1,16,256]{4,3,2,1,0:T(8,128)S(1)} %shard_map.46.sent_ref, f32[2,2,4,16,256]{4,3,2,1,0:T(8,128)S(1)} %shard_map.45._.far_ref, f32[96,256]{1,0:T(8,128)S(1)} %collective-permute-done.7.message), custom_call_target="tpu_custom_call" | custom-call | flops 1 | bytes 1 | tf_op jit(solution)/shard_map/pallas_call | solution.py:563
  (17 shorter events, 0.1 us)
Async XLA Ops:
  0.0 6.4 %collective-permute-start = (f32[2,2,3,16,256]{4,3,2,1,0:T(8,128)}, f32[2,2,3,16,256]{4,3,2,1,0:T(8,128)S(1)}, u32[]{:S(2)}, u32[]{:S(2)}) collective-permute-start(f32[2,2,3,16,256]{4,3,2,1,0:T(8,128)} %base_a.1), channel_id=1, source_target_pairs={{0,4},{4,0},{8,12},{12,8},{1,5},{5,1},{9,13},{13,9},{2,6},{6,2},{1... | collective-permute-start | bytes 589832 | tf_op jit(solution)/shard_map/ppermute | solution.py:552
  0.5 8.5 %collective-permute-start.1 = (f32[2,2,3,16,256]{4,3,2,1,0:T(8,128)}, f32[2,2,3,16,256]{4,3,2,1,0:T(8,128)S(1)}, u32[]{:S(2)}, u32[]{:S(2)}) collective-permute-start(f32[2,2,3,16,256]{4,3,2,1,0:T(8,128)} %base_a.1), channel_id=1, source_target_pairs={{0,8},{4,12},{8,0},{12,4},{1,9},{5,13},{9,1},{13,5},{2,10},{6,14},... | collective-permute-start | bytes 589832 | tf_op jit(solution)/shard_map/ppermute | solution.py:549
  3.0 7.3 %collective-permute-start.3 = (f32[2,2,5,16,256]{4,3,2,1,0:T(8,128)}, f32[2,2,5,16,256]{4,3,2,1,0:T(8,128)S(1)}, u32[]{:S(2)}, u32[]{:S(2)}) collective-permute-start(f32[2,2,5,16,256]{4,3,2,1,0:T(8,128)} %q_from.1), channel_id=1, source_target_pairs={{0,4},{4,0},{8,12},{12,8},{1,5},{5,1},{9,13},{13,9},{2,6},{6,2},{1... | collective-permute-start | bytes 983048 | tf_op jit(solution)/shard_map/ppermute | solution.py:552
  4.2 5.7 %collective-permute-start.4 = (f32[24,256]{1,0:T(8,128)S(1)}, f32[24,256]{1,0:T(8,128)S(1)}, u32[]{:S(2)}, u32[]{:S(2)}) collective-permute-start(f32[24,256]{1,0:T(8,128)S(1)} %shard_map.38), channel_id=1, source_target_pairs={{0,1},{1,2},{2,3},{3,0},{4,5},{5,6},{6,7},{7,4},{8,9},{9,10},{10,1... | collective-permute-start | bytes 73736 | tf_op jit(solution)/shard_map/ppermute | solution.py:555
  5.9 4.5 %copy-start = (f32[2,2,3,16,256]{4,3,2,1,0:T(8,128)S(1)}, f32[2,2,3,16,256]{4,3,2,1,0:T(8,128)}, u32[]{:S(2)}) copy-start(f32[2,2,3,16,256]{4,3,2,1,0:T(8,128)} %base_a.1) | copy-start | bytes 589828
  5.9 8.5 %collective-permute-start.8 = (f32[2,2,4,16,256]{4,3,2,1,0:T(8,128)S(1)}, f32[2,2,4,16,256]{4,3,2,1,0:T(8,128)S(1)}, u32[]{:S(2)}, u32[]{:S(2)}) collective-permute-start(f32[2,2,4,16,256]{4,3,2,1,0:T(8,128)S(1)} %get-tuple-element.16), channel_id=1, source_target_pairs={{0,8},{4,12},{8,0},{12,4},{1,9},{5,13},{9,1},{13,5},{2,10},{6,14},... | collective-permute-start | bytes 786440 | tf_op jit(solution)/shard_map/ppermute | solution.py:549
  6.4 3.9 %collective-permute-start.5 = (f32[24,256]{1,0:T(8,128)S(1)}, f32[24,256]{1,0:T(8,128)S(1)}, u32[]{:S(2)}, u32[]{:S(2)}) collective-permute-start(f32[24,256]{1,0:T(8,128)S(1)} %shard_map.39), channel_id=1, source_target_pairs={{0,3},{1,0},{2,1},{3,2},{4,7},{5,4},{6,5},{7,6},{8,11},{9,8},{10,9... | collective-permute-start | bytes 73736 | tf_op jit(solution)/shard_map/ppermute | solution.py:555
  8.9 1.4 %collective-permute-start.2 = (f32[2,2,3,16,256]{4,3,2,1,0:T(8,128)S(1)}, f32[2,2,3,16,256]{4,3,2,1,0:T(8,128)S(1)}, u32[]{:S(2)}, u32[]{:S(2)}) collective-permute-start(f32[2,2,3,16,256]{4,3,2,1,0:T(8,128)S(1)} %collective-permute-done.1.base_c), channel_id=1, source_target_pairs={{0,4},{4,0},{8,12},{12,8},{1,5},{5,1},{9,13},{13,9},{2,6},{6,2},{1... | collective-permute-start | bytes 589832 | tf_op jit(solution)/shard_map/ppermute | solution.py:552
  10.3 1.2 %collective-permute-start.6 = (f32[48,256]{1,0:T(8,128)S(1)}, f32[48,256]{1,0:T(8,128)S(1)}, u32[]{:S(2)}, u32[]{:S(2)}) collective-permute-start(f32[48,256]{1,0:T(8,128)S(1)} %constant_dynamic-update-slice_fusion.halo_ref.halo_own), channel_id=1, source_target_pairs={{0,4},{4,0},{8,12},{12,8},{1,5},{5,1},{9,13},{13,9},{2,6},{6,2},{1... | collective-permute-start | bytes 147464 | tf_op jit(solution)/shard_map/ppermute | solution.py:552
  11.6 5.0 %collective-permute-start.7 = (f32[96,256]{1,0:T(8,128)S(1)}, f32[96,256]{1,0:T(8,128)S(1)}, u32[]{:S(2)}, u32[]{:S(2)}) collective-permute-start(f32[96,256]{1,0:T(8,128)S(1)} %shard_map.42.after), channel_id=1, source_target_pairs={{0,8},{4,12},{8,0},{12,4},{1,9},{5,13},{9,1},{13,5},{2,10},{6,14},... | collective-permute-start | bytes 294920 | tf_op jit(solution)/shard_map/ppermute | solution.py:549
  14.4 1.9 %collective-permute-start.10 = (f32[88,256]{1,0:T(8,128)S(1)}, f32[88,256]{1,0:T(8,128)S(1)}, u32[]{:S(2)}, u32[]{:S(2)}) collective-permute-start(f32[88,256]{1,0:T(8,128)S(1)} %get-tuple-element.18), channel_id=1, source_target_pairs={{0,4},{4,0},{8,12},{12,8},{1,5},{5,1},{9,13},{13,9},{2,6},{6,2},{1... | collective-permute-start | bytes 270344 | tf_op jit(solution)/shard_map/ppermute | solution.py:552
  14.5 1.8 %collective-permute-start.11 = (f32[88,256]{1,0:T(8,128)S(1)}, f32[88,256]{1,0:T(8,128)S(1)}, u32[]{:S(2)}, u32[]{:S(2)}) collective-permute-start(f32[88,256]{1,0:T(8,128)S(1)} %get-tuple-element.17), channel_id=1, source_target_pairs={{0,4},{4,0},{8,12},{12,8},{1,5},{5,1},{9,13},{13,9},{2,6},{6,2},{1... | collective-permute-start | bytes 270344 | tf_op jit(solution)/shard_map/ppermute | solution.py:552
  15.0 1.3 %collective-permute-start.9 = (f32[80,256]{1,0:T(8,128)S(1)}, f32[80,256]{1,0:T(8,128)S(1)}, u32[]{:S(2)}, u32[]{:S(2)}) collective-permute-start(f32[80,256]{1,0:T(8,128)S(1)} %slice.12), channel_id=1, source_target_pairs={{0,4},{4,0},{8,12},{12,8},{1,5},{5,1},{9,13},{13,9},{2,6},{6,2},{1... | collective-permute-start | bytes 245768 | tf_op jit(solution)/shard_map/ppermute | solution.py:552
